TPU v7x, 256 devices: a whole 4x4x8 slice. The times are simulated.
256 devices in a mesh: ctx: 16 (over y_lo, x, core), tp: 16 (over y_hi, z).
Axes of the slice: x: 4, y: 4 (y_hi: 2, y_lo: 2; y = y_hi * 2 + y_lo), z: 8, core: 2. Of those that a mesh axis runs over, the one named last changes fastest.
Arguments:
- queries: bfloat16 [4096, 8192], P('ctx', 'tp'), may hold values from -6 to 6
- keys_copied: bfloat16 [4096, 2048], P('ctx', 'tp'), may hold values from -6 to 6, as said below
- values_copied: bfloat16 [4096, 2048], P('ctx', 'tp'), may hold values from -6 to 6, as said below
- attention_output_saved: bfloat16 [4096, 8192], P('ctx', 'tp'), may hold values from -6 to 6
- log_norm: float32 [64, 4096], P('tp', 'ctx'), as said below
- block_output_gradient: bfloat16 [4096, 8192], P(('ctx', 'tp')), may hold values from -6 to 6
- w_out: bfloat16 [8192, 8192], P('tp'), may hold values from -0.0625 to 0.0625
- adapter_down_factor: bfloat16 [8192, 64], P('tp'), may hold values from -0.0625 to 0.0625
- adapter_up: bfloat16 [64, 8192], replicated, may hold values from -0.0625 to 0.0625
Outputs:
- grad_query: bfloat16 [4096, 8192], P('ctx', 'tp')
- grad_keys: bfloat16 [4096, 2048], P('ctx', 'tp')
- grad_values: bfloat16 [4096, 2048], P('ctx', 'tp')
- down_factor_gradient: float32 [8192, 64], P('tp')
- up_factor_gradient: bfloat16 [64, 8192], replicated
Inputs may be any that keep to these rules, and one draw needn't show every extreme that they name: log_norm[h, r] minus the natural logarithm of (1 + pos(r)) lies between 0 and 1.5. `keys_copied`: for every g below 8, the 128 columns from 2 * g * 128 equal the 128 columns that follow them. `values_copied`: for every g below 8, the 128 columns from 2 * g * 128 equal the 128 columns that follow them.
All inputs are finite; a program needn't handle non-finite values.
Results may differ from a plain program's by a relative error of at most 0.022.
Values may be sent and summed in bfloat16 or wider, within the bound.
No kernel may reach another device: no remote copies, remote signals or barrier semaphores. Data moves between devices by JAX's collectives and lax.ppermute only.
A program may use at most 64 MiB of HBM per device.

v0:
```python
import functools

import jax
import jax.numpy as jnp
from jax import lax
from jax.experimental import pallas as pl
from jax.experimental.pallas import tpu as pltpu
from jax.sharding import Mesh, PartitionSpec as P

CTX = ("ylo", "x", "core")
TP = ("yhi", "z")
SIZES = (2, 4, 2, 2, 8)
ADAPTER_SCALE = 2.0
LOG2E = 1.4426950408889634
F32 = jnp.float32
BF16 = jnp.bfloat16
HALF = 128
HEAD_DIM = 128
LAST = (((1,), (1,)), ((), ()))
FIRST = (((0,), (0,)), ((), ()))


def turned(x, axis, by):
    size = lax.axis_size(axis)
    return lax.ppermute(x, axis, [(i, (i + by) % size) for i in range(size)])


def rolled(x, by, axis=0):
    size = x.shape[axis]
    twice = jnp.concatenate([x, x], axis)
    return lax.dynamic_slice_in_dim(twice, by, size, axis)


def gathered_round(x, axis, far_up, before_last=lambda up, down: (up, down)):
    up, down, blocks = x, x, {0: x}
    for step in range(1, 4):
        up, down = turned(up, axis, 1), turned(down, axis, -1)
        blocks[8 - step], blocks[step] = up, down
    up, down = before_last(up, down)
    blocks[4] = turned(up, axis, 1) if far_up else turned(down, axis, -1)
    return [blocks[j] for j in range(8)]


def place_kernel(where_ref, *refs):
    blocks, out_ref = refs[:-1], refs[-1]
    width = blocks[0].shape[1]
    for j, block in enumerate(blocks):
        to = pl.multiple_of(lax.rem(where_ref[2] + j, len(blocks)) * width, 128)
        out_ref[:, pl.ds(to, width)] = block[...]


def placed_round(where, blocks):
    rows, width = blocks[0].shape
    vmem = pl.BlockSpec(memory_space=pltpu.VMEM)
    return pl.pallas_call(
        place_kernel,
        out_shape=jax.ShapeDtypeStruct((rows, width * len(blocks)), blocks[0].dtype),
        in_specs=[pl.BlockSpec(memory_space=pltpu.SMEM)] + [vmem] * len(blocks),
        out_specs=vmem,
        compiler_params=pltpu.CompilerParams(vmem_limit_bytes=16 * 1024 * 1024),
        cost_estimate=pl.CostEstimate(flops=0, bytes_accessed=2**20, transcendentals=0),
    )(where, *blocks)


def sum_kernel(pieces_ref, sum_ref, low_ref):
    total = pieces_ref[0].astype(F32)
    for i in range(1, pieces_ref.shape[0]):
        total += pieces_ref[i].astype(F32)
    sum_ref[...] = total
    low_ref[...] = total.astype(BF16)


def summed(pieces):
    vmem = pl.BlockSpec(memory_space=pltpu.VMEM)
    return pl.pallas_call(
        sum_kernel,
        out_shape=(
            jax.ShapeDtypeStruct(pieces.shape[1:], F32),
            jax.ShapeDtypeStruct(pieces.shape[1:], BF16),
        ),
        in_specs=[vmem],
        out_specs=(vmem, vmem),
        compiler_params=pltpu.CompilerParams(vmem_limit_bytes=16 * 1024 * 1024),
        cost_estimate=pl.CostEstimate(flops=2 * 10**10, bytes_accessed=2**21, transcendentals=0),
    )(pieces)


STEP = 1024
AHEAD = 3


def row_copies(blocks, rows, sems, z):
    copies = []
    for j, block in enumerate(blocks):
        to = pl.multiple_of(lax.rem(z + j, 8) * 16, 16)
        width = rows.shape[1]
        copies.append(
            pltpu.make_async_copy(block.at[:, :width], rows.at[pl.ds(to, 16), :], sems.at[j])
        )
    return copies


def column_copies(source, to, sems):
    return [
        pltpu.make_async_copy(
            source.at[:, i * STEP : (i + 1) * STEP], to.at[:, i * STEP : (i + 1) * STEP], sems.at[i]
        )
        for i in range(source.shape[1] // STEP)
    ]


def product_of(rows, row_copy, w, w_copy):
    for copy in row_copy + w_copy[:AHEAD]:
        copy.start()
    for copy in row_copy:
        copy.wait()
    product = None
    for i, copy in enumerate(w_copy):
        copy.wait()
        for later in w_copy[i + AHEAD : i + AHEAD + 1]:
            later.start()
        at = slice(i * STEP, (i + 1) * STEP)
        term = lax.dot_general(rows[:, at], w[:, at], LAST, preferred_element_type=F32)
        product = term if product is None else product + term
    return product


def cotangent_of(rows, up):
    cots = None
    for i in range(up.shape[1] // STEP):
        at = slice(i * STEP, (i + 1) * STEP)
        term = lax.dot_general(rows[:, at], up[:, at], LAST, preferred_element_type=F32)
        cots = term if cots is None else cots + term
    return cots.astype(BF16)


def own_kernel(where_ref, *refs):
    blocks, (w_ref, up_ref, product_ref, cots_ref, chunk_ref) = refs[:8], refs[8:13]
    rows, w, up, row_sems, w_sems, up_sems = refs[13:]
    z = where_ref[2]
    row_copy = row_copies(blocks, rows, row_sems, z)
    product_ref[...] = product_of(rows, row_copy, w, column_copies(w_ref, w, w_sems))
    up_copy = column_copies(up_ref, up, up_sems)
    for copy in up_copy:
        copy.start()
    for copy in up_copy:
        copy.wait()
    cots_ref[...] = cotangent_of(rows, up)
    chunk_ref[...] = rows[:, pl.ds(pl.multiple_of(z * 1024, 1024), 1024)]


def own_call(where, blocks, w, up):
    vmem = pl.BlockSpec(memory_space=pltpu.VMEM)
    anywhere = pl.BlockSpec(memory_space=pl.ANY)
    hbm = pl.BlockSpec(memory_space=pltpu.HBM)
    rank, width = up.shape
    return pl.pallas_call(
        own_kernel,
        out_shape=(
            jax.ShapeDtypeStruct((128, w.shape[0]), F32),
            jax.ShapeDtypeStruct((128, rank), BF16),
            jax.ShapeDtypeStruct((128, 1024), BF16),
        ),
        in_specs=[pl.BlockSpec(memory_space=pltpu.SMEM)] + [anywhere] * 8 + [hbm] * 2,
        out_specs=(vmem,) * 3,
        scratch_shapes=[
            pltpu.VMEM((128, width), BF16),
            pltpu.VMEM(w.shape, BF16),
            pltpu.VMEM((rank, width), BF16),
            pltpu.SemaphoreType.DMA((8,)),
            pltpu.SemaphoreType.DMA((width // STEP,)),
            pltpu.SemaphoreType.DMA((width // STEP,)),
        ],
        compiler_params=pltpu.CompilerParams(vmem_limit_bytes=54 * 1024 * 1024),
        cost_estimate=pl.CostEstimate(flops=8 * 10**9, bytes_accessed=2**23, transcendentals=0),
    )(where, *blocks, w, up)


def adapter_kernel(where_ref, *refs):
    peer = refs[:8]
    up_ref, chunk_ref, own_cots_ref, o_ref, cots_ref, mine_ref, yours_ref = refs[8:15]
    rows, up, tails, chunks, row_sems, tail_sems, up_sems = refs[15:]
    yhi, z, core = where_ref[1], where_ref[2], where_ref[3]
    copies = column_copies(up_ref, up, up_sems) + row_copies(peer, rows, row_sems, z)
    copies += [
        pltpu.make_async_copy(block.at[:, rows.shape[1] :], tails.at[j], tail_sems.at[j])
        for j, block in enumerate(peer)
    ]
    for copy in copies:
        copy.start()
    chunks[yhi] = chunk_ref[...]
    for copy in copies:
        copy.wait()
    mixed = tails[0].astype(F32)
    for j in range(1, 8):
        mixed += tails[j].astype(F32)
    mixed = mixed.astype(BF16)
    mixed = jnp.concatenate([mixed[:, i * 256 : i * 256 + 256] for i in range(4)])
    chunks[1 - yhi] = rows[:, pl.ds(pl.multiple_of(z * 1024, 1024), 1024)]
    peer_cots, own_cots = cotangent_of(rows, up), own_cots_ref[...]
    cots = jnp.concatenate(
        [jnp.where(yhi == 0, own_cots, peer_cots), jnp.where(yhi == 0, peer_cots, own_cots)]
    )
    cots_ref[...] = cots
    columns = chunks[...].reshape(256, 1024)
    up_part = ADAPTER_SCALE * jnp.dot(mixed, columns, preferred_element_type=F32)
    down_part = lax.dot_general(cots, o_ref[...], FIRST, preferred_element_type=F32)
    down_part = ADAPTER_SCALE * down_part
    first = jnp.concatenate([up_part[:, :512], down_part[:, :256]], 1)
    second = jnp.concatenate([up_part[:, 512:], down_part[:, 256:]], 1)
    mine_ref[...] = jnp.where(core == 0, first, second)
    yours_ref[...] = jnp.where(core == 0, second, first).astype(BF16)


def adapter_call(where, peer, up, chunk, own_cots, o):
    vmem = pl.BlockSpec(memory_space=pltpu.VMEM)
    anywhere = pl.BlockSpec(memory_space=pl.ANY)
    rank, width = up.shape
    return pl.pallas_call(
        adapter_kernel,
        out_shape=(
            jax.ShapeDtypeStruct((256, rank), BF16),
            jax.ShapeDtypeStruct((rank, 768), F32),
            jax.ShapeDtypeStruct((rank, 768), BF16),
        ),
        in_specs=[pl.BlockSpec(memory_space=pltpu.SMEM)]
        + [anywhere] * 8
        + [pl.BlockSpec(memory_space=pltpu.HBM)]
        + [vmem] * 3,
        out_specs=(vmem,) * 3,
        scratch_shapes=[
            pltpu.VMEM((128, width), BF16),
            pltpu.VMEM((rank, width), BF16),
            pltpu.VMEM((8, 16, 1024), BF16),
            pltpu.VMEM((2, 128, 1024), BF16),
            pltpu.SemaphoreType.DMA((8,)),
            pltpu.SemaphoreType.DMA((8,)),
            pltpu.SemaphoreType.DMA((width // STEP,)),
        ],
        compiler_params=pltpu.CompilerParams(vmem_limit_bytes=20 * 1024 * 1024),
        cost_estimate=pl.CostEstimate(flops=10**9, bytes_accessed=2**22, transcendentals=0),
    )(where, *peer, up, chunk, own_cots, o)


def peer_kernel(where_ref, *refs):
    blocks, (w_ref, own_ref, cots_ref, down_ref, g_ref) = refs[:8], refs[8:13]
    rows, w, own, cots, row_sems, w_sems, sems = refs[13:]
    small = [
        pltpu.make_async_copy(own_ref, own, sems.at[0]),
        pltpu.make_async_copy(cots_ref, cots, sems.at[1]),
    ]
    for copy in small:
        copy.start()
    yhi = where_ref[1]
    row_copy = row_copies(blocks, rows, row_sems, where_ref[2])
    product = product_of(rows, row_copy, w, column_copies(w_ref, w, w_sems))
    for copy in small:
        copy.wait()
    adapter = ADAPTER_SCALE * jnp.dot(cots[...], down_ref[...], preferred_element_type=F32)
    for half in range(2):
        part = jnp.where(yhi == half, own[...], product)
        g_ref[half] = (part + adapter[half * 128 : half * 128 + 128]).astype(BF16)


def peer_call(where, blocks, w, own, cots, down):
    vmem = pl.BlockSpec(memory_space=pltpu.VMEM)
    anywhere = pl.BlockSpec(memory_space=pl.ANY)
    width = w.shape[1]
    return pl.pallas_call(
        peer_kernel,
        out_shape=jax.ShapeDtypeStruct((2, 128, w.shape[0]), BF16),
        in_specs=[pl.BlockSpec(memory_space=pltpu.SMEM)]
        + [anywhere] * 8
        + [pl.BlockSpec(memory_space=pltpu.HBM), anywhere, anywhere, vmem],
        out_specs=vmem,
        scratch_shapes=[
            pltpu.VMEM((128, width), BF16),
            pltpu.VMEM(w.shape, BF16),
            pltpu.VMEM(own.shape, F32),
            pltpu.VMEM(cots.shape, BF16),
            pltpu.SemaphoreType.DMA((8,)),
            pltpu.SemaphoreType.DMA((width // STEP,)),
            pltpu.SemaphoreType.DMA((2,)),
        ],
        compiler_params=pltpu.CompilerParams(vmem_limit_bytes=54 * 1024 * 1024),
        cost_estimate=pl.CostEstimate(flops=8 * 10**9, bytes_accessed=2**23, transcendentals=0),
    )(where, *blocks, w, own, cots, down)


def tile(q, g, norm, delta, keys, values, visible):
    scale = HEAD_DIM**-0.5
    scores = lax.dot_general(keys, q, LAST, preferred_element_type=F32)
    prob = jnp.exp2(scores * (scale * LOG2E) - norm)
    if visible is not None:
        prob = jnp.where(visible, prob, 0.0)
    prob_grad = lax.dot_general(values, g, LAST, preferred_element_type=F32)
    score_grad = (prob * (prob_grad - delta)).astype(BF16)
    value_grad = jnp.dot(prob.astype(BF16), g, preferred_element_type=F32)
    key_grad = jnp.dot(score_grad, q, preferred_element_type=F32) * scale
    query_grad = lax.dot_general(score_grad, keys, FIRST, preferred_element_type=F32)
    return query_grad, key_grad, value_grad


def late_kernel(
    q_ref, o_ref, g_ref, norm_ref, kv_ref, qs, gs, norm, delta, dq_sum, dkv_ref
):
    heads = q_ref.shape[1] // HEAD_DIM
    for half in range(2):
        rows = slice(half * HALF, (half + 1) * HALF)
        for h in range(heads):
            cols = slice(h * HEAD_DIM, (h + 1) * HEAD_DIM)
            into = slice(h * HALF, (h + 1) * HALF)
            qs[half, into, :] = q_ref[rows, cols]
            norm[half, :, into] = norm_ref[h : h + 1, rows] * LOG2E
            g = g_ref[half, :, cols]
            gs[half, into, :] = g
            product = g.astype(F32) * o_ref[rows, cols].astype(F32)
            delta[half, :, into] = jnp.sum(product.T, axis=0, keepdims=True)
    dq_sum[0] = jnp.zeros_like(dq_sum[0])
    dkv_ref[:, HALF:, :] = jnp.zeros((16, HALF, 2 * HEAD_DIM), BF16)
    for s in range(0, 16, 2):
        keys = kv_ref[s : s + 2, :HALF, :HEAD_DIM].reshape(2 * HALF, HEAD_DIM)
        values = kv_ref[s : s + 2, :HALF, HEAD_DIM:].reshape(2 * HALF, HEAD_DIM)
        query_grad, key_grad, value_grad = tile(
            qs[1], gs[1], norm[1], delta[1], keys, values, None
        )
        if s:
            dq_sum[1] += query_grad
        else:
            dq_sum[1] = query_grad
        dkv_ref[s : s + 2, :HALF, :HEAD_DIM] = key_grad.astype(BF16).reshape(2, HALF, HEAD_DIM)
        dkv_ref[s : s + 2, :HALF, HEAD_DIM:] = value_grad.astype(BF16).reshape(2, HALF, HEAD_DIM)


def rest_kernel(
    where_ref, qs, gs, norm, delta, dq_in, kv_ref, dkv_in, dq_ref, mine_ref, yours_ref, dq_sum, dkv_ref
):
    c = where_ref[0]
    heads = dq_ref.shape[1] // HEAD_DIM
    scale = HEAD_DIM**-0.5
    dkv_ref[...] = dkv_in[...]
    dq_sum[...] = dq_in[...]
    key_at = lax.broadcasted_iota(jnp.int32, (HALF, heads * HALF), 0)
    query_at = lax.broadcasted_iota(jnp.int32, (HALF, heads * HALF), 1) % HALF
    ahead = query_at - key_at

    def unit(i):
        late = (i > c).astype(jnp.int32)
        s = i - late
        first = pl.multiple_of(late * HALF, HALF)
        visible = ahead >= jnp.where(s == c, 0, -HALF)
        keys = kv_ref[s, pl.ds(first, HALF), :HEAD_DIM]
        values = kv_ref[s, pl.ds(first, HALF), HEAD_DIM:]
        query_grad, key_grad, value_grad = tile(
            qs[late], gs[late], norm[late], delta[late], keys, values, visible
        )
        return late, s, first, query_grad, jnp.concatenate([key_grad, value_grad], 1)

    def stored(late, s, first, query_grad, now):
        dq_sum[late] += query_grad
        before = dkv_ref[s, pl.ds(first, HALF), :].astype(F32)
        dkv_ref[s, pl.ds(first, HALF), :] = (before + now).astype(BF16)

    for first in range(0, 17, 4):
        for done in [unit(i) for i in range(first, min(first + 4, 17))]:
            stored(*done)
    core = where_ref[3]
    for k in range(8):
        mine_ref[k] = dkv_ref[2 * k + core]
        yours_ref[k] = dkv_ref[2 * k + 1 - core]
    for half in range(2):
        for h in range(heads):
            dq_ref[half * HALF : (half + 1) * HALF, h * HEAD_DIM : (h + 1) * HEAD_DIM] = (
                dq_sum[half, h * HALF : (h + 1) * HALF, :] * scale
            ).astype(BF16)


def late_call(q, o, g, log_norm, kv):
    side = q.shape[1] // HEAD_DIM * HALF
    vmem = pl.BlockSpec(memory_space=pltpu.VMEM)
    stacked = jax.ShapeDtypeStruct((2, side, HEAD_DIM), BF16)
    line = jax.ShapeDtypeStruct((2, 1, side), F32)
    return pl.pallas_call(
        late_kernel,
        out_shape=(
            stacked,
            stacked,
            line,
            line,
            jax.ShapeDtypeStruct((2, side, HEAD_DIM), F32),
            jax.ShapeDtypeStruct(kv.shape, BF16),
        ),
        in_specs=[vmem] * 5,
        out_specs=(vmem,) * 6,
        compiler_params=pltpu.CompilerParams(vmem_limit_bytes=24 * 1024 * 1024),
        cost_estimate=pl.CostEstimate(
            flops=10**10, bytes_accessed=2**22, transcendentals=10**6
        ),
    )(q, o, g, log_norm, kv)


def rest_call(where, kept, kv):
    qs, gs, norm, delta, dq, dkv = kept
    side = qs.shape[1]
    vmem = pl.BlockSpec(memory_space=pltpu.VMEM)
    half = jax.ShapeDtypeStruct((dkv.shape[0] // 2, *dkv.shape[1:]), BF16)
    return pl.pallas_call(
        rest_kernel,
        out_shape=(jax.ShapeDtypeStruct((2 * HALF, side), BF16), half, half),
        in_specs=[pl.BlockSpec(memory_space=pltpu.SMEM)] + [vmem] * 7,
        out_specs=(vmem,) * 3,
        scratch_shapes=[
            pltpu.VMEM((2, side, HEAD_DIM), F32),
            pltpu.VMEM(dkv.shape, BF16),
        ],
        compiler_params=pltpu.CompilerParams(vmem_limit_bytes=24 * 1024 * 1024),
        cost_estimate=pl.CostEstimate(
            flops=10**10, bytes_accessed=2**22, transcendentals=10**6
        ),
    )(where, qs, gs, norm, delta, dq, kv, dkv)


def local(q, k, v, o, log_norm, dy, w, down, up):
    ylo, x, core, yhi, z = (lax.axis_index(a) for a in CTX + TP)
    where = jnp.stack([ylo * 8 + x * 2 + core, yhi, z, core]).astype(jnp.int32)
    together = lax.optimization_barrier
    own_blocks = gathered_round(dy, "z", True)
    mixed = lax.dot_general(down, o, (((0,), (1,)), ((), ())), preferred_element_type=F32)
    mixed = jnp.concatenate([mixed[i * 16 : i * 16 + 16] for i in range(4)], 1)
    peer = turned(dy, "yhi", 1)
    other = turned(mixed.astype(BF16), "yhi", 1)
    peer = jnp.concatenate([peer, (mixed + other.astype(F32)).astype(BF16)], 1)
    own, own_cots, chunk = own_call(where, own_blocks, w, up)
    peer_blocks = gathered_round(peer, "z", False)
    kv, _ = together((jnp.concatenate([k, v], 1), peer))
    kv = lax.all_to_all(jnp.broadcast_to(kv[None], (16,) + kv.shape), CTX, 0, 0)
    cots, mine, yours = adapter_call(where, peer_blocks, up, chunk, own_cots, o)
    low = (mine + turned(yours, "core", 1).astype(F32)).astype(BF16)
    blocks, cots, low = together((peer_blocks, cots, low))
    g = peer_call(where, blocks, w, own, cots, down.T)
    total = low.astype(F32) + turned(low, "ylo", 1).astype(F32)
    low, g = together((total.astype(BF16), g))
    kept = late_call(q, o, g, log_norm, kv)
    total = low.astype(F32) + lax.ppermute(low, "x", [(i, i ^ 1) for i in range(4)]).astype(F32)
    low, kept = together((total.astype(BF16), kept))
    dq, mine, yours = rest_call(where, kept, kv)
    total = low.astype(F32) + lax.ppermute(low, "x", [(i, 3 - i) for i in range(4)]).astype(F32)
    low, mine, yours = together((total.astype(BF16), mine, yours))
    mine = (mine.astype(F32) + turned(yours, "core", 1).astype(F32)).astype(BF16)
    pieces = lax.all_to_all(mine, CTX[:2], 0, 0)
    other = turned(low, "core", 1)
    first, second = jnp.where(core == 0, low, other), jnp.where(core == 0, other, low)
    down_grad = jnp.concatenate([first[:, 512:], second[:, 512:]], 1).astype(F32).T
    up_total = jnp.concatenate([first[:, :512], second[:, :512]], 1)
    up_grad = placed_round(where, gathered_round(up_total, "z", True))
    dkv_sum, low = summed(pieces)
    other = lax.ppermute(low, "z", [(i, i ^ 1) for i in range(8)])
    dkv_sum = (dkv_sum + other.astype(F32)).astype(BF16)
    return dq, dkv_sum[:, :128], dkv_sum[:, 128:], down_grad, up_grad


def solution(mesh):
    fine = Mesh(mesh.devices.reshape(SIZES), CTX + TP)
    placed = (
        P(CTX, TP),
        P(CTX, TP),
        P(CTX, TP),
        P(CTX, TP),
        P(TP, CTX),
        P(CTX + TP, None),
        P(TP, None),
        P(TP, None),
        P(),
    )
    return jax.shard_map(
        local,
        mesh=fine,
        in_specs=placed,
        out_specs=(P(CTX, TP), P(CTX, TP), P(CTX, TP), P(TP, None), P()),
        check_vma=False,
    )
```

profile of v0, /device:TPU:2, one launch (start us, length us, event | category | flops | bytes accessed | tf_op | source)
XLA Modules:
  0.0 139.8 jit_solution(8902903171457127783)
XLA Ops:
  0.6 3.3 %collective-permute-start = (bf16[16,8192]{1,0:T(8,128)(2,1)}, bf16[16,8192]{1,0:T(8,128)(2,1)S(1)}, u32[]{:S(2)}, u32[]{:S(2)}) collective-permute-start(bf16[16,8192]{1,0:T(8,128)(2,1)} %refs_0_.1), channel_id=1, source_target_pairs={{0,8},{8,0},{1,9},{9,1},{2,10},{10,2},{3,11},{11,3},{4,12},{12,4},... | collective-permute-start | bytes 786440 | tf_op jit(solution)/shard_map/ppermute | solution.py:25
  3.9 1.2 fusion.3
  5.1 0.4 collective-permute-start.1
  5.6 1.9 %collective-permute-start.12 = (bf16[16,8192]{1,0:T(8,128)(2,1)}, bf16[16,8192]{1,0:T(8,128)(2,1)S(1)}, u32[]{:S(2)}, u32[]{:S(2)}) collective-permute-start(bf16[16,8192]{1,0:T(8,128)(2,1)} %refs_0_.1), channel_id=1, source_target_pairs={{0,1},{1,2},{2,3},{3,4},{4,5},{5,6},{6,7},{7,0},{8,9},{9,10},{10,1... | collective-permute-start | bytes 786440 | tf_op jit(solution)/shard_map/ppermute | solution.py:25
  7.5 3.7 %collective-permute-done.1 = bf16[16,1024]{1,0:T(8,128)(2,1)S(1)} collective-permute-done((bf16[16,1024]{1,0:T(8,128)(2,1)S(1)}, bf16[16,1024]{1,0:T(8,128)(2,1)S(1)}, u32[]{:S(2)}, u32[]{:S(2)}) %collective-permute-start.1) | collective-permute-done | bytes 32800 | tf_op jit(solution)/shard_map/ppermute | solution.py:25
  11.2 0.0 copy-start
  11.2 5.9 %collective-permute-start.2 = (bf16[16,9216]{1,0:T(8,128)(2,1)S(1)}, bf16[16,9216]{1,0:T(8,128)(2,1)S(1)}, u32[]{:S(2)}, u32[]{:S(2)}) collective-permute-start(bf16[16,9216]{1,0:T(8,128)(2,1)S(1)} %pad_maximum_fusion.refs_0_), channel_id=1, source_target_pairs={{0,7},{1,0},{2,1},{3,2},{4,3},{5,4},{6,5},{7,6},{8,15},{9,8},{10,9... | collective-permute-start | bytes 884744 | tf_op jit(solution)/shard_map/ppermute | solution.py:25
  17.2 1.0 collective-permute-start.9
  18.2 0.0 collective-permute-done.12.refs_7_
  18.2 1.0 collective-permute-start.13
  19.2 0.1 collective-permute-start.6
  19.3 5.3 %collective-permute-done.2.refs_1_ = bf16[16,9216]{1,0:T(8,128)(2,1)S(1)} collective-permute-done((bf16[16,9216]{1,0:T(8,128)(2,1)S(1)}, bf16[16,9216]{1,0:T(8,128)(2,1)S(1)}, u32[]{:S(2)}, u32[]{:S(2)}) %collective-permute-start.2) | collective-permute-done | bytes 294944 | tf_op jit(solution)/shard_map/ppermute | solution.py:25
  24.6 3.7 %collective-permute-start.3 = (bf16[16,9216]{1,0:T(8,128)(2,1)S(1)}, bf16[16,9216]{1,0:T(8,128)(2,1)S(1)}, u32[]{:S(2)}, u32[]{:S(2)}) collective-permute-start(bf16[16,9216]{1,0:T(8,128)(2,1)S(1)} %collective-permute-done.2.refs_1_), channel_id=1, source_target_pairs={{0,7},{1,0},{2,1},{3,2},{4,3},{5,4},{6,5},{7,6},{8,15},{9,8},{10,9... | collective-permute-start | bytes 884744 | tf_op jit(solution)/shard_map/ppermute | solution.py:25
  28.3 2.0 %collective-permute-done.9.refs_1_ = bf16[16,8192]{1,0:T(8,128)(2,1)S(1)} collective-permute-done((bf16[16,8192]{1,0:T(8,128)(2,1)}, bf16[16,8192]{1,0:T(8,128)(2,1)S(1)}, u32[]{:S(2)}, u32[]{:S(2)}) %collective-permute-start.9) | collective-permute-done | bytes 262176 | tf_op jit(solution)/shard_map/ppermute | solution.py:25
  30.4 3.6 %collective-permute-start.10 = (bf16[16,8192]{1,0:T(8,128)(2,1)S(1)}, bf16[16,8192]{1,0:T(8,128)(2,1)}, u32[]{:S(2)}, u32[]{:S(2)}) collective-permute-start(bf16[16,8192]{1,0:T(8,128)(2,1)S(1)} %collective-permute-done.9.refs_1_), channel_id=1, source_target_pairs={{0,7},{1,0},{2,1},{3,2},{4,3},{5,4},{6,5},{7,6},{8,15},{9,8},{10,9... | collective-permute-start | bytes 786440 | tf_op jit(solution)/shard_map/ppermute | solution.py:25
  34.0 0.0 collective-permute-done.13.refs_6_
  34.0 0.0 collective-permute-start.14
  34.0 0.1 collective-permute-start.7
  34.1 2.5 %collective-permute-done.3.refs_2_ = bf16[16,9216]{1,0:T(8,128)(2,1)S(1)} collective-permute-done((bf16[16,9216]{1,0:T(8,128)(2,1)S(1)}, bf16[16,9216]{1,0:T(8,128)(2,1)S(1)}, u32[]{:S(2)}, u32[]{:S(2)}) %collective-permute-start.3) | collective-permute-done | bytes 294944 | tf_op jit(solution)/shard_map/ppermute | solution.py:25
  36.6 3.7 %collective-permute-start.4 = (bf16[16,9216]{1,0:T(8,128)(2,1)S(1)}, bf16[16,9216]{1,0:T(8,128)(2,1)}, u32[]{:S(2)}, u32[]{:S(2)}) collective-permute-start(bf16[16,9216]{1,0:T(8,128)(2,1)S(1)} %collective-permute-done.3.refs_2_), channel_id=1, source_target_pairs={{0,7},{1,0},{2,1},{3,2},{4,3},{5,4},{6,5},{7,6},{8,15},{9,8},{10,9... | collective-permute-start | bytes 884744 | tf_op jit(solution)/shard_map/ppermute | solution.py:25
  40.3 1.9 %collective-permute-done.10.refs_2_ = bf16[16,8192]{1,0:T(8,128)(2,1)} collective-permute-done((bf16[16,8192]{1,0:T(8,128)(2,1)S(1)}, bf16[16,8192]{1,0:T(8,128)(2,1)}, u32[]{:S(2)}, u32[]{:S(2)}) %collective-permute-start.10) | collective-permute-done | bytes 262176 | tf_op jit(solution)/shard_map/ppermute | solution.py:25
  42.2 3.8 %collective-permute-start.11 = (bf16[16,8192]{1,0:T(8,128)(2,1)}, bf16[16,8192]{1,0:T(8,128)(2,1)}, u32[]{:S(2)}, u32[]{:S(2)}) collective-permute-start(bf16[16,8192]{1,0:T(8,128)(2,1)} %collective-permute-done.10.refs_2_), channel_id=1, source_target_pairs={{0,7},{1,0},{2,1},{3,2},{4,3},{5,4},{6,5},{7,6},{8,15},{9,8},{10,9... | collective-permute-start | bytes 786440 | tf_op jit(solution)/shard_map/ppermute | solution.py:25
  46.0 0.0 collective-permute-done.14.refs_5_
  46.0 0.7 pad_add_fusion.where_ref
  46.7 0.9 pad_maximum_fusion.1
  47.6 1.6 %broadcast_in_dim.2 = bf16[16,256,256]{2,1,0:T(8,128)(2,1)} broadcast(bf16[256,256]{1,0:T(8,128)(2,1)S(1)} %pad_maximum_fusion.1), dimensions={1,2} | broadcast | bytes 2228224 | tf_op jit(solution)/shard_map/broadcast_in_dim | solution.py:436
  49.1 5.9 %all-to-all-start = ((bf16[16,256,256]{2,1,0:T(8,128)(2,1)}), bf16[16,256,256]{2,1,0:T(8,128)(2,1)S(1)}, u32[]{:S(2)}, u32[]{:S(2)}) async-start(bf16[16,256,256]{2,1,0:T(8,128)(2,1)} %broadcast_in_dim.2), calls=%async_computation | async-start | bytes 4194304 | tf_op jit(solution)/shard_map/all_to_all | solution.py:436
  55.0 0.0 copy-start.2
  55.0 0.1 collective-permute-start.8
  55.1 3.5 %collective-permute-start.5 = (bf16[16,9216]{1,0:T(8,128)(2,1)}, bf16[16,9216]{1,0:T(8,128)(2,1)S(1)}, u32[]{:S(2)}, u32[]{:S(2)}) collective-permute-start(bf16[16,9216]{1,0:T(8,128)(2,1)} %collective-permute-done.4.refs_3_), channel_id=1, source_target_pairs={{0,7},{1,0},{2,1},{3,2},{4,3},{5,4},{6,5},{7,6},{8,15},{9,8},{10,9... | collective-permute-start | bytes 884744 | tf_op jit(solution)/shard_map/ppermute | solution.py:25
  58.6 9.9 %shard_map.128 = (f32[128,512]{1,0:T(8,128)}, bf16[128,64]{1,0:T(8,128)(2,1)}, bf16[128,1024]{1,0:T(8,128)(2,1)}) custom-call(s32[4]{0:T(128)} %pad_add_fusion.where_ref, bf16[16,8192]{1,0:T(8,128)(2,1)} %refs_0_.1, bf16[16,8192]{1,0:T(8,128)(2,1)} %copy-done.17, bf16[16,8192]{1,0:T(8,128)(2,1)} %collective-permute-done.10.refs_2_, ...), custom_call_target="tpu_custom_call" | custom-call | flops 8000000000 | bytes 8388608 | tf_op jit(solution)/shard_map/pallas_call | solution.py:157
  68.6 1.1 copy-done.8
  69.7 0.8 copy-done.9
  70.4 3.1 %shard_map.129 = (bf16[256,64]{1,0:T(8,128)(2,1)S(1)}, f32[64,768]{1,0:T(8,128)S(1)}, bf16[64,768]{1,0:T(8,128)(2,1)S(1)}) custom-call(s32[4]{0:T(128)S(1)} %copy-done.10, bf16[16,9216]{1,0:T(8,128)(2,1)S(1)} %pad_maximum_fusion.refs_0_, bf16[16,9216]{1,0:T(8,128)(2,1)S(1)} %collective-permute-done.2.refs_1_, ...), custom_call_target="tpu_custom_call" | custom-call | flops 1000000000 | bytes 4194304 | tf_op jit(solution)/shard_map/pallas_call | solution.py:219
  73.5 0.0 copy-start.13
  73.5 0.1 collective-permute-start.16
  73.6 1.3 collective-permute-done.16
  75.0 1.6 %collective-permute-start.17 = (bf16[64,768]{1,0:T(8,128)(2,1)S(1)}, bf16[64,768]{1,0:T(8,128)(2,1)S(1)}, u32[]{:S(2)}, u32[]{:S(2)}) collective-permute-start(bf16[64,768]{1,0:T(8,128)(2,1)S(1)} %add_convert_fusion.5), channel_id=1, source_target_pairs={{0,128},{128,0},{1,129},{129,1},{2,130},{130,2},{3,131},{131,3},{4... | collective-permute-start | bytes 294920 | tf_op jit(solution)/shard_map/ppermute | solution.py:25
  76.5 7.7 %shard_map.130.g_ref = bf16[2,128,512]{2,1,0:T(8,128)(2,1)} custom-call(s32[4]{0:T(128)} %pad_add_fusion.where_ref, bf16[16,9216]{1,0:T(8,128)(2,1)} %copy-done, bf16[16,9216]{1,0:T(8,128)(2,1)} %copy-done.3, bf16[16,9216]{1,0:T(8,128)(2,1)} %copy-done.5, bf16[16,9216]{1,0:T(8,128)(2,1)} %collective-permute-done.4.refs_3_, bf16[16,9216]{1,0:T(8,128)(2,1)} %copy-done.7, ...), custom_call_target="tpu_custom_call" | custom-call | flops 8000000000 | bytes 8388608 | tf_op jit(solution)/shard_map/pallas_call | solution.py:269
  84.3 0.6 collective-permute-start.18
  85.0 4.1 %collective-permute-done.18 = bf16[64,768]{1,0:T(8,128)(2,1)S(1)} collective-permute-done((bf16[64,768]{1,0:T(8,128)(2,1)S(1)}, bf16[64,768]{1,0:T(8,128)(2,1)S(1)}, u32[]{:S(2)}, u32[]{:S(2)}) %collective-permute-start.18) | collective-permute-done | bytes 98336 | tf_op jit(solution)/shard_map/ppermute | solution.py:444
  89.1 0.0 copy-start.15
  89.1 0.9 copy-done.15
  90.0 3.3 %shard_map.131 = (bf16[2,512,128]{2,1,0:T(8,128)(2,1)S(1)}, bf16[2,512,128]{2,1,0:T(8,128)(2,1)S(1)}, f32[2,1,512]{2,1,0:T(1,128)S(1)}, f32[2,1,512]{2,1,0:T(1,1...) custom-call(bf16[256,512]{1,0:T(8,128)(2,1)S(1)} %copy-done.12, bf16[256,512]{1,0:T(8,128)(2,1)S(1)} %copy-done.1, ...), custom_call_target="tpu_custom_call" | custom-call | flops 10000000000 | bytes 4194304 | tf_op jit(solution)/shard_map/pallas_call | solution.py:383
  93.3 1.8 %collective-permute-start.19 = (bf16[64,768]{1,0:T(8,128)(2,1)S(1)}, bf16[64,768]{1,0:T(8,128)(2,1)S(1)}, u32[]{:S(2)}, u32[]{:S(2)}) collective-permute-start(bf16[64,768]{1,0:T(8,128)(2,1)S(1)} %add_convert_fusion.3), channel_id=1, source_target_pairs={{0,96},{32,64},{64,32},{96,0},{1,97},{33,65},{65,33},{97,1},{2,98}... | collective-permute-start | bytes 294920 | tf_op jit(solution)/shard_map/ppermute | solution.py:447
  95.1 6.4 %shard_map.132 = (bf16[256,512]{1,0:T(8,128)(2,1)}, bf16[8,256,256]{2,1,0:T(8,128)(2,1)S(1)}, bf16[8,256,256]{2,1,0:T(8,128)(2,1)S(1)}) custom-call(s32[4]{0:T(128)S(1)} %copy-done.11, bf16[2,512,128]{2,1,0:T(8,128)(2,1)S(1)} %get-tuple-element.70.qs, bf16[2,512,128]{2,1,0:T(8,128)(2,1)S(1)} %get-tuple-element.71.gs, ...), custom_call_target="tpu_custom_call" | custom-call | flops 10000000000 | bytes 4194304 | tf_op jit(solution)/shard_map/pallas_call | solution.py:407
  101.5 0.1 collective-permute-start.20
  101.6 2.6 %collective-permute-done.20 = bf16[8,256,256]{2,1,0:T(8,128)(2,1)S(1)} collective-permute-done((bf16[8,256,256]{2,1,0:T(8,128)(2,1)S(1)}, bf16[8,256,256]{2,1,0:T(8,128)(2,1)S(1)}, u32[]{:S(2)}, u32[]{:S(2)}) %collective-permute-start.20) | collective-permute-done | bytes 1048608 | tf_op jit(solution)/shard_map/ppermute | solution.py:25
  104.2 1.3 add_convert_fusion
  105.5 5.2 %all-to-all-start.1 = ((bf16[8,256,256]{2,1,0:T(8,128)(2,1)}), bf16[8,256,256]{2,1,0:T(8,128)(2,1)S(1)}, u32[]{:S(2)}, u32[]{:S(2)}) async-start(bf16[8,256,256]{2,1,0:T(8,128)(2,1)} %add_convert_fusion), calls=%async_computation.1 | async-start | bytes 2097152 | tf_op jit(solution)/shard_map/all_to_all | solution.py:450
  110.7 1.3 collective-permute-done.22
  112.1 0.1 collective-permute-start.26
  112.2 3.2 %collective-permute-start.23 = (bf16[64,1024]{1,0:T(8,128)(2,1)S(1)}, bf16[64,1024]{1,0:T(8,128)(2,1)S(1)}, u32[]{:S(2)}, u32[]{:S(2)}) collective-permute-start(bf16[64,1024]{1,0:T(8,128)(2,1)S(1)} %pad_maximum_fusion.2.refs_0_), channel_id=1, source_target_pairs={{0,7},{1,0},{2,1},{3,2},{4,3},{5,4},{6,5},{7,6},{8,15},{9,8},{10,9... | collective-permute-start | bytes 393224 | tf_op jit(solution)/shard_map/ppermute | solution.py:25
  115.4 3.5 %collective-permute-done.26.refs_7_ = bf16[64,1024]{1,0:T(8,128)(2,1)S(1)} collective-permute-done((bf16[64,1024]{1,0:T(8,128)(2,1)S(1)}, bf16[64,1024]{1,0:T(8,128)(2,1)S(1)}, u32[]{:S(2)}, u32[]{:S(2)}) %collective-permute-start.26) | collective-permute-done | bytes 131104 | tf_op jit(solution)/shard_map/ppermute | solution.py:25
  118.9 3.2 %collective-permute-start.24 = (bf16[64,1024]{1,0:T(8,128)(2,1)S(1)}, bf16[64,1024]{1,0:T(8,128)(2,1)S(1)}, u32[]{:S(2)}, u32[]{:S(2)}) collective-permute-start(bf16[64,1024]{1,0:T(8,128)(2,1)S(1)} %collective-permute-done.23.refs_1_), channel_id=1, source_target_pairs={{0,7},{1,0},{2,1},{3,2},{4,3},{5,4},{6,5},{7,6},{8,15},{9,8},{10,9... | collective-permute-start | bytes 393224 | tf_op jit(solution)/shard_map/ppermute | solution.py:25
  122.2 2.9 %collective-permute-done.27.refs_6_ = bf16[64,1024]{1,0:T(8,128)(2,1)S(1)} collective-permute-done((bf16[64,1024]{1,0:T(8,128)(2,1)S(1)}, bf16[64,1024]{1,0:T(8,128)(2,1)S(1)}, u32[]{:S(2)}, u32[]{:S(2)}) %collective-permute-start.27) | collective-permute-done | bytes 131104 | tf_op jit(solution)/shard_map/ppermute | solution.py:25
  125.1 3.2 %collective-permute-start.25 = (bf16[64,1024]{1,0:T(8,128)(2,1)S(1)}, bf16[64,1024]{1,0:T(8,128)(2,1)S(1)}, u32[]{:S(2)}, u32[]{:S(2)}) collective-permute-start(bf16[64,1024]{1,0:T(8,128)(2,1)S(1)} %collective-permute-done.24.refs_2_), channel_id=1, source_target_pairs={{0,7},{1,0},{2,1},{3,2},{4,3},{5,4},{6,5},{7,6},{8,15},{9,8},{10,9... | collective-permute-start | bytes 393224 | tf_op jit(solution)/shard_map/ppermute | solution.py:25
  128.4 2.9 %collective-permute-done.28.refs_5_ = bf16[64,1024]{1,0:T(8,128)(2,1)S(1)} collective-permute-done((bf16[64,1024]{1,0:T(8,128)(2,1)S(1)}, bf16[64,1024]{1,0:T(8,128)(2,1)S(1)}, u32[]{:S(2)}, u32[]{:S(2)}) %collective-permute-start.28) | collective-permute-done | bytes 131104 | tf_op jit(solution)/shard_map/ppermute | solution.py:25
  131.3 0.1 shard_map.133
  131.4 0.1 collective-permute-start.21
  131.6 0.7 convert_bitcast_fusion
  132.2 5.2 %collective-permute-done.29.refs_4_ = bf16[64,1024]{1,0:T(8,128)(2,1)S(1)} collective-permute-done((bf16[64,1024]{1,0:T(8,128)(2,1)S(1)}, bf16[64,1024]{1,0:T(8,128)(2,1)S(1)}, u32[]{:S(2)}, u32[]{:S(2)}) %collective-permute-start.29) | collective-permute-done | bytes 131104 | tf_op jit(solution)/shard_map/ppermute | solution.py:25
  137.5 1.6 %shard_map.134 = bf16[64,8192]{1,0:T(8,128)(2,1)} custom-call(s32[4]{0:T(128)S(1)} %copy-done.11, bf16[64,1024]{1,0:T(8,128)(2,1)S(1)} %pad_maximum_fusion.2.refs_0_, bf16[64,1024]{1,0:T(8,128)(2,1)S(1)} %collective-permute-done.23.refs_1_, bf16[64,1024]{1,0:T(8,128)(2,1)S(1)} %collective-permute-done.24.refs_2_, ...), custom_call_target="tpu_custom_call" | custom-call | bytes 1048576 | tf_op jit(solution)/shard_map/pallas_call | solution.py:55
  139.1 0.7 fusion.1
  (67 shorter events, 0.3 us)
Async XLA Ops:
  0.6 10.6 %collective-permute-start = (bf16[16,8192]{1,0:T(8,128)(2,1)}, bf16[16,8192]{1,0:T(8,128)(2,1)S(1)}, u32[]{:S(2)}, u32[]{:S(2)}) collective-permute-start(bf16[16,8192]{1,0:T(8,128)(2,1)} %refs_0_.1), channel_id=1, source_target_pairs={{0,8},{8,0},{1,9},{9,1},{2,10},{10,2},{3,11},{11,3},{4,12},{12,4},... | collective-permute-start | bytes 786440 | tf_op jit(solution)/shard_map/ppermute | solution.py:25
  5.1 6.0 %collective-permute-start.1 = (bf16[16,1024]{1,0:T(8,128)(2,1)S(1)}, bf16[16,1024]{1,0:T(8,128)(2,1)S(1)}, u32[]{:S(2)}, u32[]{:S(2)}) collective-permute-start(bf16[16,1024]{1,0:T(8,128)(2,1)S(1)} %fusion), channel_id=1, source_target_pairs={{0,8},{8,0},{1,9},{9,1},{2,10},{10,2},{3,11},{11,3},{4,12},{12,4},... | collective-permute-start | bytes 98312 | tf_op jit(solution)/shard_map/ppermute | solution.py:25
  5.6 12.6 %collective-permute-start.12 = (bf16[16,8192]{1,0:T(8,128)(2,1)}, bf16[16,8192]{1,0:T(8,128)(2,1)S(1)}, u32[]{:S(2)}, u32[]{:S(2)}) collective-permute-start(bf16[16,8192]{1,0:T(8,128)(2,1)} %refs_0_.1), channel_id=1, source_target_pairs={{0,1},{1,2},{2,3},{3,4},{4,5},{5,6},{6,7},{7,0},{8,9},{9,10},{10,1... | collective-permute-start | bytes 786440 | tf_op jit(solution)/shard_map/ppermute | solution.py:25
  11.2 57.3 %copy-start = (bf16[16,9216]{1,0:T(8,128)(2,1)}, bf16[16,9216]{1,0:T(8,128)(2,1)S(1)}, u32[]{:S(2)}) copy-start(bf16[16,9216]{1,0:T(8,128)(2,1)S(1)} %pad_maximum_fusion.refs_0_) | copy-start | bytes 884740
  11.2 13.4 %collective-permute-start.2 = (bf16[16,9216]{1,0:T(8,128)(2,1)S(1)}, bf16[16,9216]{1,0:T(8,128)(2,1)S(1)}, u32[]{:S(2)}, u32[]{:S(2)}) collective-permute-start(bf16[16,9216]{1,0:T(8,128)(2,1)S(1)} %pad_maximum_fusion.refs_0_), channel_id=1, source_target_pairs={{0,7},{1,0},{2,1},{3,2},{4,3},{5,4},{6,5},{7,6},{8,15},{9,8},{10,9... | collective-permute-start | bytes 884744 | tf_op jit(solution)/shard_map/ppermute | solution.py:25
  17.2 13.2 %collective-permute-start.9 = (bf16[16,8192]{1,0:T(8,128)(2,1)}, bf16[16,8192]{1,0:T(8,128)(2,1)S(1)}, u32[]{:S(2)}, u32[]{:S(2)}) collective-permute-start(bf16[16,8192]{1,0:T(8,128)(2,1)} %refs_0_.1), channel_id=1, source_target_pairs={{0,7},{1,0},{2,1},{3,2},{4,3},{5,4},{6,5},{7,6},{8,15},{9,8},{10,9... | collective-permute-start | bytes 786440 | tf_op jit(solution)/shard_map/ppermute | solution.py:25
  18.2 27.8 %copy-start.16 = (bf16[16,8192]{1,0:T(8,128)(2,1)}, bf16[16,8192]{1,0:T(8,128)(2,1)S(1)}, u32[]{:S(2)}) copy-start(bf16[16,8192]{1,0:T(8,128)(2,1)S(1)} %collective-permute-done.12.refs_7_) | copy-start | bytes 786436
  18.2 15.8 %collective-permute-start.13 = (bf16[16,8192]{1,0:T(8,128)(2,1)S(1)}, bf16[16,8192]{1,0:T(8,128)(2,1)S(1)}, u32[]{:S(2)}, u32[]{:S(2)}) collective-permute-start(bf16[16,8192]{1,0:T(8,128)(2,1)S(1)} %collective-permute-done.12.refs_7_), channel_id=1, source_target_pairs={{0,1},{1,2},{2,3},{3,4},{4,5},{5,6},{6,7},{7,0},{8,9},{9,10},{10,1... | collective-permute-start | bytes 786440 | tf_op jit(solution)/shard_map/ppermute | solution.py:25
  19.2 14.8 %collective-permute-start.6 = (bf16[16,9216]{1,0:T(8,128)(2,1)S(1)}, bf16[16,9216]{1,0:T(8,128)(2,1)S(1)}, u32[]{:S(2)}, u32[]{:S(2)}) collective-permute-start(bf16[16,9216]{1,0:T(8,128)(2,1)S(1)} %pad_maximum_fusion.refs_0_), channel_id=1, source_target_pairs={{0,1},{1,2},{2,3},{3,4},{4,5},{5,6},{6,7},{7,0},{8,9},{9,10},{10,1... | collective-permute-start | bytes 884744 | tf_op jit(solution)/shard_map/ppermute | solution.py:25
  24.6 43.9 %copy-start.3 = (bf16[16,9216]{1,0:T(8,128)(2,1)}, bf16[16,9216]{1,0:T(8,128)(2,1)S(1)}, u32[]{:S(2)}) copy-start(bf16[16,9216]{1,0:T(8,128)(2,1)S(1)} %collective-permute-done.2.refs_1_) | copy-start | bytes 884740
  24.6 11.9 %collective-permute-start.3 = (bf16[16,9216]{1,0:T(8,128)(2,1)S(1)}, bf16[16,9216]{1,0:T(8,128)(2,1)S(1)}, u32[]{:S(2)}, u32[]{:S(2)}) collective-permute-start(bf16[16,9216]{1,0:T(8,128)(2,1)S(1)} %collective-permute-done.2.refs_1_), channel_id=1, source_target_pairs={{0,7},{1,0},{2,1},{3,2},{4,3},{5,4},{6,5},{7,6},{8,15},{9,8},{10,9... | collective-permute-start | bytes 884744 | tf_op jit(solution)/shard_map/ppermute | solution.py:25
  30.4 6.2 %copy-start.17 = (bf16[16,8192]{1,0:T(8,128)(2,1)}, bf16[16,8192]{1,0:T(8,128)(2,1)S(1)}, u32[]{:S(2)}) copy-start(bf16[16,8192]{1,0:T(8,128)(2,1)S(1)} %collective-permute-done.9.refs_1_) | copy-start | bytes 786436
  30.4 11.8 %collective-permute-start.10 = (bf16[16,8192]{1,0:T(8,128)(2,1)S(1)}, bf16[16,8192]{1,0:T(8,128)(2,1)}, u32[]{:S(2)}, u32[]{:S(2)}) collective-permute-start(bf16[16,8192]{1,0:T(8,128)(2,1)S(1)} %collective-permute-done.9.refs_1_), channel_id=1, source_target_pairs={{0,7},{1,0},{2,1},{3,2},{4,3},{5,4},{6,5},{7,6},{8,15},{9,8},{10,9... | collective-permute-start | bytes 786440 | tf_op jit(solution)/shard_map/ppermute | solution.py:25
  34.0 8.2 %copy-start.18 = (bf16[16,8192]{1,0:T(8,128)(2,1)}, bf16[16,8192]{1,0:T(8,128)(2,1)S(1)}, u32[]{:S(2)}) copy-start(bf16[16,8192]{1,0:T(8,128)(2,1)S(1)} %collective-permute-done.13.refs_6_) | copy-start | bytes 786436
  34.0 12.0 %collective-permute-start.14 = (bf16[16,8192]{1,0:T(8,128)(2,1)S(1)}, bf16[16,8192]{1,0:T(8,128)(2,1)}, u32[]{:S(2)}, u32[]{:S(2)}) collective-permute-start(bf16[16,8192]{1,0:T(8,128)(2,1)S(1)} %collective-permute-done.13.refs_6_), channel_id=1, source_target_pairs={{0,1},{1,2},{2,3},{3,4},{4,5},{5,6},{6,7},{7,0},{8,9},{9,10},{10,1... | collective-permute-start | bytes 786440 | tf_op jit(solution)/shard_map/ppermute | solution.py:25
  34.0 34.6 %copy-start.4 = (bf16[16,9216]{1,0:T(8,128)(2,1)}, bf16[16,9216]{1,0:T(8,128)(2,1)S(1)}, u32[]{:S(2)}) copy-start(bf16[16,9216]{1,0:T(8,128)(2,1)S(1)} %collective-permute-done.6.refs_7_) | copy-start | bytes 884740
  34.0 21.0 %collective-permute-start.7 = (bf16[16,9216]{1,0:T(8,128)(2,1)S(1)}, bf16[16,9216]{1,0:T(8,128)(2,1)}, u32[]{:S(2)}, u32[]{:S(2)}) collective-permute-start(bf16[16,9216]{1,0:T(8,128)(2,1)S(1)} %collective-permute-done.6.refs_7_), channel_id=1, source_target_pairs={{0,1},{1,2},{2,3},{3,4},{4,5},{5,6},{6,7},{7,0},{8,9},{9,10},{10,1... | collective-permute-start | bytes 884744 | tf_op jit(solution)/shard_map/ppermute | solution.py:25
  36.6 32.0 %copy-start.5 = (bf16[16,9216]{1,0:T(8,128)(2,1)}, bf16[16,9216]{1,0:T(8,128)(2,1)S(1)}, u32[]{:S(2)}) copy-start(bf16[16,9216]{1,0:T(8,128)(2,1)S(1)} %collective-permute-done.3.refs_2_) | copy-start | bytes 884740
  36.6 18.5 %collective-permute-start.4 = (bf16[16,9216]{1,0:T(8,128)(2,1)S(1)}, bf16[16,9216]{1,0:T(8,128)(2,1)}, u32[]{:S(2)}, u32[]{:S(2)}) collective-permute-start(bf16[16,9216]{1,0:T(8,128)(2,1)S(1)} %collective-permute-done.3.refs_2_), channel_id=1, source_target_pairs={{0,7},{1,0},{2,1},{3,2},{4,3},{5,4},{6,5},{7,6},{8,15},{9,8},{10,9... | collective-permute-start | bytes 884744 | tf_op jit(solution)/shard_map/ppermute | solution.py:25
  42.2 16.4 %collective-permute-start.11 = (bf16[16,8192]{1,0:T(8,128)(2,1)}, bf16[16,8192]{1,0:T(8,128)(2,1)}, u32[]{:S(2)}, u32[]{:S(2)}) collective-permute-start(bf16[16,8192]{1,0:T(8,128)(2,1)} %collective-permute-done.10.refs_2_), channel_id=1, source_target_pairs={{0,7},{1,0},{2,1},{3,2},{4,3},{5,4},{6,5},{7,6},{8,15},{9,8},{10,9... | collective-permute-start | bytes 786440 | tf_op jit(solution)/shard_map/ppermute | solution.py:25
  46.0 12.6 %collective-permute-start.15 = (bf16[16,8192]{1,0:T(8,128)(2,1)}, bf16[16,8192]{1,0:T(8,128)(2,1)}, u32[]{:S(2)}, u32[]{:S(2)}) collective-permute-start(bf16[16,8192]{1,0:T(8,128)(2,1)} %collective-permute-done.14.refs_5_), channel_id=1, source_target_pairs={{0,1},{1,2},{2,3},{3,4},{4,5},{5,6},{6,7},{7,0},{8,9},{9,10},{10,1... | collective-permute-start | bytes 786440 | tf_op jit(solution)/shard_map/ppermute | solution.py:25
  49.1 40.0 %all-to-all-start = ((bf16[16,256,256]{2,1,0:T(8,128)(2,1)}), bf16[16,256,256]{2,1,0:T(8,128)(2,1)S(1)}, u32[]{:S(2)}, u32[]{:S(2)}) async-start(bf16[16,256,256]{2,1,0:T(8,128)(2,1)} %broadcast_in_dim.2), calls=%async_computation | async-start | bytes 4194304 | tf_op jit(solution)/shard_map/all_to_all | solution.py:436
  55.0 13.6 %copy-start.1 = (bf16[256,512]{1,0:T(8,128)(2,1)S(1)}, bf16[256,512]{1,0:T(8,128)(2,1)}, u32[]{:S(2)}) copy-start(bf16[256,512]{1,0:T(8,128)(2,1)} %o_ref.1) | copy-start | bytes 786436
  55.0 13.6 %copy-start.2 = (bf16[64,8192]{1,0:T(8,128)(2,1)S(1)}, bf16[64,8192]{1,0:T(8,128)(2,1)}, u32[]{:S(2)}) copy-start(bf16[64,8192]{1,0:T(8,128)(2,1)} %refs_8_.4) | copy-start | bytes 3145732
  55.0 13.6 %copy-start.10 = (s32[4]{0:T(128)S(1)}, s32[4]{0:T(128)}, u32[]{:S(2)}) copy-start(s32[4]{0:T(128)} %pad_add_fusion.where_ref) | copy-start | bytes 52
  55.0 13.5 %collective-permute-start.8 = (bf16[16,9216]{1,0:T(8,128)(2,1)}, bf16[16,9216]{1,0:T(8,128)(2,1)S(1)}, u32[]{:S(2)}, u32[]{:S(2)}) collective-permute-start(bf16[16,9216]{1,0:T(8,128)(2,1)} %collective-permute-done.7.refs_6_), channel_id=1, source_target_pairs={{0,1},{1,2},{2,3},{3,4},{4,5},{5,6},{6,7},{7,0},{8,9},{9,10},{10,1... | collective-permute-start | bytes 884744 | tf_op jit(solution)/shard_map/ppermute | solution.py:25
  55.1 13.4 %collective-permute-start.5 = (bf16[16,9216]{1,0:T(8,128)(2,1)}, bf16[16,9216]{1,0:T(8,128)(2,1)S(1)}, u32[]{:S(2)}, u32[]{:S(2)}) collective-permute-start(bf16[16,9216]{1,0:T(8,128)(2,1)} %collective-permute-done.4.refs_3_), channel_id=1, source_target_pairs={{0,7},{1,0},{2,1},{3,2},{4,3},{5,4},{6,5},{7,6},{8,15},{9,8},{10,9... | collective-permute-start | bytes 884744 | tf_op jit(solution)/shard_map/ppermute | solution.py:25
  68.5 6.4 %copy-start.6 = (bf16[16,9216]{1,0:T(8,128)(2,1)}, bf16[16,9216]{1,0:T(8,128)(2,1)S(1)}, u32[]{:S(2)}) copy-start(bf16[16,9216]{1,0:T(8,128)(2,1)S(1)} %collective-permute-done.8.refs_5_) | copy-start | bytes 884740
  68.5 6.4 %copy-start.7 = (bf16[16,9216]{1,0:T(8,128)(2,1)}, bf16[16,9216]{1,0:T(8,128)(2,1)S(1)}, u32[]{:S(2)}) copy-start(bf16[16,9216]{1,0:T(8,128)(2,1)S(1)} %collective-permute-done.5.refs_4_) | copy-start | bytes 884740
  68.6 1.1 copy-start.8
  69.7 0.8 copy-start.9
  73.5 3.0 %copy-start.13 = (bf16[256,64]{1,0:T(8,128)(2,1)}, bf16[256,64]{1,0:T(8,128)(2,1)S(1)}, u32[]{:S(2)}) copy-start(bf16[256,64]{1,0:T(8,128)(2,1)S(1)} %get-tuple-element.60.refs_10_) | copy-start | bytes 98308
  73.5 1.4 collective-permute-start.16
  75.0 9.3 %collective-permute-start.17 = (bf16[64,768]{1,0:T(8,128)(2,1)S(1)}, bf16[64,768]{1,0:T(8,128)(2,1)S(1)}, u32[]{:S(2)}, u32[]{:S(2)}) collective-permute-start(bf16[64,768]{1,0:T(8,128)(2,1)S(1)} %add_convert_fusion.5), channel_id=1, source_target_pairs={{0,128},{128,0},{1,129},{129,1},{2,130},{130,2},{3,131},{131,3},{4... | collective-permute-start | bytes 294920 | tf_op jit(solution)/shard_map/ppermute | solution.py:25
  76.5 12.6 %copy-start.12 = (bf16[256,512]{1,0:T(8,128)(2,1)S(1)}, bf16[256,512]{1,0:T(8,128)(2,1)}, u32[]{:S(2)}) copy-start(bf16[256,512]{1,0:T(8,128)(2,1)} %q_ref.1) | copy-start | bytes 786436
  76.5 12.6 %copy-start.14 = (f32[4,256]{1,0:T(4,128)S(1)}, f32[4,256]{1,0:T(4,128)}, u32[]{:S(2)}) copy-start(f32[4,256]{1,0:T(4,128)} %norm_ref.1) | copy-start | bytes 12292
  84.3 4.7 %collective-permute-start.18 = (bf16[64,768]{1,0:T(8,128)(2,1)S(1)}, bf16[64,768]{1,0:T(8,128)(2,1)S(1)}, u32[]{:S(2)}, u32[]{:S(2)}) collective-permute-start(bf16[64,768]{1,0:T(8,128)(2,1)S(1)} %add_convert_fusion.4), channel_id=1, source_target_pairs={{0,32},{32,0},{64,96},{96,64},{1,33},{33,1},{65,97},{97,65},{2,34}... | collective-permute-start | bytes 294920 | tf_op jit(solution)/shard_map/ppermute | solution.py:444
  89.1 6.0 %copy-start.11 = (s32[4]{0:T(128)S(1)}, s32[4]{0:T(128)}, u32[]{:S(2)}) copy-start(s32[4]{0:T(128)} %pad_add_fusion.where_ref) | copy-start | bytes 52
  89.1 1.0 copy-start.15
  93.3 8.1 %collective-permute-start.19 = (bf16[64,768]{1,0:T(8,128)(2,1)S(1)}, bf16[64,768]{1,0:T(8,128)(2,1)S(1)}, u32[]{:S(2)}, u32[]{:S(2)}) collective-permute-start(bf16[64,768]{1,0:T(8,128)(2,1)S(1)} %add_convert_fusion.3), channel_id=1, source_target_pairs={{0,96},{32,64},{64,32},{96,0},{1,97},{33,65},{65,33},{97,1},{2,98}... | collective-permute-start | bytes 294920 | tf_op jit(solution)/shard_map/ppermute | solution.py:447
  101.5 2.7 %collective-permute-start.20 = (bf16[8,256,256]{2,1,0:T(8,128)(2,1)S(1)}, bf16[8,256,256]{2,1,0:T(8,128)(2,1)S(1)}, u32[]{:S(2)}, u32[]{:S(2)}) collective-permute-start(bf16[8,256,256]{2,1,0:T(8,128)(2,1)S(1)} %get-tuple-element.81), channel_id=1, source_target_pairs={{0,16},{16,0},{1,17},{17,1},{2,18},{18,2},{3,19},{19,3},{4,20},{20... | collective-permute-start | bytes 3145736 | tf_op jit(solution)/shard_map/ppermute | solution.py:25
  105.5 25.8 %all-to-all-start.1 = ((bf16[8,256,256]{2,1,0:T(8,128)(2,1)}), bf16[8,256,256]{2,1,0:T(8,128)(2,1)S(1)}, u32[]{:S(2)}, u32[]{:S(2)}) async-start(bf16[8,256,256]{2,1,0:T(8,128)(2,1)} %add_convert_fusion), calls=%async_computation.1 | async-start | bytes 2097152 | tf_op jit(solution)/shard_map/all_to_all | solution.py:450
  110.7 1.3 collective-permute-start.22
  112.1 6.8 %collective-permute-start.26 = (bf16[64,1024]{1,0:T(8,128)(2,1)S(1)}, bf16[64,1024]{1,0:T(8,128)(2,1)S(1)}, u32[]{:S(2)}, u32[]{:S(2)}) collective-permute-start(bf16[64,1024]{1,0:T(8,128)(2,1)S(1)} %pad_maximum_fusion.2.refs_0_), channel_id=1, source_target_pairs={{0,1},{1,2},{2,3},{3,4},{4,5},{5,6},{6,7},{7,0},{8,9},{9,10},{10,1... | collective-permute-start | bytes 393224 | tf_op jit(solution)/shard_map/ppermute | solution.py:25
  112.2 6.8 %collective-permute-start.23 = (bf16[64,1024]{1,0:T(8,128)(2,1)S(1)}, bf16[64,1024]{1,0:T(8,128)(2,1)S(1)}, u32[]{:S(2)}, u32[]{:S(2)}) collective-permute-start(bf16[64,1024]{1,0:T(8,128)(2,1)S(1)} %pad_maximum_fusion.2.refs_0_), channel_id=1, source_target_pairs={{0,7},{1,0},{2,1},{3,2},{4,3},{5,4},{6,5},{7,6},{8,15},{9,8},{10,9... | collective-permute-start | bytes 393224 | tf_op jit(solution)/shard_map/ppermute | solution.py:25
  118.9 6.2 %collective-permute-start.27 = (bf16[64,1024]{1,0:T(8,128)(2,1)S(1)}, bf16[64,1024]{1,0:T(8,128)(2,1)S(1)}, u32[]{:S(2)}, u32[]{:S(2)}) collective-permute-start(bf16[64,1024]{1,0:T(8,128)(2,1)S(1)} %collective-permute-done.26.refs_7_), channel_id=1, source_target_pairs={{0,1},{1,2},{2,3},{3,4},{4,5},{5,6},{6,7},{7,0},{8,9},{9,10},{10,1... | collective-permute-start | bytes 393224 | tf_op jit(solution)/shard_map/ppermute | solution.py:25
  118.9 6.2 %collective-permute-start.24 = (bf16[64,1024]{1,0:T(8,128)(2,1)S(1)}, bf16[64,1024]{1,0:T(8,128)(2,1)S(1)}, u32[]{:S(2)}, u32[]{:S(2)}) collective-permute-start(bf16[64,1024]{1,0:T(8,128)(2,1)S(1)} %collective-permute-done.23.refs_1_), channel_id=1, source_target_pairs={{0,7},{1,0},{2,1},{3,2},{4,3},{5,4},{6,5},{7,6},{8,15},{9,8},{10,9... | collective-permute-start | bytes 393224 | tf_op jit(solution)/shard_map/ppermute | solution.py:25
  125.1 6.2 %collective-permute-start.28 = (bf16[64,1024]{1,0:T(8,128)(2,1)S(1)}, bf16[64,1024]{1,0:T(8,128)(2,1)S(1)}, u32[]{:S(2)}, u32[]{:S(2)}) collective-permute-start(bf16[64,1024]{1,0:T(8,128)(2,1)S(1)} %collective-permute-done.27.refs_6_), channel_id=1, source_target_pairs={{0,1},{1,2},{2,3},{3,4},{4,5},{5,6},{6,7},{7,0},{8,9},{9,10},{10,1... | collective-permute-start | bytes 393224 | tf_op jit(solution)/shard_map/ppermute | solution.py:25
  125.1 7.1 %collective-permute-start.25 = (bf16[64,1024]{1,0:T(8,128)(2,1)S(1)}, bf16[64,1024]{1,0:T(8,128)(2,1)S(1)}, u32[]{:S(2)}, u32[]{:S(2)}) collective-permute-start(bf16[64,1024]{1,0:T(8,128)(2,1)S(1)} %collective-permute-done.24.refs_2_), channel_id=1, source_target_pairs={{0,7},{1,0},{2,1},{3,2},{4,3},{5,4},{6,5},{7,6},{8,15},{9,8},{10,9... | collective-permute-start | bytes 393224 | tf_op jit(solution)/shard_map/ppermute | solution.py:25
  131.3 6.2 %collective-permute-start.29 = (bf16[64,1024]{1,0:T(8,128)(2,1)S(1)}, bf16[64,1024]{1,0:T(8,128)(2,1)S(1)}, u32[]{:S(2)}, u32[]{:S(2)}) collective-permute-start(bf16[64,1024]{1,0:T(8,128)(2,1)S(1)} %collective-permute-done.28.refs_5_), channel_id=1, source_target_pairs={{0,1},{1,2},{2,3},{3,4},{4,5},{5,6},{6,7},{7,0},{8,9},{9,10},{10,1... | collective-permute-start | bytes 393224 | tf_op jit(solution)/shard_map/ppermute | solution.py:25
  131.4 7.6 %collective-permute-start.21 = (bf16[256,256]{1,0:T(8,128)(2,1)S(1)}, bf16[256,256]{1,0:T(8,128)(2,1)S(1)}, u32[]{:S(2)}, u32[]{:S(2)}) collective-permute-start(bf16[256,256]{1,0:T(8,128)(2,1)S(1)} %get-tuple-element.83), channel_id=1, source_target_pairs={{0,1},{1,0},{2,3},{3,2},{4,5},{5,4},{6,7},{7,6},{8,9},{9,8},{10,11... | collective-permute-start | bytes 393224 | tf_op jit(solution)/shard_map/ppermute | solution.py:457
where the time goes:
time: 140 us
  starting transfers between devices  57.2 us (41%)
  waiting for transfers between devices  39.5 us (28%)
  Pallas kernels  32 us (23%)
  local copies, waits for them, and re-layouts  5.09 us (4%)
  other arithmetic  3.67 us (3%)
    ppermute x27, starting transfers between devices, turned(): return lax.ppermute(x, axis, [(i, (i + by) % size) for i in range(size)])  43.6 us
    ppermute x27, waiting for transfers between devices, turned(): return lax.ppermute(x, axis, [(i, (i + by) % size) for i in range(size)])  35.4 us
    pallas_call x1, Pallas kernels, own_call(): pl.pallas_call(own_kernel, out_shape=(jax.ShapeDtypeStruct((128, w.shape[...  9.88 us
    pallas_call x1, Pallas kernels, peer_call(): pl.pallas_call(peer_kernel, out_shape=jax.ShapeDtypeStruct((2, 128, w.sha...  7.74 us
    pallas_call x1, Pallas kernels, rest_call(): pl.pallas_call(rest_kernel, out_shape=(jax.ShapeDtypeStruct((2 * HALF, si...  6.35 us
    all_to_all x1, starting transfers between devices, local(): kv = lax.all_to_all(jnp.broadcast_to(kv[None], (16,) + kv.shape), CTX, 0, 0)  5.86 us
    all_to_all x1, starting transfers between devices, local(): pieces = lax.all_to_all(mine, CTX[:2], 0, 0)  5.24 us
    ppermute x1, waiting for transfers between devices, local(): lax.ppermute(low, 'x', [(i, i ^ 1) for i in range(4)]).astype(F32)  4.05 us
  transfers between devices with their start and end apart: 32, of which 13 were waited for; matrix products, arithmetic and copies ran while one was open for 4% of the time, Pallas kernels for 21%

commit v1 on v0

v1 whole, which is shorter than its diff:
```python
import functools

import jax
import jax.numpy as jnp
from jax import lax
from jax.experimental import pallas as pl
from jax.experimental.pallas import tpu as pltpu
from jax.sharding import Mesh, PartitionSpec as P

CTX = ("ylo", "x", "core")
TP = ("yhi", "z")
SIZES = (2, 4, 2, 2, 8)
ADAPTER_SCALE = 2.0
LOG2E = 1.4426950408889634
F32 = jnp.float32
BF16 = jnp.bfloat16
HALF = 128
HEAD_DIM = 128
LAST = (((1,), (1,)), ((), ()))
FIRST = (((0,), (0,)), ((), ()))


def turned(x, axis, by):
    size = lax.axis_size(axis)
    return lax.ppermute(x, axis, [(i, (i + by) % size) for i in range(size)])


def rolled(x, by, axis=0):
    size = x.shape[axis]
    twice = jnp.concatenate([x, x], axis)
    return lax.dynamic_slice_in_dim(twice, by, size, axis)


def gathered_round(x, axis, far_up, before_last=lambda up, down: (up, down)):
    up, down, blocks = x, x, {0: x}
    for step in range(1, 4):
        up, down = turned(up, axis, 1), turned(down, axis, -1)
        blocks[8 - step], blocks[step] = up, down
    up, down = before_last(up, down)
    blocks[4] = turned(up, axis, 1) if far_up else turned(down, axis, -1)
    return [blocks[j] for j in range(8)]


def place_kernel(where_ref, *refs):
    blocks, out_ref = refs[:-1], refs[-1]
    width = blocks[0].shape[1]
    at = 0
    for block in blocks:
        part = lax.rem(where_ref[2] + at // width, PARTS)
        to = pl.multiple_of(part * width + at % width, 128)
        out_ref[:, pl.ds(to, block.shape[1])] = block[...]
        at += block.shape[1]


def placed_round(where, blocks):
    rows, width = blocks[0].shape
    vmem = pl.BlockSpec(memory_space=pltpu.VMEM)
    return pl.pallas_call(
        place_kernel,
        out_shape=jax.ShapeDtypeStruct((rows, width * PARTS), blocks[0].dtype),
        in_specs=[pl.BlockSpec(memory_space=pltpu.SMEM)] + [vmem] * len(blocks),
        out_specs=vmem,
        compiler_params=pltpu.CompilerParams(vmem_limit_bytes=16 * 1024 * 1024),
        cost_estimate=pl.CostEstimate(flops=0, bytes_accessed=2**20, transcendentals=0),
    )(where, *blocks)


def sum_kernel(pieces_ref, sum_ref, low_ref):
    total = pieces_ref[0].astype(F32)
    for i in range(1, pieces_ref.shape[0]):
        total += pieces_ref[i].astype(F32)
    sum_ref[...] = total
    low_ref[...] = total.astype(BF16)


def summed(pieces):
    vmem = pl.BlockSpec(memory_space=pltpu.VMEM)
    return pl.pallas_call(
        sum_kernel,
        out_shape=(
            jax.ShapeDtypeStruct(pieces.shape[1:], F32),
            jax.ShapeDtypeStruct(pieces.shape[1:], BF16),
        ),
        in_specs=[vmem],
        out_specs=(vmem, vmem),
        compiler_params=pltpu.CompilerParams(vmem_limit_bytes=16 * 1024 * 1024),
        cost_estimate=pl.CostEstimate(flops=2 * 10**10, bytes_accessed=2**21, transcendentals=0),
    )(pieces)


STEP = 1024
PARTS = 4


def row_copies(blocks, rows, sems, z):
    width = rows.shape[1]
    copies = []
    for j, block in enumerate(blocks):
        to = pl.multiple_of(lax.rem(z + j, 8) * 16, 16)
        copies.append(
            pltpu.make_async_copy(block.at[:, :width], rows.at[pl.ds(to, 16), :], sems.at[j])
        )
    return copies


def column_copies(source, to, sems):
    return [
        pltpu.make_async_copy(
            source.at[:, i * STEP : (i + 1) * STEP], to.at[:, i * STEP : (i + 1) * STEP], sems.at[i]
        )
        for i in range(source.shape[1] // STEP)
    ]


def cotangent_of(rows, up):
    cots = None
    for i in range(up.shape[1] // STEP):
        at = slice(i * STEP, (i + 1) * STEP)
        term = lax.dot_general(rows[:, at], up[:, at], LAST, preferred_element_type=F32)
        cots = term if cots is None else cots + term
    return cots.astype(BF16)


def own_kernel(where_ref, *refs):
    blocks, (up_ref, rows, cots_ref) = refs[:8], refs[8:11]
    up, row_sems, up_sems = refs[11:]
    copies = row_copies(blocks, rows, row_sems, where_ref[2]) + column_copies(up_ref, up, up_sems)
    for copy in copies:
        copy.start()
    for copy in copies:
        copy.wait()
    cots_ref[...] = cotangent_of(rows, up)


def own_call(where, blocks, up):
    vmem = pl.BlockSpec(memory_space=pltpu.VMEM)
    anywhere = pl.BlockSpec(memory_space=pl.ANY)
    rank, width = up.shape
    return pl.pallas_call(
        own_kernel,
        out_shape=(
            jax.ShapeDtypeStruct((128, width), BF16),
            jax.ShapeDtypeStruct((128, rank), BF16),
        ),
        in_specs=[pl.BlockSpec(memory_space=pltpu.SMEM)] + [anywhere] * 9,
        out_specs=(vmem,) * 2,
        scratch_shapes=[
            pltpu.VMEM((rank, width), BF16),
            pltpu.SemaphoreType.DMA((8,)),
            pltpu.SemaphoreType.DMA((width // STEP,)),
        ],
        compiler_params=pltpu.CompilerParams(vmem_limit_bytes=48 * 1024 * 1024),
        cost_estimate=pl.CostEstimate(flops=2 * 10**9, bytes_accessed=2**22, transcendentals=0),
    )(where, *blocks, up)


def adapter_kernel(where_ref, *refs):
    peer = refs[:8]
    up_ref, own_ref, own_cots_ref, o_ref, rows, cots_ref, mine_ref, yours_ref = refs[8:16]
    up, tails, chunks, row_sems, tail_sems, up_sems = refs[16:]
    yhi, z, core = where_ref[1], where_ref[2], where_ref[3]
    copies = column_copies(up_ref, up, up_sems) + row_copies(peer, rows, row_sems, z)
    copies += [
        pltpu.make_async_copy(block.at[:, rows.shape[1] :], tails.at[j], tail_sems.at[j])
        for j, block in enumerate(peer)
    ]
    for copy in copies:
        copy.start()
    wide = chunks.shape[2]
    at = pl.ds(pl.multiple_of(lax.rem(z, PARTS) * wide, wide), wide)
    chunks[yhi] = own_ref[:, at]
    for copy in copies:
        copy.wait()
    mixed = tails[0].astype(F32)
    for j in range(1, 8):
        mixed += tails[j].astype(F32)
    mixed = mixed.astype(BF16)
    mixed = jnp.concatenate([mixed[:, i * 256 : i * 256 + 256] for i in range(4)])
    chunks[1 - yhi] = rows[:, at]
    peer_cots, own_cots = cotangent_of(rows, up), own_cots_ref[...]
    cots = jnp.concatenate(
        [jnp.where(yhi == 0, own_cots, peer_cots), jnp.where(yhi == 0, peer_cots, own_cots)]
    )
    cots_ref[...] = cots
    columns = chunks[...].reshape(256, wide)
    up_part = ADAPTER_SCALE * jnp.dot(mixed, columns, preferred_element_type=F32)
    down_part = lax.dot_general(cots, o_ref[...], FIRST, preferred_element_type=F32)
    down_part = ADAPTER_SCALE * down_part
    cut = wide // 2
    first = jnp.concatenate([up_part[:, :cut], down_part[:, :256]], 1)
    second = jnp.concatenate([up_part[:, cut:], down_part[:, 256:]], 1)
    mine_ref[...] = jnp.where(core == 0, first, second)
    yours_ref[...] = jnp.where(core == 0, second, first).astype(BF16)


def adapter_call(where, peer, up, own_rows, own_cots, o):
    vmem = pl.BlockSpec(memory_space=pltpu.VMEM)
    anywhere = pl.BlockSpec(memory_space=pl.ANY)
    rank, width = up.shape
    return pl.pallas_call(
        adapter_kernel,
        out_shape=(
            jax.ShapeDtypeStruct((128, width), BF16),
            jax.ShapeDtypeStruct((256, rank), BF16),
            jax.ShapeDtypeStruct((rank, width // PARTS // 2 + 256), F32),
            jax.ShapeDtypeStruct((rank, width // PARTS // 2 + 256), BF16),
        ),
        in_specs=[pl.BlockSpec(memory_space=pltpu.SMEM)] + [anywhere] * 9 + [vmem] * 3,
        out_specs=(vmem,) * 4,
        scratch_shapes=[
            pltpu.VMEM((rank, width), BF16),
            pltpu.VMEM((8, 16, 1024), BF16),
            pltpu.VMEM((2, 128, width // PARTS), BF16),
            pltpu.SemaphoreType.DMA((8,)),
            pltpu.SemaphoreType.DMA((8,)),
            pltpu.SemaphoreType.DMA((width // STEP,)),
        ],
        compiler_params=pltpu.CompilerParams(vmem_limit_bytes=24 * 1024 * 1024),
        cost_estimate=pl.CostEstimate(flops=2 * 10**9, bytes_accessed=2**22, transcendentals=0),
    )(where, *peer, up, own_rows, own_cots, o)


def gradient_kernel(where_ref, own_ref, peer_ref, w_ref, cots_ref, down_ref, g_ref):
    yhi = where_ref[1]
    product = None
    for i in range(w_ref.shape[1] // STEP):
        at = slice(i * STEP, (i + 1) * STEP)
        rows = jnp.concatenate([own_ref[:, at], peer_ref[:, at]])
        term = lax.dot_general(rows, w_ref[:, at], LAST, preferred_element_type=F32)
        product = term if product is None else product + term
    adapter = jnp.dot(cots_ref[...], down_ref[...], preferred_element_type=F32)
    adapter = ADAPTER_SCALE * adapter
    for half in range(2):
        part = jnp.where(yhi == half, product[:128], product[128:])
        g_ref[half] = (part + adapter[half * 128 : half * 128 + 128]).astype(BF16)


def gradient_call(where, own_rows, peer_rows, w, cots, down):
    vmem = pl.BlockSpec(memory_space=pltpu.VMEM)
    return pl.pallas_call(
        gradient_kernel,
        out_shape=jax.ShapeDtypeStruct((2, 128, w.shape[0]), BF16),
        in_specs=[pl.BlockSpec(memory_space=pltpu.SMEM)] + [vmem] * 5,
        out_specs=vmem,
        compiler_params=pltpu.CompilerParams(vmem_limit_bytes=20 * 1024 * 1024),
        cost_estimate=pl.CostEstimate(flops=10**10, bytes_accessed=2**23, transcendentals=0),
    )(where, own_rows, peer_rows, w, cots, down)


def tile(q, g, norm, delta, keys, values, visible):
    scale = HEAD_DIM**-0.5
    scores = lax.dot_general(keys, q, LAST, preferred_element_type=F32)
    prob = jnp.exp2(scores * (scale * LOG2E) - norm)
    if visible is not None:
        prob = jnp.where(visible, prob, 0.0)
    prob_grad = lax.dot_general(values, g, LAST, preferred_element_type=F32)
    score_grad = (prob * (prob_grad - delta)).astype(BF16)
    value_grad = jnp.dot(prob.astype(BF16), g, preferred_element_type=F32)
    key_grad = jnp.dot(score_grad, q, preferred_element_type=F32) * scale
    query_grad = lax.dot_general(score_grad, keys, FIRST, preferred_element_type=F32)
    return query_grad, key_grad, value_grad


def late_kernel(
    q_ref, o_ref, g_ref, norm_ref, kv_ref, other_kv_ref,
    qs, gs, norm, delta, dq_sum, dkv_ref, other_dkv_ref,
):
    heads = q_ref.shape[1] // HEAD_DIM
    for half in range(2):
        rows = slice(half * HALF, (half + 1) * HALF)
        for h in range(heads):
            cols = slice(h * HEAD_DIM, (h + 1) * HEAD_DIM)
            into = slice(h * HALF, (h + 1) * HALF)
            qs[half, into, :] = q_ref[rows, cols]
            norm[half, :, into] = norm_ref[h : h + 1, rows] * LOG2E
            g = g_ref[half, :, cols]
            gs[half, into, :] = g
            product = g.astype(F32) * o_ref[rows, cols].astype(F32)
            delta[half, :, into] = jnp.sum(product.T, axis=0, keepdims=True)
    dq_sum[0] = jnp.zeros_like(dq_sum[0])
    for source, to in ((kv_ref, dkv_ref), (other_kv_ref, other_dkv_ref)):
        to[:, HALF:, :] = jnp.zeros((8, HALF, 2 * HEAD_DIM), BF16)
        for k in range(0, 8, 2):
            keys = source[k : k + 2, :HALF, :HEAD_DIM].reshape(2 * HALF, HEAD_DIM)
            values = source[k : k + 2, :HALF, HEAD_DIM:].reshape(2 * HALF, HEAD_DIM)
            query_grad, key_grad, value_grad = tile(
                qs[1], gs[1], norm[1], delta[1], keys, values, None
            )
            if k or source is not kv_ref:
                dq_sum[1] += query_grad
            else:
                dq_sum[1] = query_grad
            key_grad = key_grad.astype(BF16).reshape(2, HALF, HEAD_DIM)
            value_grad = value_grad.astype(BF16).reshape(2, HALF, HEAD_DIM)
            to[k : k + 2, :HALF, :HEAD_DIM] = key_grad
            to[k : k + 2, :HALF, HEAD_DIM:] = value_grad


def rest_kernel(
    where_ref, qs, gs, norm, delta, dq_in, kv_ref, other_kv_ref, dkv_in, other_dkv_in,
    dq_ref, mine_ref, yours_ref, dq_sum, kv, dkv_ref,
):
    c, core = where_ref[0], where_ref[3]
    heads = dq_ref.shape[1] // HEAD_DIM
    scale = HEAD_DIM**-0.5
    kv[0], kv[1] = kv_ref[...], other_kv_ref[...]
    dkv_ref[0], dkv_ref[1] = dkv_in[...], other_dkv_in[...]
    dq_sum[...] = dq_in[...]
    key_at = lax.broadcasted_iota(jnp.int32, (HALF, heads * HALF), 0)
    query_at = lax.broadcasted_iota(jnp.int32, (HALF, heads * HALF), 1) % HALF
    ahead = query_at - key_at

    def unit(i):
        late = (i > c).astype(jnp.int32)
        s = i - late
        first = pl.multiple_of(late * HALF, HALF)
        visible = ahead >= jnp.where(s == c, 0, -HALF)
        other = jnp.where(lax.rem(s, 2) == core, 0, 1)
        k = lax.div(s, 2)
        keys = kv[other, k, pl.ds(first, HALF), :HEAD_DIM]
        values = kv[other, k, pl.ds(first, HALF), HEAD_DIM:]
        query_grad, key_grad, value_grad = tile(
            qs[late], gs[late], norm[late], delta[late], keys, values, visible
        )
        return late, (other, k), first, query_grad, jnp.concatenate([key_grad, value_grad], 1)

    def stored(late, block, first, query_grad, now):
        dq_sum[late] += query_grad
        before = dkv_ref[*block, pl.ds(first, HALF), :].astype(F32)
        dkv_ref[*block, pl.ds(first, HALF), :] = (before + now).astype(BF16)

    for first in range(0, 17, 4):
        for done in [unit(i) for i in range(first, min(first + 4, 17))]:
            stored(*done)
    mine_ref[...] = dkv_ref[0]
    yours_ref[...] = dkv_ref[1]
    for half in range(2):
        for h in range(heads):
            dq_ref[half * HALF : (half + 1) * HALF, h * HEAD_DIM : (h + 1) * HEAD_DIM] = (
                dq_sum[half, h * HALF : (h + 1) * HALF, :] * scale
            ).astype(BF16)


def late_call(q, o, g, log_norm, kv, other_kv):
    side = q.shape[1] // HEAD_DIM * HALF
    vmem = pl.BlockSpec(memory_space=pltpu.VMEM)
    stacked = jax.ShapeDtypeStruct((2, side, HEAD_DIM), BF16)
    line = jax.ShapeDtypeStruct((2, 1, side), F32)
    half = jax.ShapeDtypeStruct(kv.shape, BF16)
    return pl.pallas_call(
        late_kernel,
        out_shape=(
            stacked,
            stacked,
            line,
            line,
            jax.ShapeDtypeStruct((2, side, HEAD_DIM), F32),
            half,
            half,
        ),
        in_specs=[vmem] * 6,
        out_specs=(vmem,) * 7,
        compiler_params=pltpu.CompilerParams(vmem_limit_bytes=24 * 1024 * 1024),
        cost_estimate=pl.CostEstimate(
            flops=10**10, bytes_accessed=2**22, transcendentals=10**6
        ),
    )(q, o, g, log_norm, kv, other_kv)


def rest_call(where, kept, kv, other_kv):
    qs, gs, norm, delta, dq, dkv, other_dkv = kept
    side = qs.shape[1]
    vmem = pl.BlockSpec(memory_space=pltpu.VMEM)
    half = jax.ShapeDtypeStruct(dkv.shape, BF16)
    return pl.pallas_call(
        rest_kernel,
        out_shape=(jax.ShapeDtypeStruct((2 * HALF, side), BF16), half, half),
        in_specs=[pl.BlockSpec(memory_space=pltpu.SMEM)] + [vmem] * 9,
        out_specs=(vmem,) * 3,
        scratch_shapes=[
            pltpu.VMEM((2, side, HEAD_DIM), F32),
            pltpu.VMEM((2, *kv.shape), BF16),
            pltpu.VMEM((2, *dkv.shape), BF16),
        ],
        compiler_params=pltpu.CompilerParams(vmem_limit_bytes=24 * 1024 * 1024),
        cost_estimate=pl.CostEstimate(
            flops=10**10, bytes_accessed=2**22, transcendentals=10**6
        ),
    )(where, qs, gs, norm, delta, dq, kv, other_kv, dkv, other_dkv)


def local(q, k, v, o, log_norm, dy, w, down, up):
    ylo, x, core, yhi, z = (lax.axis_index(a) for a in CTX + TP)
    where = jnp.stack([ylo * 8 + x * 2 + core, yhi, z, core]).astype(jnp.int32)
    together = lax.optimization_barrier
    own_blocks = gathered_round(dy, "z", True)
    mixed = lax.dot_general(down, o, (((0,), (1,)), ((), ())), preferred_element_type=F32)
    mixed = jnp.concatenate([mixed[i * 16 : i * 16 + 16] for i in range(4)], 1)
    peer = turned(dy, "yhi", 1)
    other = turned(mixed.astype(BF16), "yhi", 1)
    peer = jnp.concatenate([peer, (mixed + other.astype(F32)).astype(BF16)], 1)
    kv, peer = together((jnp.concatenate([k, v], 1), peer))
    kv = lax.all_to_all(jnp.broadcast_to(kv[None], (8,) + kv.shape), CTX[:2], 0, 0)
    own_blocks, kv = together((own_blocks, kv))
    other_kv = turned(kv, "core", 1)
    own_rows, own_cots = own_call(where, own_blocks, up)
    peer_blocks = gathered_round(peer, "z", False)
    peer_rows, cots, mine, yours = adapter_call(where, peer_blocks, up, own_rows, own_cots, o)
    low = (mine + turned(yours, "core", 1).astype(F32)).astype(BF16)
    cots, low = together((cots, low))
    g = gradient_call(where, own_rows, peer_rows, w, cots, down.T)
    total = low.astype(F32) + turned(low, "ylo", 1).astype(F32)
    low, g = together((total.astype(BF16), g))
    kept = late_call(q, o, g, log_norm, kv, other_kv)
    total = low.astype(F32) + lax.ppermute(low, "x", [(i, i ^ 1) for i in range(4)]).astype(F32)
    low, kept = together((total.astype(BF16), kept))
    dq, mine, yours = rest_call(where, kept, kv, other_kv)
    total = low.astype(F32) + lax.ppermute(low, "x", [(i, 3 - i) for i in range(4)]).astype(F32)
    low, mine, yours = together((total.astype(BF16), mine, yours))
    other = turned(low, "core", 1)
    mine = (mine.astype(F32) + turned(yours, "core", 1).astype(F32)).astype(BF16)
    other, mine = together((other, mine))
    pieces = lax.all_to_all(mine, CTX[:2], 0, 0)
    first, second = jnp.where(core == 0, low, other), jnp.where(core == 0, other, low)
    cut = low.shape[1] - 256
    down_grad = jnp.concatenate([first[:, cut:], second[:, cut:]], 1).astype(F32).T
    up_total = jnp.concatenate([first[:, :cut], second[:, :cut]], 1)
    before, after = turned(up_total, "z", 1), turned(up_total, "z", -1)
    far = (turned(before[:, :cut], "z", 1), turned(after[:, cut:], "z", -1))
    up_grad = placed_round(where, [up_total, after, *far, before])
    dkv_sum, low = summed(pieces)
    other = lax.ppermute(low, "z", [(i, i ^ 1) for i in range(8)])
    dkv_sum = (dkv_sum + other.astype(F32)).astype(BF16)
    return dq, dkv_sum[:, :128], dkv_sum[:, 128:], down_grad, up_grad


def solution(mesh):
    fine = Mesh(mesh.devices.reshape(SIZES), CTX + TP)
    placed = (
        P(CTX, TP),
        P(CTX, TP),
        P(CTX, TP),
        P(CTX, TP),
        P(TP, CTX),
        P(CTX + TP, None),
        P(TP, None),
        P(TP, None),
        P(),
    )
    return jax.shard_map(
        local,
        mesh=fine,
        in_specs=placed,
        out_specs=(P(CTX, TP), P(CTX, TP), P(CTX, TP), P(TP, None), P()),
        check_vma=False,
    )
```

time: 140 us -> 126 us (0.900)
  Pallas kernels: 32 us -> 21.4 us
  starting transfers between devices: 57.2 us -> 47.7 us
  waiting for transfers between devices: 39.5 us -> 44.5 us
    pallas_call x3, Pallas kernels: 20.7 us -> 9.77 us  [the longest x1 3.8 us: adapter_call(): pl.pallas_call(adapter_kernel, out_shape=(jax.ShapeDtypeStruct((128, widt...]
    ppermute x27 -> x25, starting transfers between devices: 43.6 us -> 34.3 us  [turned(): return lax.ppermute(x, axis, [(i, (i + by) % size) for i in range(size)])]
    ppermute x1, waiting for transfers between devices: 0.01 us -> 2.67 us  [local(): other = lax.ppermute(low, 'z', [(i, i ^ 1) for i in range(8)])]
    all_to_all x1, waiting for transfers between devices: 0.01 us -> 2.28 us  [local(): pieces = lax.all_to_all(mine, CTX[:2], 0, 0)]
    unnamed x38 -> x26, local copies, waits for them, and re-layouts: 2.84 us -> 4.29 us
    ppermute x27 -> x25, waiting for transfers between devices: 35.4 us -> 34.4 us  [turned(): return lax.ppermute(x, axis, [(i, (i + by) % size) for i in range(size)])]
  transfers between devices with their start and end apart: 32 -> 30, of which waited for: 13 -> 15; matrix products, arithmetic and copies ran while one was open for 4% -> 4% of each run, Pallas kernels for 21% -> 11%
where the time goes in v1:
time: 126 us; the launch traced here: 125 us
  starting transfers between devices  47.7 us (38%)
  waiting for transfers between devices  44.5 us (35%)
  Pallas kernels  21.4 us (17%)
  local copies, waits for them, and re-layouts  6.04 us (5%)
  other arithmetic  3.13 us (2%)
    ppermute x25, waiting for transfers between devices, turned(): return lax.ppermute(x, axis, [(i, (i + by) % size) for i in range(size)])  34.4 us
    ppermute x25, starting transfers between devices, turned(): return lax.ppermute(x, axis, [(i, (i + by) % size) for i in range(size)])  34.3 us
    pallas_call x1, Pallas kernels, rest_call(): pl.pallas_call(rest_kernel, out_shape=(jax.ShapeDtypeStruct((2 * HALF, si...  6.58 us
    all_to_all x1, starting transfers between devices, local(): lax.all_to_all(jnp.broadcast_to(kv[None], (8,) + kv.shape), CTX[:2], 0, 0)  5.84 us
    all_to_all x1, starting transfers between devices, local(): pieces = lax.all_to_all(mine, CTX[:2], 0, 0)  5.24 us
    ppermute x1, waiting for transfers between devices, local(): lax.ppermute(low, 'x', [(i, i ^ 1) for i in range(4)]).astype(F32)  5.14 us
    unnamed x26, local copies, waits for them, and re-layouts  4.29 us
    pallas_call x1, Pallas kernels, adapter_call(): pl.pallas_call(adapter_kernel, out_shape=(jax.ShapeDtypeStruct((128, widt...  3.8 us
  transfers between devices with their start and end apart: 30, of which 15 were waited for; matrix products, arithmetic and copies ran while one was open for 4% of the time, Pallas kernels for 11%

profile of v1, /device:TPU:2, one launch (start us, length us, event | category | flops | bytes accessed | tf_op | source)
XLA Modules:
  0.0 124.9 jit_solution(7866804515630532720)
XLA Ops:
  0.6 3.3 %collective-permute-start = (bf16[16,8192]{1,0:T(8,128)(2,1)}, bf16[16,8192]{1,0:T(8,128)(2,1)S(1)}, u32[]{:S(2)}, u32[]{:S(2)}) collective-permute-start(bf16[16,8192]{1,0:T(8,128)(2,1)} %refs_0_), channel_id=1, source_target_pairs={{0,8},{8,0},{1,9},{9,1},{2,10},{10,2},{3,11},{11,3},{4,12},{12,4},... | collective-permute-start | bytes 786440 | tf_op jit(solution)/shard_map/ppermute | solution.py:25
  3.9 1.9 %collective-permute-start.12 = (bf16[16,8192]{1,0:T(8,128)(2,1)}, bf16[16,8192]{1,0:T(8,128)(2,1)}, u32[]{:S(2)}, u32[]{:S(2)}) collective-permute-start(bf16[16,8192]{1,0:T(8,128)(2,1)} %refs_0_), channel_id=1, source_target_pairs={{0,1},{1,2},{2,3},{3,4},{4,5},{5,6},{6,7},{7,0},{8,9},{9,10},{10,1... | collective-permute-start | bytes 786440 | tf_op jit(solution)/shard_map/ppermute | solution.py:25
  5.8 1.2 fusion.3
  7.1 0.4 collective-permute-start.1
  7.5 0.9 pad_maximum_fusion.2
  8.4 4.2 %collective-permute-done.1 = bf16[16,1024]{1,0:T(8,128)(2,1)S(1)} collective-permute-done((bf16[16,1024]{1,0:T(8,128)(2,1)S(1)}, bf16[16,1024]{1,0:T(8,128)(2,1)S(1)}, u32[]{:S(2)}, u32[]{:S(2)}) %collective-permute-start.1) | collective-permute-done | bytes 32800 | tf_op jit(solution)/shard_map/ppermute | solution.py:25
  12.6 4.5 %collective-permute-start.2 = (bf16[16,9216]{1,0:T(8,128)(2,1)S(1)}, bf16[16,9216]{1,0:T(8,128)(2,1)S(1)}, u32[]{:S(2)}, u32[]{:S(2)}) collective-permute-start(bf16[16,9216]{1,0:T(8,128)(2,1)S(1)} %pad_maximum_fusion.refs_0_), channel_id=1, source_target_pairs={{0,7},{1,0},{2,1},{3,2},{4,3},{5,4},{6,5},{7,6},{8,15},{9,8},{10,9... | collective-permute-start | bytes 884744 | tf_op jit(solution)/shard_map/ppermute | solution.py:25
  17.2 1.0 broadcast_in_dim.2
  18.2 5.8 %all-to-all-start = ((bf16[8,256,256]{2,1,0:T(8,128)(2,1)}), bf16[8,256,256]{2,1,0:T(8,128)(2,1)S(1)}, u32[]{:S(2)}, u32[]{:S(2)}) async-start(bf16[8,256,256]{2,1,0:T(8,128)(2,1)} %broadcast_in_dim.2), calls=%async_computation | async-start | bytes 2097152 | tf_op jit(solution)/shard_map/all_to_all | solution.py:403
  24.0 1.0 collective-permute-start.9
  25.1 1.0 collective-permute-start.13
  26.1 0.0 collective-permute-start.6
  26.1 3.2 %collective-permute-start.3 = (bf16[16,9216]{1,0:T(8,128)(2,1)S(1)}, bf16[16,9216]{1,0:T(8,128)(2,1)}, u32[]{:S(2)}, u32[]{:S(2)}) collective-permute-start(bf16[16,9216]{1,0:T(8,128)(2,1)S(1)} %collective-permute-done.2.refs_1_), channel_id=1, source_target_pairs={{0,7},{1,0},{2,1},{3,2},{4,3},{5,4},{6,5},{7,6},{8,15},{9,8},{10,9... | collective-permute-start | bytes 884744 | tf_op jit(solution)/shard_map/ppermute | solution.py:25
  29.3 4.0 %collective-permute-done.9.refs_1_ = bf16[16,8192]{1,0:T(8,128)(2,1)S(1)} collective-permute-done((bf16[16,8192]{1,0:T(8,128)(2,1)S(1)}, bf16[16,8192]{1,0:T(8,128)(2,1)S(1)}, u32[]{:S(2)}, u32[]{:S(2)}) %collective-permute-start.9) | collective-permute-done | bytes 262176 | tf_op jit(solution)/shard_map/ppermute | solution.py:25
  33.3 1.6 %collective-permute-start.10 = (bf16[16,8192]{1,0:T(8,128)(2,1)S(1)}, bf16[16,8192]{1,0:T(8,128)(2,1)}, u32[]{:S(2)}, u32[]{:S(2)}) collective-permute-start(bf16[16,8192]{1,0:T(8,128)(2,1)S(1)} %collective-permute-done.9.refs_1_), channel_id=1, source_target_pairs={{0,7},{1,0},{2,1},{3,2},{4,3},{5,4},{6,5},{7,6},{8,15},{9,8},{10,9... | collective-permute-start | bytes 786440 | tf_op jit(solution)/shard_map/ppermute | solution.py:25
  34.9 0.7 copy-done.6
  35.6 0.1 collective-permute-done.13.refs_6_
  35.7 0.3 collective-permute-start.14
  36.0 0.7 copy-done.8
  36.7 5.3 %collective-permute-done.6.refs_7_ = bf16[16,9216]{1,0:T(8,128)(2,1)S(1)} collective-permute-done((bf16[16,9216]{1,0:T(8,128)(2,1)S(1)}, bf16[16,9216]{1,0:T(8,128)(2,1)S(1)}, u32[]{:S(2)}, u32[]{:S(2)}) %collective-permute-start.6) | collective-permute-done | bytes 294944 | tf_op jit(solution)/shard_map/ppermute | solution.py:25
  42.1 3.2 %collective-permute-start.4 = (bf16[16,9216]{1,0:T(8,128)(2,1)}, bf16[16,9216]{1,0:T(8,128)(2,1)}, u32[]{:S(2)}, u32[]{:S(2)}) collective-permute-start(bf16[16,9216]{1,0:T(8,128)(2,1)} %collective-permute-done.3.refs_2_), channel_id=1, source_target_pairs={{0,7},{1,0},{2,1},{3,2},{4,3},{5,4},{6,5},{7,6},{8,15},{9,8},{10,9... | collective-permute-start | bytes 884744 | tf_op jit(solution)/shard_map/ppermute | solution.py:25
  45.3 0.0 collective-permute-done.10.refs_2_
  45.3 1.1 collective-permute-start.11
  46.4 1.3 %collective-permute-done.14.refs_5_ = bf16[16,8192]{1,0:T(8,128)(2,1)} collective-permute-done((bf16[16,8192]{1,0:T(8,128)(2,1)S(1)}, bf16[16,8192]{1,0:T(8,128)(2,1)}, u32[]{:S(2)}, u32[]{:S(2)}) %collective-permute-start.14) | collective-permute-done | bytes 262176 | tf_op jit(solution)/shard_map/ppermute | solution.py:25
  47.8 6.3 %collective-permute-done.7.refs_6_ = bf16[16,9216]{1,0:T(8,128)(2,1)} collective-permute-done((bf16[16,9216]{1,0:T(8,128)(2,1)S(1)}, bf16[16,9216]{1,0:T(8,128)(2,1)}, u32[]{:S(2)}, u32[]{:S(2)}) %collective-permute-start.7) | collective-permute-done | bytes 294944 | tf_op jit(solution)/shard_map/ppermute | solution.py:25
  54.1 3.2 %collective-permute-start.5 = (bf16[16,9216]{1,0:T(8,128)(2,1)}, bf16[16,9216]{1,0:T(8,128)(2,1)}, u32[]{:S(2)}, u32[]{:S(2)}) collective-permute-start(bf16[16,9216]{1,0:T(8,128)(2,1)} %collective-permute-done.4.refs_3_), channel_id=1, source_target_pairs={{0,7},{1,0},{2,1},{3,2},{4,3},{5,4},{6,5},{7,6},{8,15},{9,8},{10,9... | collective-permute-start | bytes 884744 | tf_op jit(solution)/shard_map/ppermute | solution.py:25
  57.3 0.1 pad_add_fusion.where_ref
  57.4 0.1 collective-permute-done.11.refs_3_
  57.5 2.2 %collective-permute-done.15.refs_4_ = bf16[16,8192]{1,0:T(8,128)(2,1)} collective-permute-done((bf16[16,8192]{1,0:T(8,128)(2,1)}, bf16[16,8192]{1,0:T(8,128)(2,1)}, u32[]{:S(2)}, u32[]{:S(2)}) %collective-permute-start.15) | collective-permute-done | bytes 262176 | tf_op jit(solution)/shard_map/ppermute | solution.py:25
  59.7 0.9 copy-done.4
  60.6 0.9 copy-done.7
  61.6 0.9 copy-done.9
  62.5 3.0 %shard_map.128 = (bf16[128,8192]{1,0:T(8,128)(2,1)S(1)}, bf16[128,64]{1,0:T(8,128)(2,1)S(1)}) custom-call(s32[4]{0:T(128)S(1)} %pad_add_fusion.where_ref, bf16[16,8192]{1,0:T(8,128)(2,1)S(1)} %copy-done.4, bf16[16,8192]{1,0:T(8,128)(2,1)S(1)} %copy-done.7, bf16[16,8192]{1,0:T(8,128)(2,1)} %collective-permute-done.10.refs_2_, ...), custom_call_target="tpu_custom_call" | custom-call | flops 2000000000 | bytes 4194304 | tf_op jit(solution)/shard_map/pallas_call | solution.py:139
  65.6 0.0 copy-start.1
  65.6 0.0 slice-start.1
  65.6 3.8 %shard_map.129 = (bf16[128,8192]{1,0:T(8,128)(2,1)S(1)}, bf16[256,64]{1,0:T(8,128)(2,1)S(1)}, f32[64,1280]{1,0:T(8,128)S(1)}, bf16[64,1280]{1,0:T(8,128)(2,1)S(1)}) custom-call(s32[4]{0:T(128)S(1)} %pad_add_fusion.where_ref, bf16[16,9216]{1,0:T(8,128)(2,1)S(1)} %pad_maximum_fusion.refs_0_, bf16[16,9216]{1,0:T(8,128)(2,1)S(1)} %collective-permute-done.2.refs_1_, ...), custom_call_target="tpu_custom_call" | custom-call | flops 2000000000 | bytes 4194304 | tf_op jit(solution)/shard_map/pallas_call | solution.py:200
  69.4 0.1 collective-permute-start.16
  69.5 0.5 collective-permute-start.19
  70.0 0.9 collective-permute-done.16
  70.9 1.5 %collective-permute-start.17 = (bf16[64,1280]{1,0:T(8,128)(2,1)S(1)}, bf16[64,1280]{1,0:T(8,128)(2,1)S(1)}, u32[]{:S(2)}, u32[]{:S(2)}) collective-permute-start(bf16[64,1280]{1,0:T(8,128)(2,1)S(1)} %add_convert_fusion.4), channel_id=1, source_target_pairs={{0,128},{128,0},{1,129},{129,1},{2,130},{130,2},{3,131},{131,3},{4... | collective-permute-start | bytes 491528 | tf_op jit(solution)/shard_map/ppermute | solution.py:25
  72.5 3.0 %shard_map.130.g_ref = bf16[2,128,512]{2,1,0:T(8,128)(2,1)S(1)} custom-call(s32[4]{0:T(128)S(1)} %pad_add_fusion.where_ref, bf16[128,8192]{1,0:T(8,128)(2,1)S(1)} %get-tuple-element.61.refs_9_.own_ref, bf16[128,8192]{1,0:T(8,128)(2,1)S(1)} %get-tuple-element.67.peer_ref, bf16[512,8192]{1,0:T(8,128)(2,1)S(1)} %bitcast.11, ...), custom_call_target="tpu_custom_call" | custom-call | flops 10000000000 | bytes 8388608 | tf_op jit(solution)/shard_map/pallas_call | solution.py:240
  75.5 1.8 %collective-permute-done.17 = bf16[64,1280]{1,0:T(8,128)(2,1)S(1)} collective-permute-done((bf16[64,1280]{1,0:T(8,128)(2,1)S(1)}, bf16[64,1280]{1,0:T(8,128)(2,1)S(1)}, u32[]{:S(2)}, u32[]{:S(2)}) %collective-permute-start.17) | collective-permute-done | bytes 163872 | tf_op jit(solution)/shard_map/ppermute | solution.py:25
  77.3 0.4 collective-permute-start.18
  77.7 5.1 %collective-permute-done.18 = bf16[64,1280]{1,0:T(8,128)(2,1)S(1)} collective-permute-done((bf16[64,1280]{1,0:T(8,128)(2,1)S(1)}, bf16[64,1280]{1,0:T(8,128)(2,1)S(1)}, u32[]{:S(2)}, u32[]{:S(2)}) %collective-permute-start.18) | collective-permute-done | bytes 163872 | tf_op jit(solution)/shard_map/ppermute | solution.py:415
  82.9 3.3 %shard_map.131 = (bf16[2,512,128]{2,1,0:T(8,128)(2,1)S(1)}, bf16[2,512,128]{2,1,0:T(8,128)(2,1)S(1)}, f32[2,1,512]{2,1,0:T(1,128)S(1)}, f32[2,1,512]{2,1,0:T(1,1...) custom-call(bf16[256,512]{1,0:T(8,128)(2,1)S(1)} %copy-done.5, ...), custom_call_target="tpu_custom_call" | custom-call | flops 10000000000 | bytes 4194304 | tf_op jit(solution)/shard_map/pallas_call | solution.py:350
  86.2 1.8 %collective-permute-start.20 = (bf16[64,1280]{1,0:T(8,128)(2,1)S(1)}, bf16[64,1280]{1,0:T(8,128)(2,1)S(1)}, u32[]{:S(2)}, u32[]{:S(2)}) collective-permute-start(bf16[64,1280]{1,0:T(8,128)(2,1)S(1)} %add_convert_fusion.2), channel_id=1, source_target_pairs={{0,96},{32,64},{64,32},{96,0},{1,97},{33,65},{65,33},{97,1},{2,98}... | collective-permute-start | bytes 491528 | tf_op jit(solution)/shard_map/ppermute | solution.py:418
  88.0 6.6 %shard_map.132 = (bf16[256,512]{1,0:T(8,128)(2,1)}, bf16[8,256,256]{2,1,0:T(8,128)(2,1)S(1)}, bf16[8,256,256]{2,1,0:T(8,128)(2,1)S(1)}) custom-call(s32[4]{0:T(128)S(1)} %pad_add_fusion.where_ref, bf16[2,512,128]{2,1,0:T(8,128)(2,1)S(1)} %get-tuple-element.79.qs, bf16[2,512,128]{2,1,0:T(8,128)(2,1)S(1)} %get-tuple-element.80.gs, ...), custom_call_target="tpu_custom_call" | custom-call | flops 10000000000 | bytes 4194304 | tf_op jit(solution)/shard_map/pallas_call | solution.py:375
  94.6 0.1 collective-permute-start.22
  94.7 0.5 collective-permute-start.21
  95.2 2.1 %collective-permute-done.22 = bf16[8,256,256]{2,1,0:T(8,128)(2,1)S(1)} collective-permute-done((bf16[8,256,256]{2,1,0:T(8,128)(2,1)S(1)}, bf16[8,256,256]{2,1,0:T(8,128)(2,1)S(1)}, u32[]{:S(2)}, u32[]{:S(2)}) %collective-permute-start.22) | collective-permute-done | bytes 1048608 | tf_op jit(solution)/shard_map/ppermute | solution.py:25
  97.4 1.2 add_convert_fusion
  98.6 5.2 %all-to-all-start.1 = ((bf16[8,256,256]{2,1,0:T(8,128)(2,1)}), bf16[8,256,256]{2,1,0:T(8,128)(2,1)S(1)}, u32[]{:S(2)}, u32[]{:S(2)}) async-start(bf16[8,256,256]{2,1,0:T(8,128)(2,1)} %add_convert_fusion), calls=%async_computation.1 | async-start | bytes 2097152 | tf_op jit(solution)/shard_map/all_to_all | solution.py:423
  103.9 0.1 collective-permute-start.25
  104.0 3.2 %collective-permute-start.24 = (bf16[64,2048]{1,0:T(8,128)(2,1)S(1)}, bf16[64,2048]{1,0:T(8,128)(2,1)S(1)}, u32[]{:S(2)}, u32[]{:S(2)}) collective-permute-start(bf16[64,2048]{1,0:T(8,128)(2,1)S(1)} %pad_maximum_fusion.1.refs_0_), channel_id=1, source_target_pairs={{0,7},{1,0},{2,1},{3,2},{4,3},{5,4},{6,5},{7,6},{8,15},{9,8},{10,9... | collective-permute-start | bytes 786440 | tf_op jit(solution)/shard_map/ppermute | solution.py:25
  107.2 6.0 %collective-permute-done.25.refs_4_ = bf16[64,2048]{1,0:T(8,128)(2,1)S(1)} collective-permute-done((bf16[64,2048]{1,0:T(8,128)(2,1)S(1)}, bf16[64,2048]{1,0:T(8,128)(2,1)S(1)}, u32[]{:S(2)}, u32[]{:S(2)}) %collective-permute-start.25) | collective-permute-done | bytes 262176 | tf_op jit(solution)/shard_map/ppermute | solution.py:25
  113.3 0.1 collective-permute-start.26
  113.4 3.3 %collective-permute-start.27 = (bf16[64,1024]{1,0:T(8,128)(2,1)S(1)}, bf16[64,1024]{1,0:T(8,128)(2,1)S(1)}, u32[]{:S(2)}, u32[]{:S(2)}) collective-permute-start(bf16[64,1024]{1,0:T(8,128)(2,1)S(1)} %slice.59), channel_id=1, source_target_pairs={{0,7},{1,0},{2,1},{3,2},{4,3},{5,4},{6,5},{7,6},{8,15},{9,8},{10,9... | collective-permute-start | bytes 393224 | tf_op jit(solution)/shard_map/ppermute | solution.py:25
  116.7 2.3 %all-to-all-done.1.pieces_ref = bf16[8,256,256]{2,1,0:T(8,128)(2,1)S(1)} async-done(((bf16[8,256,256]{2,1,0:T(8,128)(2,1)}), bf16[8,256,256]{2,1,0:T(8,128)(2,1)S(1)}, u32[]{:S(2)}, u32[]{:S(2)}) %all-to-all-start.1) | async-done | bytes 1048608 | tf_op jit(solution)/shard_map/all_to_all | solution.py:423
  119.0 0.1 shard_map.133
  119.1 0.1 collective-permute-start.23
  119.2 0.7 convert_bitcast_fusion
  119.9 1.6 %shard_map.134 = bf16[64,8192]{1,0:T(8,128)(2,1)} custom-call(s32[4]{0:T(128)S(1)} %pad_add_fusion.where_ref, bf16[64,2048]{1,0:T(8,128)(2,1)S(1)} %pad_maximum_fusion.1.refs_0_, bf16[64,2048]{1,0:T(8,128)(2,1)S(1)} %collective-permute-done.24.refs_1_, bf16[64,1024]{1,0:T(8,128)(2,1)S(1)} %collective-permute-done.26.refs_2_, ...), custom_call_target="tpu_custom_call" | custom-call | bytes 1048576 | tf_op jit(solution)/shard_map/pallas_call | solution.py:58
  121.5 2.7 %collective-permute-done.23 = bf16[256,256]{1,0:T(8,128)(2,1)S(1)} collective-permute-done((bf16[256,256]{1,0:T(8,128)(2,1)S(1)}, bf16[256,256]{1,0:T(8,128)(2,1)S(1)}, u32[]{:S(2)}, u32[]{:S(2)}) %collective-permute-start.23) | collective-permute-done | bytes 131104 | tf_op jit(solution)/shard_map/ppermute | solution.py:432
  124.2 0.7 fusion.1
  (54 shorter events, 0.4 us)
Async XLA Ops:
  0.6 12.0 %collective-permute-start = (bf16[16,8192]{1,0:T(8,128)(2,1)}, bf16[16,8192]{1,0:T(8,128)(2,1)S(1)}, u32[]{:S(2)}, u32[]{:S(2)}) collective-permute-start(bf16[16,8192]{1,0:T(8,128)(2,1)} %refs_0_), channel_id=1, source_target_pairs={{0,8},{8,0},{1,9},{9,1},{2,10},{10,2},{3,11},{11,3},{4,12},{12,4},... | collective-permute-start | bytes 786440 | tf_op jit(solution)/shard_map/ppermute | solution.py:25
  3.9 21.1 %collective-permute-start.12 = (bf16[16,8192]{1,0:T(8,128)(2,1)}, bf16[16,8192]{1,0:T(8,128)(2,1)}, u32[]{:S(2)}, u32[]{:S(2)}) collective-permute-start(bf16[16,8192]{1,0:T(8,128)(2,1)} %refs_0_), channel_id=1, source_target_pairs={{0,1},{1,2},{2,3},{3,4},{4,5},{5,6},{6,7},{7,0},{8,9},{9,10},{10,1... | collective-permute-start | bytes 786440 | tf_op jit(solution)/shard_map/ppermute | solution.py:25
  7.0 17.0 %copy-start.3 = (bf16[16,8192]{1,0:T(8,128)(2,1)S(1)}, bf16[16,8192]{1,0:T(8,128)(2,1)}, u32[]{:S(2)}) copy-start(bf16[16,8192]{1,0:T(8,128)(2,1)} %refs_0_) | copy-start | bytes 786436
  7.1 52.6 %copy-start.2 = (bf16[64,8192]{1,0:T(8,128)(2,1)S(1)}, bf16[64,8192]{1,0:T(8,128)(2,1)}, u32[]{:S(2)}) copy-start(bf16[64,8192]{1,0:T(8,128)(2,1)} %refs_8_.3) | copy-start | bytes 3145732
  7.1 5.5 %collective-permute-start.1 = (bf16[16,1024]{1,0:T(8,128)(2,1)S(1)}, bf16[16,1024]{1,0:T(8,128)(2,1)S(1)}, u32[]{:S(2)}, u32[]{:S(2)}) collective-permute-start(bf16[16,1024]{1,0:T(8,128)(2,1)S(1)} %fusion), channel_id=1, source_target_pairs={{0,8},{8,0},{1,9},{9,1},{2,10},{10,2},{3,11},{11,3},{4,12},{12,4},... | collective-permute-start | bytes 98312 | tf_op jit(solution)/shard_map/ppermute | solution.py:25
  12.6 13.5 %collective-permute-start.2 = (bf16[16,9216]{1,0:T(8,128)(2,1)S(1)}, bf16[16,9216]{1,0:T(8,128)(2,1)S(1)}, u32[]{:S(2)}, u32[]{:S(2)}) collective-permute-start(bf16[16,9216]{1,0:T(8,128)(2,1)S(1)} %pad_maximum_fusion.refs_0_), channel_id=1, source_target_pairs={{0,7},{1,0},{2,1},{3,2},{4,3},{5,4},{6,5},{7,6},{8,15},{9,8},{10,9... | collective-permute-start | bytes 884744 | tf_op jit(solution)/shard_map/ppermute | solution.py:25
  18.2 41.5 %all-to-all-start = ((bf16[8,256,256]{2,1,0:T(8,128)(2,1)}), bf16[8,256,256]{2,1,0:T(8,128)(2,1)S(1)}, u32[]{:S(2)}, u32[]{:S(2)}) async-start(bf16[8,256,256]{2,1,0:T(8,128)(2,1)} %broadcast_in_dim.2), calls=%async_computation | async-start | bytes 2097152 | tf_op jit(solution)/shard_map/all_to_all | solution.py:403
  24.0 9.2 %collective-permute-start.9 = (bf16[16,8192]{1,0:T(8,128)(2,1)S(1)}, bf16[16,8192]{1,0:T(8,128)(2,1)S(1)}, u32[]{:S(2)}, u32[]{:S(2)}) collective-permute-start(bf16[16,8192]{1,0:T(8,128)(2,1)S(1)} %copy-done.3), channel_id=1, source_target_pairs={{0,7},{1,0},{2,1},{3,2},{4,3},{5,4},{6,5},{7,6},{8,15},{9,8},{10,9... | collective-permute-start | bytes 786440 | tf_op jit(solution)/shard_map/ppermute | solution.py:25
  25.1 10.7 %collective-permute-start.13 = (bf16[16,8192]{1,0:T(8,128)(2,1)}, bf16[16,8192]{1,0:T(8,128)(2,1)S(1)}, u32[]{:S(2)}, u32[]{:S(2)}) collective-permute-start(bf16[16,8192]{1,0:T(8,128)(2,1)} %collective-permute-done.12.refs_7_), channel_id=1, source_target_pairs={{0,1},{1,2},{2,3},{3,4},{4,5},{5,6},{6,7},{7,0},{8,9},{9,10},{10,1... | collective-permute-start | bytes 786440 | tf_op jit(solution)/shard_map/ppermute | solution.py:25
  26.1 16.0 %collective-permute-start.6 = (bf16[16,9216]{1,0:T(8,128)(2,1)S(1)}, bf16[16,9216]{1,0:T(8,128)(2,1)S(1)}, u32[]{:S(2)}, u32[]{:S(2)}) collective-permute-start(bf16[16,9216]{1,0:T(8,128)(2,1)S(1)} %pad_maximum_fusion.refs_0_), channel_id=1, source_target_pairs={{0,1},{1,2},{2,3},{3,4},{4,5},{5,6},{6,7},{7,0},{8,9},{9,10},{10,1... | collective-permute-start | bytes 884744 | tf_op jit(solution)/shard_map/ppermute | solution.py:25
  26.1 15.9 %collective-permute-start.3 = (bf16[16,9216]{1,0:T(8,128)(2,1)S(1)}, bf16[16,9216]{1,0:T(8,128)(2,1)}, u32[]{:S(2)}, u32[]{:S(2)}) collective-permute-start(bf16[16,9216]{1,0:T(8,128)(2,1)S(1)} %collective-permute-done.2.refs_1_), channel_id=1, source_target_pairs={{0,7},{1,0},{2,1},{3,2},{4,3},{5,4},{6,5},{7,6},{8,15},{9,8},{10,9... | collective-permute-start | bytes 884744 | tf_op jit(solution)/shard_map/ppermute | solution.py:25
  33.3 12.0 %collective-permute-start.10 = (bf16[16,8192]{1,0:T(8,128)(2,1)S(1)}, bf16[16,8192]{1,0:T(8,128)(2,1)}, u32[]{:S(2)}, u32[]{:S(2)}) collective-permute-start(bf16[16,8192]{1,0:T(8,128)(2,1)S(1)} %collective-permute-done.9.refs_1_), channel_id=1, source_target_pairs={{0,7},{1,0},{2,1},{3,2},{4,3},{5,4},{6,5},{7,6},{8,15},{9,8},{10,9... | collective-permute-start | bytes 786440 | tf_op jit(solution)/shard_map/ppermute | solution.py:25
  34.9 0.7 copy-start.6
  35.7 12.0 %collective-permute-start.14 = (bf16[16,8192]{1,0:T(8,128)(2,1)S(1)}, bf16[16,8192]{1,0:T(8,128)(2,1)}, u32[]{:S(2)}, u32[]{:S(2)}) collective-permute-start(bf16[16,8192]{1,0:T(8,128)(2,1)S(1)} %collective-permute-done.13.refs_6_), channel_id=1, source_target_pairs={{0,1},{1,2},{2,3},{3,4},{4,5},{5,6},{6,7},{7,0},{8,9},{9,10},{10,1... | collective-permute-start | bytes 786440 | tf_op jit(solution)/shard_map/ppermute | solution.py:25
  36.0 0.7 copy-start.8
  42.0 12.0 %collective-permute-start.7 = (bf16[16,9216]{1,0:T(8,128)(2,1)S(1)}, bf16[16,9216]{1,0:T(8,128)(2,1)}, u32[]{:S(2)}, u32[]{:S(2)}) collective-permute-start(bf16[16,9216]{1,0:T(8,128)(2,1)S(1)} %collective-permute-done.6.refs_7_), channel_id=1, source_target_pairs={{0,1},{1,2},{2,3},{3,4},{4,5},{5,6},{6,7},{7,0},{8,9},{9,10},{10,1... | collective-permute-start | bytes 884744 | tf_op jit(solution)/shard_map/ppermute | solution.py:25
  42.1 12.0 %collective-permute-start.4 = (bf16[16,9216]{1,0:T(8,128)(2,1)}, bf16[16,9216]{1,0:T(8,128)(2,1)}, u32[]{:S(2)}, u32[]{:S(2)}) collective-permute-start(bf16[16,9216]{1,0:T(8,128)(2,1)} %collective-permute-done.3.refs_2_), channel_id=1, source_target_pairs={{0,7},{1,0},{2,1},{3,2},{4,3},{5,4},{6,5},{7,6},{8,15},{9,8},{10,9... | collective-permute-start | bytes 884744 | tf_op jit(solution)/shard_map/ppermute | solution.py:25
  45.3 12.2 %collective-permute-start.11 = (bf16[16,8192]{1,0:T(8,128)(2,1)}, bf16[16,8192]{1,0:T(8,128)(2,1)}, u32[]{:S(2)}, u32[]{:S(2)}) collective-permute-start(bf16[16,8192]{1,0:T(8,128)(2,1)} %collective-permute-done.10.refs_2_), channel_id=1, source_target_pairs={{0,7},{1,0},{2,1},{3,2},{4,3},{5,4},{6,5},{7,6},{8,15},{9,8},{10,9... | collective-permute-start | bytes 786440 | tf_op jit(solution)/shard_map/ppermute | solution.py:25
  47.8 11.9 %collective-permute-start.15 = (bf16[16,8192]{1,0:T(8,128)(2,1)}, bf16[16,8192]{1,0:T(8,128)(2,1)}, u32[]{:S(2)}, u32[]{:S(2)}) collective-permute-start(bf16[16,8192]{1,0:T(8,128)(2,1)} %collective-permute-done.14.refs_5_), channel_id=1, source_target_pairs={{0,1},{1,2},{2,3},{3,4},{4,5},{5,6},{6,7},{7,0},{8,9},{9,10},{10,1... | collective-permute-start | bytes 786440 | tf_op jit(solution)/shard_map/ppermute | solution.py:25
  54.1 11.5 %collective-permute-start.8 = (bf16[16,9216]{1,0:T(8,128)(2,1)}, bf16[16,9216]{1,0:T(8,128)(2,1)}, u32[]{:S(2)}, u32[]{:S(2)}) collective-permute-start(bf16[16,9216]{1,0:T(8,128)(2,1)} %collective-permute-done.7.refs_6_), channel_id=1, source_target_pairs={{0,1},{1,2},{2,3},{3,4},{4,5},{5,6},{6,7},{7,0},{8,9},{9,10},{10,1... | collective-permute-start | bytes 884744 | tf_op jit(solution)/shard_map/ppermute | solution.py:25
  54.1 11.5 %collective-permute-start.5 = (bf16[16,9216]{1,0:T(8,128)(2,1)}, bf16[16,9216]{1,0:T(8,128)(2,1)}, u32[]{:S(2)}, u32[]{:S(2)}) collective-permute-start(bf16[16,9216]{1,0:T(8,128)(2,1)} %collective-permute-done.4.refs_3_), channel_id=1, source_target_pairs={{0,7},{1,0},{2,1},{3,2},{4,3},{5,4},{6,5},{7,6},{8,15},{9,8},{10,9... | collective-permute-start | bytes 884744 | tf_op jit(solution)/shard_map/ppermute | solution.py:25
  57.4 8.2 %copy-start = (bf16[256,512]{1,0:T(8,128)(2,1)S(1)}, bf16[256,512]{1,0:T(8,128)(2,1)}, u32[]{:S(2)}) copy-start(bf16[256,512]{1,0:T(8,128)(2,1)} %o_ref.1) | copy-start | bytes 786436
  59.7 1.0 copy-start.4
  60.6 0.9 copy-start.7
  61.6 0.9 copy-start.9
  62.5 10.0 %slice-start = ((s8[8388608]{0:T(1024)(128)(4,1)}), s8[4194304]{0:T(1024)(128)(4,1)S(1)}, s32[]{:S(2)}) async-start(s8[8388608]{0:T(1024)(128)(4,1)} %bitcast.10), calls=%async_computation.2 | async-start | bytes 8388608
  65.6 6.9 %copy-start.1 = (bf16[512,64]{0,1:T(8,128)(2,1)S(1)}, bf16[512,64]{0,1:T(8,128)(2,1)}, u32[]{:S(2)}) copy-start(bf16[512,64]{0,1:T(8,128)(2,1)} %param.16) | copy-start | bytes 196612
  65.6 6.9 %slice-start.1 = ((s8[8388608]{0:T(1024)(128)(4,1)}), s8[4194304]{0:T(1024)(128)(4,1)S(1)}, s32[]{:S(2)}) async-start(s8[8388608]{0:T(1024)(128)(4,1)} %bitcast.10), calls=%async_computation.3 | async-start | bytes 8388608
  69.4 1.5 %collective-permute-start.16 = (bf16[64,1280]{1,0:T(8,128)(2,1)S(1)}, bf16[64,1280]{1,0:T(8,128)(2,1)S(1)}, u32[]{:S(2)}, u32[]{:S(2)}) collective-permute-start(bf16[64,1280]{1,0:T(8,128)(2,1)S(1)} %get-tuple-element.65), channel_id=1, source_target_pairs={{0,16},{16,0},{1,17},{17,1},{2,18},{18,2},{3,19},{19,3},{4,20},{20... | collective-permute-start | bytes 491528 | tf_op jit(solution)/shard_map/ppermute | solution.py:25
  69.5 13.4 %collective-permute-start.19 = (bf16[8,256,256]{2,1,0:T(8,128)(2,1)S(1)}, bf16[8,256,256]{2,1,0:T(8,128)(2,1)S(1)}, u32[]{:S(2)}, u32[]{:S(2)}) collective-permute-start(bf16[8,256,256]{2,1,0:T(8,128)(2,1)S(1)} %all-to-all-done.kv_ref), channel_id=1, source_target_pairs={{0,16},{16,0},{1,17},{17,1},{2,18},{18,2},{3,19},{19,3},{4,20},{20... | collective-permute-start | bytes 3145736 | tf_op jit(solution)/shard_map/ppermute | solution.py:25
  70.9 6.3 %collective-permute-start.17 = (bf16[64,1280]{1,0:T(8,128)(2,1)S(1)}, bf16[64,1280]{1,0:T(8,128)(2,1)S(1)}, u32[]{:S(2)}, u32[]{:S(2)}) collective-permute-start(bf16[64,1280]{1,0:T(8,128)(2,1)S(1)} %add_convert_fusion.4), channel_id=1, source_target_pairs={{0,128},{128,0},{1,129},{129,1},{2,130},{130,2},{3,131},{131,3},{4... | collective-permute-start | bytes 491528 | tf_op jit(solution)/shard_map/ppermute | solution.py:25
  72.5 10.4 %copy-start.5 = (bf16[256,512]{1,0:T(8,128)(2,1)S(1)}, bf16[256,512]{1,0:T(8,128)(2,1)}, u32[]{:S(2)}) copy-start(bf16[256,512]{1,0:T(8,128)(2,1)} %q_ref.1) | copy-start | bytes 786436
  72.5 10.4 %copy-start.10 = (f32[4,256]{1,0:T(4,128)S(1)}, f32[4,256]{1,0:T(4,128)}, u32[]{:S(2)}) copy-start(f32[4,256]{1,0:T(4,128)} %norm_ref.1) | copy-start | bytes 12292
  77.3 5.5 %collective-permute-start.18 = (bf16[64,1280]{1,0:T(8,128)(2,1)S(1)}, bf16[64,1280]{1,0:T(8,128)(2,1)S(1)}, u32[]{:S(2)}, u32[]{:S(2)}) collective-permute-start(bf16[64,1280]{1,0:T(8,128)(2,1)S(1)} %add_convert_fusion.3), channel_id=1, source_target_pairs={{0,32},{32,0},{64,96},{96,64},{1,33},{33,1},{65,97},{97,65},{2,34}... | collective-permute-start | bytes 491528 | tf_op jit(solution)/shard_map/ppermute | solution.py:415
  86.2 8.4 %collective-permute-start.20 = (bf16[64,1280]{1,0:T(8,128)(2,1)S(1)}, bf16[64,1280]{1,0:T(8,128)(2,1)S(1)}, u32[]{:S(2)}, u32[]{:S(2)}) collective-permute-start(bf16[64,1280]{1,0:T(8,128)(2,1)S(1)} %add_convert_fusion.2), channel_id=1, source_target_pairs={{0,96},{32,64},{64,32},{96,0},{1,97},{33,65},{65,33},{97,1},{2,98}... | collective-permute-start | bytes 491528 | tf_op jit(solution)/shard_map/ppermute | solution.py:418
  94.6 2.7 %collective-permute-start.22 = (bf16[8,256,256]{2,1,0:T(8,128)(2,1)S(1)}, bf16[8,256,256]{2,1,0:T(8,128)(2,1)S(1)}, u32[]{:S(2)}, u32[]{:S(2)}) collective-permute-start(bf16[8,256,256]{2,1,0:T(8,128)(2,1)S(1)} %get-tuple-element.92), channel_id=1, source_target_pairs={{0,16},{16,0},{1,17},{17,1},{2,18},{18,2},{3,19},{19,3},{4,20},{20... | collective-permute-start | bytes 3145736 | tf_op jit(solution)/shard_map/ppermute | solution.py:25
  94.7 3.9 %collective-permute-start.21 = (bf16[64,1280]{1,0:T(8,128)(2,1)S(1)}, bf16[64,1280]{1,0:T(8,128)(2,1)S(1)}, u32[]{:S(2)}, u32[]{:S(2)}) collective-permute-start(bf16[64,1280]{1,0:T(8,128)(2,1)S(1)} %add_convert_fusion.1), channel_id=1, source_target_pairs={{0,16},{16,0},{1,17},{17,1},{2,18},{18,2},{3,19},{19,3},{4,20},{20... | collective-permute-start | bytes 491528 | tf_op jit(solution)/shard_map/ppermute | solution.py:25
  98.6 20.4 %all-to-all-start.1 = ((bf16[8,256,256]{2,1,0:T(8,128)(2,1)}), bf16[8,256,256]{2,1,0:T(8,128)(2,1)S(1)}, u32[]{:S(2)}, u32[]{:S(2)}) async-start(bf16[8,256,256]{2,1,0:T(8,128)(2,1)} %add_convert_fusion), calls=%async_computation.1 | async-start | bytes 2097152 | tf_op jit(solution)/shard_map/all_to_all | solution.py:423
  103.9 9.4 %collective-permute-start.25 = (bf16[64,2048]{1,0:T(8,128)(2,1)S(1)}, bf16[64,2048]{1,0:T(8,128)(2,1)S(1)}, u32[]{:S(2)}, u32[]{:S(2)}) collective-permute-start(bf16[64,2048]{1,0:T(8,128)(2,1)S(1)} %pad_maximum_fusion.1.refs_0_), channel_id=1, source_target_pairs={{0,1},{1,2},{2,3},{3,4},{4,5},{5,6},{6,7},{7,0},{8,9},{9,10},{10,1... | collective-permute-start | bytes 786440 | tf_op jit(solution)/shard_map/ppermute | solution.py:25
  104.0 9.4 %collective-permute-start.24 = (bf16[64,2048]{1,0:T(8,128)(2,1)S(1)}, bf16[64,2048]{1,0:T(8,128)(2,1)S(1)}, u32[]{:S(2)}, u32[]{:S(2)}) collective-permute-start(bf16[64,2048]{1,0:T(8,128)(2,1)S(1)} %pad_maximum_fusion.1.refs_0_), channel_id=1, source_target_pairs={{0,7},{1,0},{2,1},{3,2},{4,3},{5,4},{6,5},{7,6},{8,15},{9,8},{10,9... | collective-permute-start | bytes 786440 | tf_op jit(solution)/shard_map/ppermute | solution.py:25
  113.3 6.6 %collective-permute-start.26 = (bf16[64,1024]{1,0:T(8,128)(2,1)S(1)}, bf16[64,1024]{1,0:T(8,128)(2,1)S(1)}, u32[]{:S(2)}, u32[]{:S(2)}) collective-permute-start(bf16[64,1024]{1,0:T(8,128)(2,1)S(1)} %slice.58), channel_id=1, source_target_pairs={{0,1},{1,2},{2,3},{3,4},{4,5},{5,6},{6,7},{7,0},{8,9},{9,10},{10,1... | collective-permute-start | bytes 393224 | tf_op jit(solution)/shard_map/ppermute | solution.py:25
  113.4 6.5 %collective-permute-start.27 = (bf16[64,1024]{1,0:T(8,128)(2,1)S(1)}, bf16[64,1024]{1,0:T(8,128)(2,1)S(1)}, u32[]{:S(2)}, u32[]{:S(2)}) collective-permute-start(bf16[64,1024]{1,0:T(8,128)(2,1)S(1)} %slice.59), channel_id=1, source_target_pairs={{0,7},{1,0},{2,1},{3,2},{4,3},{5,4},{6,5},{7,6},{8,15},{9,8},{10,9... | collective-permute-start | bytes 393224 | tf_op jit(solution)/shard_map/ppermute | solution.py:25
  119.1 5.1 %collective-permute-start.23 = (bf16[256,256]{1,0:T(8,128)(2,1)S(1)}, bf16[256,256]{1,0:T(8,128)(2,1)S(1)}, u32[]{:S(2)}, u32[]{:S(2)}) collective-permute-start(bf16[256,256]{1,0:T(8,128)(2,1)S(1)} %get-tuple-element.95), channel_id=1, source_target_pairs={{0,1},{1,0},{2,3},{3,2},{4,5},{5,4},{6,7},{7,6},{8,9},{9,8},{10,11... | collective-permute-start | bytes 393224 | tf_op jit(solution)/shard_map/ppermute | solution.py:432

commit v2 on v1

--- a/solution.py
+++ b/solution.py
@@ -409,14 +409,18 @@
     low = (mine + turned(yours, "core", 1).astype(F32)).astype(BF16)
     cots, low = together((cots, low))
     g = gradient_call(where, own_rows, peer_rows, w, cots, down.T)
-    total = low.astype(F32) + turned(low, "ylo", 1).astype(F32)
-    low, g = together((total.astype(BF16), g))
+    other, g = together((turned(low, "ylo", 1), g))
+    low = (low.astype(F32) + other.astype(F32)).astype(BF16)
+    low, g = together((low, g))
     kept = late_call(q, o, g, log_norm, kv, other_kv)
-    total = low.astype(F32) + lax.ppermute(low, "x", [(i, i ^ 1) for i in range(4)]).astype(F32)
-    low, kept = together((total.astype(BF16), kept))
+    other = lax.ppermute(low, "x", [(i, i ^ 1) for i in range(4)])
+    other, kept = together((other, kept))
+    low = (low.astype(F32) + other.astype(F32)).astype(BF16)
+    low, kept = together((low, kept))
     dq, mine, yours = rest_call(where, kept, kv, other_kv)
-    total = low.astype(F32) + lax.ppermute(low, "x", [(i, 3 - i) for i in range(4)]).astype(F32)
-    low, mine, yours = together((total.astype(BF16), mine, yours))
+    other = lax.ppermute(low, "x", [(i, 3 - i) for i in range(4)])
+    other, mine, yours = together((other, mine, yours))
+    low = (low.astype(F32) + other.astype(F32)).astype(BF16)
     other = turned(low, "core", 1)
     mine = (mine.astype(F32) + turned(yours, "core", 1).astype(F32)).astype(BF16)
     other, mine = together((other, mine))

time: 126 us -> 122 us (0.968)
  waiting for transfers between devices: 44.5 us -> 40.2 us
    ppermute x2, waiting for transfers between devices: 5.14 us -> 1.83 us  [the longest x1 1.83 us: local(): other = lax.ppermute(low, 'x', [(i, i ^ 1) for i in range(4)])]
  transfers between devices with their start and end apart: 30 -> 30, of which waited for: 15 -> 15; matrix products, arithmetic and copies ran while one was open for 4% -> 5% of each run, Pallas kernels for 11% -> 14%
where the time goes in v2:
time: 122 us; the launch traced here: 121 us
  starting transfers between devices  47.7 us (39%)
  waiting for transfers between devices  40.2 us (33%)
  Pallas kernels  21.4 us (18%)
  local copies, waits for them, and re-layouts  6.04 us (5%)
  other arithmetic  4.05 us (3%)
    ppermute x25, starting transfers between devices, turned(): return lax.ppermute(x, axis, [(i, (i + by) % size) for i in range(size)])  34.4 us
    ppermute x25, waiting for transfers between devices, turned(): return lax.ppermute(x, axis, [(i, (i + by) % size) for i in range(size)])  33.4 us
    pallas_call x1, Pallas kernels, rest_call(): pl.pallas_call(rest_kernel, out_shape=(jax.ShapeDtypeStruct((2 * HALF, si...  6.58 us
    all_to_all x1, starting transfers between devices, local(): lax.all_to_all(jnp.broadcast_to(kv[None], (8,) + kv.shape), CTX[:2], 0, 0)  5.84 us
    all_to_all x1, starting transfers between devices, local(): pieces = lax.all_to_all(mine, CTX[:2], 0, 0)  5.24 us
    unnamed x26, local copies, waits for them, and re-layouts  4.29 us
    pallas_call x1, Pallas kernels, adapter_call(): pl.pallas_call(adapter_kernel, out_shape=(jax.ShapeDtypeStruct((128, widt...  3.8 us
    pallas_call x1, Pallas kernels, late_call(): pl.pallas_call(late_kernel, out_shape=(stacked, stacked, line, line, jax....  3.29 us
  transfers between devices with their start and end apart: 30, of which 15 were waited for; matrix products, arithmetic and copies ran while one was open for 5% of the time, Pallas kernels for 14%

profile of v2, /device:TPU:2, one launch (start us, length us, event | category | flops | bytes accessed | tf_op | source)
XLA Modules:
  0.0 121.4 jit_solution(15375753009526629193)
XLA Ops:
  0.6 3.3 %collective-permute-start = (bf16[16,8192]{1,0:T(8,128)(2,1)}, bf16[16,8192]{1,0:T(8,128)(2,1)S(1)}, u32[]{:S(2)}, u32[]{:S(2)}) collective-permute-start(bf16[16,8192]{1,0:T(8,128)(2,1)} %refs_0_), channel_id=1, source_target_pairs={{0,8},{8,0},{1,9},{9,1},{2,10},{10,2},{3,11},{11,3},{4,12},{12,4},... | collective-permute-start | bytes 786440 | tf_op jit(solution)/shard_map/ppermute | solution.py:25
  3.9 1.9 %collective-permute-start.12 = (bf16[16,8192]{1,0:T(8,128)(2,1)}, bf16[16,8192]{1,0:T(8,128)(2,1)}, u32[]{:S(2)}, u32[]{:S(2)}) collective-permute-start(bf16[16,8192]{1,0:T(8,128)(2,1)} %refs_0_), channel_id=1, source_target_pairs={{0,1},{1,2},{2,3},{3,4},{4,5},{5,6},{6,7},{7,0},{8,9},{9,10},{10,1... | collective-permute-start | bytes 786440 | tf_op jit(solution)/shard_map/ppermute | solution.py:25
  5.8 1.2 fusion.3
  7.1 0.4 collective-permute-start.1
  7.5 0.9 pad_maximum_fusion.2
  8.4 4.2 %collective-permute-done.1 = bf16[16,1024]{1,0:T(8,128)(2,1)S(1)} collective-permute-done((bf16[16,1024]{1,0:T(8,128)(2,1)S(1)}, bf16[16,1024]{1,0:T(8,128)(2,1)S(1)}, u32[]{:S(2)}, u32[]{:S(2)}) %collective-permute-start.1) | collective-permute-done | bytes 32800 | tf_op jit(solution)/shard_map/ppermute | solution.py:25
  12.6 4.5 %collective-permute-start.2 = (bf16[16,9216]{1,0:T(8,128)(2,1)S(1)}, bf16[16,9216]{1,0:T(8,128)(2,1)S(1)}, u32[]{:S(2)}, u32[]{:S(2)}) collective-permute-start(bf16[16,9216]{1,0:T(8,128)(2,1)S(1)} %pad_maximum_fusion.refs_0_), channel_id=1, source_target_pairs={{0,7},{1,0},{2,1},{3,2},{4,3},{5,4},{6,5},{7,6},{8,15},{9,8},{10,9... | collective-permute-start | bytes 884744 | tf_op jit(solution)/shard_map/ppermute | solution.py:25
  17.2 1.0 broadcast_in_dim.2
  18.2 5.8 %all-to-all-start = ((bf16[8,256,256]{2,1,0:T(8,128)(2,1)}), bf16[8,256,256]{2,1,0:T(8,128)(2,1)S(1)}, u32[]{:S(2)}, u32[]{:S(2)}) async-start(bf16[8,256,256]{2,1,0:T(8,128)(2,1)} %broadcast_in_dim.2), calls=%async_computation | async-start | bytes 2097152 | tf_op jit(solution)/shard_map/all_to_all | solution.py:403
  24.0 1.0 collective-permute-start.9
  25.1 1.0 collective-permute-start.13
  26.1 0.0 collective-permute-start.6
  26.1 3.2 %collective-permute-start.3 = (bf16[16,9216]{1,0:T(8,128)(2,1)S(1)}, bf16[16,9216]{1,0:T(8,128)(2,1)}, u32[]{:S(2)}, u32[]{:S(2)}) collective-permute-start(bf16[16,9216]{1,0:T(8,128)(2,1)S(1)} %collective-permute-done.2.refs_1_), channel_id=1, source_target_pairs={{0,7},{1,0},{2,1},{3,2},{4,3},{5,4},{6,5},{7,6},{8,15},{9,8},{10,9... | collective-permute-start | bytes 884744 | tf_op jit(solution)/shard_map/ppermute | solution.py:25
  29.3 4.0 %collective-permute-done.9.refs_1_ = bf16[16,8192]{1,0:T(8,128)(2,1)S(1)} collective-permute-done((bf16[16,8192]{1,0:T(8,128)(2,1)S(1)}, bf16[16,8192]{1,0:T(8,128)(2,1)S(1)}, u32[]{:S(2)}, u32[]{:S(2)}) %collective-permute-start.9) | collective-permute-done | bytes 262176 | tf_op jit(solution)/shard_map/ppermute | solution.py:25
  33.3 1.6 %collective-permute-start.10 = (bf16[16,8192]{1,0:T(8,128)(2,1)S(1)}, bf16[16,8192]{1,0:T(8,128)(2,1)}, u32[]{:S(2)}, u32[]{:S(2)}) collective-permute-start(bf16[16,8192]{1,0:T(8,128)(2,1)S(1)} %collective-permute-done.9.refs_1_), channel_id=1, source_target_pairs={{0,7},{1,0},{2,1},{3,2},{4,3},{5,4},{6,5},{7,6},{8,15},{9,8},{10,9... | collective-permute-start | bytes 786440 | tf_op jit(solution)/shard_map/ppermute | solution.py:25
  34.9 0.7 copy-done.6
  35.6 0.1 collective-permute-done.13.refs_6_
  35.7 0.3 collective-permute-start.14
  36.0 0.7 copy-done.8
  36.7 5.3 %collective-permute-done.6.refs_7_ = bf16[16,9216]{1,0:T(8,128)(2,1)S(1)} collective-permute-done((bf16[16,9216]{1,0:T(8,128)(2,1)S(1)}, bf16[16,9216]{1,0:T(8,128)(2,1)S(1)}, u32[]{:S(2)}, u32[]{:S(2)}) %collective-permute-start.6) | collective-permute-done | bytes 294944 | tf_op jit(solution)/shard_map/ppermute | solution.py:25
  42.1 3.2 %collective-permute-start.4 = (bf16[16,9216]{1,0:T(8,128)(2,1)}, bf16[16,9216]{1,0:T(8,128)(2,1)}, u32[]{:S(2)}, u32[]{:S(2)}) collective-permute-start(bf16[16,9216]{1,0:T(8,128)(2,1)} %collective-permute-done.3.refs_2_), channel_id=1, source_target_pairs={{0,7},{1,0},{2,1},{3,2},{4,3},{5,4},{6,5},{7,6},{8,15},{9,8},{10,9... | collective-permute-start | bytes 884744 | tf_op jit(solution)/shard_map/ppermute | solution.py:25
  45.3 0.0 collective-permute-done.10.refs_2_
  45.3 1.1 collective-permute-start.11
  46.4 1.3 %collective-permute-done.14.refs_5_ = bf16[16,8192]{1,0:T(8,128)(2,1)} collective-permute-done((bf16[16,8192]{1,0:T(8,128)(2,1)S(1)}, bf16[16,8192]{1,0:T(8,128)(2,1)}, u32[]{:S(2)}, u32[]{:S(2)}) %collective-permute-start.14) | collective-permute-done | bytes 262176 | tf_op jit(solution)/shard_map/ppermute | solution.py:25
  47.8 6.3 %collective-permute-done.7.refs_6_ = bf16[16,9216]{1,0:T(8,128)(2,1)} collective-permute-done((bf16[16,9216]{1,0:T(8,128)(2,1)S(1)}, bf16[16,9216]{1,0:T(8,128)(2,1)}, u32[]{:S(2)}, u32[]{:S(2)}) %collective-permute-start.7) | collective-permute-done | bytes 294944 | tf_op jit(solution)/shard_map/ppermute | solution.py:25
  54.1 3.2 %collective-permute-start.5 = (bf16[16,9216]{1,0:T(8,128)(2,1)}, bf16[16,9216]{1,0:T(8,128)(2,1)}, u32[]{:S(2)}, u32[]{:S(2)}) collective-permute-start(bf16[16,9216]{1,0:T(8,128)(2,1)} %collective-permute-done.4.refs_3_), channel_id=1, source_target_pairs={{0,7},{1,0},{2,1},{3,2},{4,3},{5,4},{6,5},{7,6},{8,15},{9,8},{10,9... | collective-permute-start | bytes 884744 | tf_op jit(solution)/shard_map/ppermute | solution.py:25
  57.3 0.1 pad_add_fusion.where_ref
  57.4 0.1 collective-permute-done.11.refs_3_
  57.5 2.2 %collective-permute-done.15.refs_4_ = bf16[16,8192]{1,0:T(8,128)(2,1)} collective-permute-done((bf16[16,8192]{1,0:T(8,128)(2,1)}, bf16[16,8192]{1,0:T(8,128)(2,1)}, u32[]{:S(2)}, u32[]{:S(2)}) %collective-permute-start.15) | collective-permute-done | bytes 262176 | tf_op jit(solution)/shard_map/ppermute | solution.py:25
  59.7 0.9 copy-done.4
  60.6 0.9 copy-done.7
  61.6 0.9 copy-done.9
  62.5 3.0 %shard_map.128 = (bf16[128,8192]{1,0:T(8,128)(2,1)S(1)}, bf16[128,64]{1,0:T(8,128)(2,1)S(1)}) custom-call(s32[4]{0:T(128)S(1)} %pad_add_fusion.where_ref, bf16[16,8192]{1,0:T(8,128)(2,1)S(1)} %copy-done.4, bf16[16,8192]{1,0:T(8,128)(2,1)S(1)} %copy-done.7, bf16[16,8192]{1,0:T(8,128)(2,1)} %collective-permute-done.10.refs_2_, ...), custom_call_target="tpu_custom_call" | custom-call | flops 2000000000 | bytes 4194304 | tf_op jit(solution)/shard_map/pallas_call | solution.py:139
  65.6 0.0 copy-start.1
  65.6 0.0 slice-start.1
  65.6 3.8 %shard_map.129 = (bf16[128,8192]{1,0:T(8,128)(2,1)S(1)}, bf16[256,64]{1,0:T(8,128)(2,1)S(1)}, f32[64,1280]{1,0:T(8,128)S(1)}, bf16[64,1280]{1,0:T(8,128)(2,1)S(1)}) custom-call(s32[4]{0:T(128)S(1)} %pad_add_fusion.where_ref, bf16[16,9216]{1,0:T(8,128)(2,1)S(1)} %pad_maximum_fusion.refs_0_, bf16[16,9216]{1,0:T(8,128)(2,1)S(1)} %collective-permute-done.2.refs_1_, ...), custom_call_target="tpu_custom_call" | custom-call | flops 2000000000 | bytes 4194304 | tf_op jit(solution)/shard_map/pallas_call | solution.py:200
  69.4 0.1 collective-permute-start.16
  69.5 0.5 collective-permute-start.19
  70.0 0.9 collective-permute-done.16
  70.9 1.5 %collective-permute-start.17 = (bf16[64,1280]{1,0:T(8,128)(2,1)S(1)}, bf16[64,1280]{1,0:T(8,128)(2,1)S(1)}, u32[]{:S(2)}, u32[]{:S(2)}) collective-permute-start(bf16[64,1280]{1,0:T(8,128)(2,1)S(1)} %add_convert_fusion.4), channel_id=1, source_target_pairs={{0,128},{128,0},{1,129},{129,1},{2,130},{130,2},{3,131},{131,3},{4... | collective-permute-start | bytes 491528 | tf_op jit(solution)/shard_map/ppermute | solution.py:25
  72.5 3.0 %shard_map.130.g_ref = bf16[2,128,512]{2,1,0:T(8,128)(2,1)S(1)} custom-call(s32[4]{0:T(128)S(1)} %pad_add_fusion.where_ref, bf16[128,8192]{1,0:T(8,128)(2,1)S(1)} %get-tuple-element.71.refs_9_.own_ref, bf16[128,8192]{1,0:T(8,128)(2,1)S(1)} %get-tuple-element.77.peer_ref, bf16[512,8192]{1,0:T(8,128)(2,1)S(1)} %bitcast.11, ...), custom_call_target="tpu_custom_call" | custom-call | flops 10000000000 | bytes 8388608 | tf_op jit(solution)/shard_map/pallas_call | solution.py:240
  75.5 1.8 %collective-permute-done.17 = bf16[64,1280]{1,0:T(8,128)(2,1)S(1)} collective-permute-done((bf16[64,1280]{1,0:T(8,128)(2,1)S(1)}, bf16[64,1280]{1,0:T(8,128)(2,1)S(1)}, u32[]{:S(2)}, u32[]{:S(2)}) %collective-permute-start.17) | collective-permute-done | bytes 163872 | tf_op jit(solution)/shard_map/ppermute | solution.py:25
  77.3 0.4 collective-permute-start.18
  77.7 3.3 %shard_map.131 = (bf16[2,512,128]{2,1,0:T(8,128)(2,1)S(1)}, bf16[2,512,128]{2,1,0:T(8,128)(2,1)S(1)}, f32[2,1,512]{2,1,0:T(1,128)S(1)}, f32[2,1,512]{2,1,0:T(1,1...) custom-call(bf16[256,512]{1,0:T(8,128)(2,1)S(1)} %copy-done.5, ...), custom_call_target="tpu_custom_call" | custom-call | flops 10000000000 | bytes 4194304 | tf_op jit(solution)/shard_map/pallas_call | solution.py:350
  81.0 1.8 %collective-permute-done.18 = bf16[64,1280]{1,0:T(8,128)(2,1)S(1)} collective-permute-done((bf16[64,1280]{1,0:T(8,128)(2,1)S(1)}, bf16[64,1280]{1,0:T(8,128)(2,1)S(1)}, u32[]{:S(2)}, u32[]{:S(2)}) %collective-permute-start.18) | collective-permute-done | bytes 163872 | tf_op jit(solution)/shard_map/ppermute | solution.py:416
  82.9 1.8 %collective-permute-start.20 = (bf16[64,1280]{1,0:T(8,128)(2,1)S(1)}, bf16[64,1280]{1,0:T(8,128)(2,1)}, u32[]{:S(2)}, u32[]{:S(2)}) collective-permute-start(bf16[64,1280]{1,0:T(8,128)(2,1)S(1)} %add_convert_fusion.2), channel_id=1, source_target_pairs={{0,96},{32,64},{64,32},{96,0},{1,97},{33,65},{65,33},{97,1},{2,98}... | collective-permute-start | bytes 491528 | tf_op jit(solution)/shard_map/ppermute | solution.py:421
  84.6 6.6 %shard_map.132 = (bf16[256,512]{1,0:T(8,128)(2,1)}, bf16[8,256,256]{2,1,0:T(8,128)(2,1)S(1)}, bf16[8,256,256]{2,1,0:T(8,128)(2,1)S(1)}) custom-call(s32[4]{0:T(128)S(1)} %pad_add_fusion.where_ref, bf16[2,512,128]{2,1,0:T(8,128)(2,1)S(1)} %get-tuple-element.99.qs, bf16[2,512,128]{2,1,0:T(8,128)(2,1)S(1)} %get-tuple-element.100.gs, ...), custom_call_target="tpu_custom_call" | custom-call | flops 10000000000 | bytes 4194304 | tf_op jit(solution)/shard_map/pallas_call | solution.py:375
  91.2 1.0 add_convert_fusion.1
  92.2 0.6 collective-permute-start.21
  92.8 1.1 collective-permute-done.22
  93.9 1.2 %add_convert_fusion = bf16[8,256,256]{2,1,0:T(8,128)(2,1)} fusion(bf16[8,256,256]{2,1,0:T(8,128)(2,1)S(1)} %collective-permute-done.22, bf16[8,256,256]{2,1,0:T(8,128)(2,1)S(1)} %get-tuple-element.111), kind=kLoop, calls=%fused_computation | loop fusion | flops 2097152 | bytes 3145728 | tf_op jit(solution)/shard_map/convert_element_type | solution.py:425
  95.1 5.2 %all-to-all-start.1 = ((bf16[8,256,256]{2,1,0:T(8,128)(2,1)}), bf16[8,256,256]{2,1,0:T(8,128)(2,1)S(1)}, u32[]{:S(2)}, u32[]{:S(2)}) async-start(bf16[8,256,256]{2,1,0:T(8,128)(2,1)} %add_convert_fusion), calls=%async_computation.1 | async-start | bytes 2097152 | tf_op jit(solution)/shard_map/all_to_all | solution.py:427
  100.5 0.1 collective-permute-start.25
  100.5 3.2 %collective-permute-start.24 = (bf16[64,2048]{1,0:T(8,128)(2,1)S(1)}, bf16[64,2048]{1,0:T(8,128)(2,1)S(1)}, u32[]{:S(2)}, u32[]{:S(2)}) collective-permute-start(bf16[64,2048]{1,0:T(8,128)(2,1)S(1)} %pad_maximum_fusion.1.refs_0_), channel_id=1, source_target_pairs={{0,7},{1,0},{2,1},{3,2},{4,3},{5,4},{6,5},{7,6},{8,15},{9,8},{10,9... | collective-permute-start | bytes 786440 | tf_op jit(solution)/shard_map/ppermute | solution.py:25
  103.8 6.0 %collective-permute-done.25.refs_4_ = bf16[64,2048]{1,0:T(8,128)(2,1)S(1)} collective-permute-done((bf16[64,2048]{1,0:T(8,128)(2,1)S(1)}, bf16[64,2048]{1,0:T(8,128)(2,1)S(1)}, u32[]{:S(2)}, u32[]{:S(2)}) %collective-permute-start.25) | collective-permute-done | bytes 262176 | tf_op jit(solution)/shard_map/ppermute | solution.py:25
  109.8 0.1 collective-permute-start.26
  109.9 3.3 %collective-permute-start.27 = (bf16[64,1024]{1,0:T(8,128)(2,1)S(1)}, bf16[64,1024]{1,0:T(8,128)(2,1)S(1)}, u32[]{:S(2)}, u32[]{:S(2)}) collective-permute-start(bf16[64,1024]{1,0:T(8,128)(2,1)S(1)} %slice.59), channel_id=1, source_target_pairs={{0,7},{1,0},{2,1},{3,2},{4,3},{5,4},{6,5},{7,6},{8,15},{9,8},{10,9... | collective-permute-start | bytes 393224 | tf_op jit(solution)/shard_map/ppermute | solution.py:25
  113.2 2.3 %all-to-all-done.1.pieces_ref = bf16[8,256,256]{2,1,0:T(8,128)(2,1)S(1)} async-done(((bf16[8,256,256]{2,1,0:T(8,128)(2,1)}), bf16[8,256,256]{2,1,0:T(8,128)(2,1)S(1)}, u32[]{:S(2)}, u32[]{:S(2)}) %all-to-all-start.1) | async-done | bytes 1048608 | tf_op jit(solution)/shard_map/all_to_all | solution.py:427
  115.5 0.1 shard_map.133
  115.7 0.1 collective-permute-start.23
  115.8 0.7 convert_bitcast_fusion
  116.5 1.6 %shard_map.134 = bf16[64,8192]{1,0:T(8,128)(2,1)} custom-call(s32[4]{0:T(128)S(1)} %pad_add_fusion.where_ref, bf16[64,2048]{1,0:T(8,128)(2,1)S(1)} %pad_maximum_fusion.1.refs_0_, bf16[64,2048]{1,0:T(8,128)(2,1)S(1)} %collective-permute-done.24.refs_1_, bf16[64,1024]{1,0:T(8,128)(2,1)S(1)} %collective-permute-done.26.refs_2_, ...), custom_call_target="tpu_custom_call" | custom-call | bytes 1048576 | tf_op jit(solution)/shard_map/pallas_call | solution.py:58
  118.0 2.7 %collective-permute-done.23 = bf16[256,256]{1,0:T(8,128)(2,1)S(1)} collective-permute-done((bf16[256,256]{1,0:T(8,128)(2,1)S(1)}, bf16[256,256]{1,0:T(8,128)(2,1)S(1)}, u32[]{:S(2)}, u32[]{:S(2)}) %collective-permute-start.23) | collective-permute-done | bytes 131104 | tf_op jit(solution)/shard_map/ppermute | solution.py:436
  120.7 0.7 fusion.1
  (54 shorter events, 0.4 us)
Async XLA Ops:
  0.6 12.0 %collective-permute-start = (bf16[16,8192]{1,0:T(8,128)(2,1)}, bf16[16,8192]{1,0:T(8,128)(2,1)S(1)}, u32[]{:S(2)}, u32[]{:S(2)}) collective-permute-start(bf16[16,8192]{1,0:T(8,128)(2,1)} %refs_0_), channel_id=1, source_target_pairs={{0,8},{8,0},{1,9},{9,1},{2,10},{10,2},{3,11},{11,3},{4,12},{12,4},... | collective-permute-start | bytes 786440 | tf_op jit(solution)/shard_map/ppermute | solution.py:25
  3.9 21.1 %collective-permute-start.12 = (bf16[16,8192]{1,0:T(8,128)(2,1)}, bf16[16,8192]{1,0:T(8,128)(2,1)}, u32[]{:S(2)}, u32[]{:S(2)}) collective-permute-start(bf16[16,8192]{1,0:T(8,128)(2,1)} %refs_0_), channel_id=1, source_target_pairs={{0,1},{1,2},{2,3},{3,4},{4,5},{5,6},{6,7},{7,0},{8,9},{9,10},{10,1... | collective-permute-start | bytes 786440 | tf_op jit(solution)/shard_map/ppermute | solution.py:25
  7.0 17.0 %copy-start.3 = (bf16[16,8192]{1,0:T(8,128)(2,1)S(1)}, bf16[16,8192]{1,0:T(8,128)(2,1)}, u32[]{:S(2)}) copy-start(bf16[16,8192]{1,0:T(8,128)(2,1)} %refs_0_) | copy-start | bytes 786436
  7.1 52.6 %copy-start.2 = (bf16[64,8192]{1,0:T(8,128)(2,1)S(1)}, bf16[64,8192]{1,0:T(8,128)(2,1)}, u32[]{:S(2)}) copy-start(bf16[64,8192]{1,0:T(8,128)(2,1)} %refs_8_.3) | copy-start | bytes 3145732
  7.1 5.5 %collective-permute-start.1 = (bf16[16,1024]{1,0:T(8,128)(2,1)S(1)}, bf16[16,1024]{1,0:T(8,128)(2,1)S(1)}, u32[]{:S(2)}, u32[]{:S(2)}) collective-permute-start(bf16[16,1024]{1,0:T(8,128)(2,1)S(1)} %fusion), channel_id=1, source_target_pairs={{0,8},{8,0},{1,9},{9,1},{2,10},{10,2},{3,11},{11,3},{4,12},{12,4},... | collective-permute-start | bytes 98312 | tf_op jit(solution)/shard_map/ppermute | solution.py:25
  12.6 13.5 %collective-permute-start.2 = (bf16[16,9216]{1,0:T(8,128)(2,1)S(1)}, bf16[16,9216]{1,0:T(8,128)(2,1)S(1)}, u32[]{:S(2)}, u32[]{:S(2)}) collective-permute-start(bf16[16,9216]{1,0:T(8,128)(2,1)S(1)} %pad_maximum_fusion.refs_0_), channel_id=1, source_target_pairs={{0,7},{1,0},{2,1},{3,2},{4,3},{5,4},{6,5},{7,6},{8,15},{9,8},{10,9... | collective-permute-start | bytes 884744 | tf_op jit(solution)/shard_map/ppermute | solution.py:25
  18.2 41.5 %all-to-all-start = ((bf16[8,256,256]{2,1,0:T(8,128)(2,1)}), bf16[8,256,256]{2,1,0:T(8,128)(2,1)S(1)}, u32[]{:S(2)}, u32[]{:S(2)}) async-start(bf16[8,256,256]{2,1,0:T(8,128)(2,1)} %broadcast_in_dim.2), calls=%async_computation | async-start | bytes 2097152 | tf_op jit(solution)/shard_map/all_to_all | solution.py:403
  24.0 9.2 %collective-permute-start.9 = (bf16[16,8192]{1,0:T(8,128)(2,1)S(1)}, bf16[16,8192]{1,0:T(8,128)(2,1)S(1)}, u32[]{:S(2)}, u32[]{:S(2)}) collective-permute-start(bf16[16,8192]{1,0:T(8,128)(2,1)S(1)} %copy-done.3), channel_id=1, source_target_pairs={{0,7},{1,0},{2,1},{3,2},{4,3},{5,4},{6,5},{7,6},{8,15},{9,8},{10,9... | collective-permute-start | bytes 786440 | tf_op jit(solution)/shard_map/ppermute | solution.py:25
  25.1 10.7 %collective-permute-start.13 = (bf16[16,8192]{1,0:T(8,128)(2,1)}, bf16[16,8192]{1,0:T(8,128)(2,1)S(1)}, u32[]{:S(2)}, u32[]{:S(2)}) collective-permute-start(bf16[16,8192]{1,0:T(8,128)(2,1)} %collective-permute-done.12.refs_7_), channel_id=1, source_target_pairs={{0,1},{1,2},{2,3},{3,4},{4,5},{5,6},{6,7},{7,0},{8,9},{9,10},{10,1... | collective-permute-start | bytes 786440 | tf_op jit(solution)/shard_map/ppermute | solution.py:25
  26.1 16.0 %collective-permute-start.6 = (bf16[16,9216]{1,0:T(8,128)(2,1)S(1)}, bf16[16,9216]{1,0:T(8,128)(2,1)S(1)}, u32[]{:S(2)}, u32[]{:S(2)}) collective-permute-start(bf16[16,9216]{1,0:T(8,128)(2,1)S(1)} %pad_maximum_fusion.refs_0_), channel_id=1, source_target_pairs={{0,1},{1,2},{2,3},{3,4},{4,5},{5,6},{6,7},{7,0},{8,9},{9,10},{10,1... | collective-permute-start | bytes 884744 | tf_op jit(solution)/shard_map/ppermute | solution.py:25
  26.1 15.9 %collective-permute-start.3 = (bf16[16,9216]{1,0:T(8,128)(2,1)S(1)}, bf16[16,9216]{1,0:T(8,128)(2,1)}, u32[]{:S(2)}, u32[]{:S(2)}) collective-permute-start(bf16[16,9216]{1,0:T(8,128)(2,1)S(1)} %collective-permute-done.2.refs_1_), channel_id=1, source_target_pairs={{0,7},{1,0},{2,1},{3,2},{4,3},{5,4},{6,5},{7,6},{8,15},{9,8},{10,9... | collective-permute-start | bytes 884744 | tf_op jit(solution)/shard_map/ppermute | solution.py:25
  33.3 12.0 %collective-permute-start.10 = (bf16[16,8192]{1,0:T(8,128)(2,1)S(1)}, bf16[16,8192]{1,0:T(8,128)(2,1)}, u32[]{:S(2)}, u32[]{:S(2)}) collective-permute-start(bf16[16,8192]{1,0:T(8,128)(2,1)S(1)} %collective-permute-done.9.refs_1_), channel_id=1, source_target_pairs={{0,7},{1,0},{2,1},{3,2},{4,3},{5,4},{6,5},{7,6},{8,15},{9,8},{10,9... | collective-permute-start | bytes 786440 | tf_op jit(solution)/shard_map/ppermute | solution.py:25
  34.9 0.7 copy-start.6
  35.7 12.0 %collective-permute-start.14 = (bf16[16,8192]{1,0:T(8,128)(2,1)S(1)}, bf16[16,8192]{1,0:T(8,128)(2,1)}, u32[]{:S(2)}, u32[]{:S(2)}) collective-permute-start(bf16[16,8192]{1,0:T(8,128)(2,1)S(1)} %collective-permute-done.13.refs_6_), channel_id=1, source_target_pairs={{0,1},{1,2},{2,3},{3,4},{4,5},{5,6},{6,7},{7,0},{8,9},{9,10},{10,1... | collective-permute-start | bytes 786440 | tf_op jit(solution)/shard_map/ppermute | solution.py:25
  36.0 0.7 copy-start.8
  42.0 12.0 %collective-permute-start.7 = (bf16[16,9216]{1,0:T(8,128)(2,1)S(1)}, bf16[16,9216]{1,0:T(8,128)(2,1)}, u32[]{:S(2)}, u32[]{:S(2)}) collective-permute-start(bf16[16,9216]{1,0:T(8,128)(2,1)S(1)} %collective-permute-done.6.refs_7_), channel_id=1, source_target_pairs={{0,1},{1,2},{2,3},{3,4},{4,5},{5,6},{6,7},{7,0},{8,9},{9,10},{10,1... | collective-permute-start | bytes 884744 | tf_op jit(solution)/shard_map/ppermute | solution.py:25
  42.1 12.0 %collective-permute-start.4 = (bf16[16,9216]{1,0:T(8,128)(2,1)}, bf16[16,9216]{1,0:T(8,128)(2,1)}, u32[]{:S(2)}, u32[]{:S(2)}) collective-permute-start(bf16[16,9216]{1,0:T(8,128)(2,1)} %collective-permute-done.3.refs_2_), channel_id=1, source_target_pairs={{0,7},{1,0},{2,1},{3,2},{4,3},{5,4},{6,5},{7,6},{8,15},{9,8},{10,9... | collective-permute-start | bytes 884744 | tf_op jit(solution)/shard_map/ppermute | solution.py:25
  45.3 12.2 %collective-permute-start.11 = (bf16[16,8192]{1,0:T(8,128)(2,1)}, bf16[16,8192]{1,0:T(8,128)(2,1)}, u32[]{:S(2)}, u32[]{:S(2)}) collective-permute-start(bf16[16,8192]{1,0:T(8,128)(2,1)} %collective-permute-done.10.refs_2_), channel_id=1, source_target_pairs={{0,7},{1,0},{2,1},{3,2},{4,3},{5,4},{6,5},{7,6},{8,15},{9,8},{10,9... | collective-permute-start | bytes 786440 | tf_op jit(solution)/shard_map/ppermute | solution.py:25
  47.8 11.9 %collective-permute-start.15 = (bf16[16,8192]{1,0:T(8,128)(2,1)}, bf16[16,8192]{1,0:T(8,128)(2,1)}, u32[]{:S(2)}, u32[]{:S(2)}) collective-permute-start(bf16[16,8192]{1,0:T(8,128)(2,1)} %collective-permute-done.14.refs_5_), channel_id=1, source_target_pairs={{0,1},{1,2},{2,3},{3,4},{4,5},{5,6},{6,7},{7,0},{8,9},{9,10},{10,1... | collective-permute-start | bytes 786440 | tf_op jit(solution)/shard_map/ppermute | solution.py:25
  54.1 11.5 %collective-permute-start.8 = (bf16[16,9216]{1,0:T(8,128)(2,1)}, bf16[16,9216]{1,0:T(8,128)(2,1)}, u32[]{:S(2)}, u32[]{:S(2)}) collective-permute-start(bf16[16,9216]{1,0:T(8,128)(2,1)} %collective-permute-done.7.refs_6_), channel_id=1, source_target_pairs={{0,1},{1,2},{2,3},{3,4},{4,5},{5,6},{6,7},{7,0},{8,9},{9,10},{10,1... | collective-permute-start | bytes 884744 | tf_op jit(solution)/shard_map/ppermute | solution.py:25
  54.1 11.5 %collective-permute-start.5 = (bf16[16,9216]{1,0:T(8,128)(2,1)}, bf16[16,9216]{1,0:T(8,128)(2,1)}, u32[]{:S(2)}, u32[]{:S(2)}) collective-permute-start(bf16[16,9216]{1,0:T(8,128)(2,1)} %collective-permute-done.4.refs_3_), channel_id=1, source_target_pairs={{0,7},{1,0},{2,1},{3,2},{4,3},{5,4},{6,5},{7,6},{8,15},{9,8},{10,9... | collective-permute-start | bytes 884744 | tf_op jit(solution)/shard_map/ppermute | solution.py:25
  57.4 8.2 %copy-start = (bf16[256,512]{1,0:T(8,128)(2,1)S(1)}, bf16[256,512]{1,0:T(8,128)(2,1)}, u32[]{:S(2)}) copy-start(bf16[256,512]{1,0:T(8,128)(2,1)} %o_ref.1) | copy-start | bytes 786436
  59.7 1.0 copy-start.4
  60.6 0.9 copy-start.7
  61.6 0.9 copy-start.9
  62.5 10.0 %slice-start = ((s8[8388608]{0:T(1024)(128)(4,1)}), s8[4194304]{0:T(1024)(128)(4,1)S(1)}, s32[]{:S(2)}) async-start(s8[8388608]{0:T(1024)(128)(4,1)} %bitcast.10), calls=%async_computation.2 | async-start | bytes 8388608
  65.6 6.9 %copy-start.1 = (bf16[512,64]{0,1:T(8,128)(2,1)S(1)}, bf16[512,64]{0,1:T(8,128)(2,1)}, u32[]{:S(2)}) copy-start(bf16[512,64]{0,1:T(8,128)(2,1)} %param.16) | copy-start | bytes 196612
  65.6 6.9 %slice-start.1 = ((s8[8388608]{0:T(1024)(128)(4,1)}), s8[4194304]{0:T(1024)(128)(4,1)S(1)}, s32[]{:S(2)}) async-start(s8[8388608]{0:T(1024)(128)(4,1)} %bitcast.10), calls=%async_computation.3 | async-start | bytes 8388608
  69.4 1.5 %collective-permute-start.16 = (bf16[64,1280]{1,0:T(8,128)(2,1)S(1)}, bf16[64,1280]{1,0:T(8,128)(2,1)S(1)}, u32[]{:S(2)}, u32[]{:S(2)}) collective-permute-start(bf16[64,1280]{1,0:T(8,128)(2,1)S(1)} %get-tuple-element.75), channel_id=1, source_target_pairs={{0,16},{16,0},{1,17},{17,1},{2,18},{18,2},{3,19},{19,3},{4,20},{20... | collective-permute-start | bytes 491528 | tf_op jit(solution)/shard_map/ppermute | solution.py:25
  69.5 8.2 %collective-permute-start.19 = (bf16[8,256,256]{2,1,0:T(8,128)(2,1)S(1)}, bf16[8,256,256]{2,1,0:T(8,128)(2,1)S(1)}, u32[]{:S(2)}, u32[]{:S(2)}) collective-permute-start(bf16[8,256,256]{2,1,0:T(8,128)(2,1)S(1)} %all-to-all-done.kv_ref), channel_id=1, source_target_pairs={{0,16},{16,0},{1,17},{17,1},{2,18},{18,2},{3,19},{19,3},{4,20},{20... | collective-permute-start | bytes 3145736 | tf_op jit(solution)/shard_map/ppermute | solution.py:25
  70.9 6.3 %collective-permute-start.17 = (bf16[64,1280]{1,0:T(8,128)(2,1)S(1)}, bf16[64,1280]{1,0:T(8,128)(2,1)S(1)}, u32[]{:S(2)}, u32[]{:S(2)}) collective-permute-start(bf16[64,1280]{1,0:T(8,128)(2,1)S(1)} %add_convert_fusion.4), channel_id=1, source_target_pairs={{0,128},{128,0},{1,129},{129,1},{2,130},{130,2},{3,131},{131,3},{4... | collective-permute-start | bytes 491528 | tf_op jit(solution)/shard_map/ppermute | solution.py:25
  72.5 5.2 %copy-start.5 = (bf16[256,512]{1,0:T(8,128)(2,1)S(1)}, bf16[256,512]{1,0:T(8,128)(2,1)}, u32[]{:S(2)}) copy-start(bf16[256,512]{1,0:T(8,128)(2,1)} %q_ref.1) | copy-start | bytes 786436
  72.5 5.2 %copy-start.10 = (f32[4,256]{1,0:T(4,128)S(1)}, f32[4,256]{1,0:T(4,128)}, u32[]{:S(2)}) copy-start(f32[4,256]{1,0:T(4,128)} %norm_ref.1) | copy-start | bytes 12292
  77.3 5.5 %collective-permute-start.18 = (bf16[64,1280]{1,0:T(8,128)(2,1)S(1)}, bf16[64,1280]{1,0:T(8,128)(2,1)S(1)}, u32[]{:S(2)}, u32[]{:S(2)}) collective-permute-start(bf16[64,1280]{1,0:T(8,128)(2,1)S(1)} %add_convert_fusion.3), channel_id=1, source_target_pairs={{0,32},{32,0},{64,96},{96,64},{1,33},{33,1},{65,97},{97,65},{2,34}... | collective-permute-start | bytes 491528 | tf_op jit(solution)/shard_map/ppermute | solution.py:416
  82.9 8.4 %collective-permute-start.20 = (bf16[64,1280]{1,0:T(8,128)(2,1)S(1)}, bf16[64,1280]{1,0:T(8,128)(2,1)}, u32[]{:S(2)}, u32[]{:S(2)}) collective-permute-start(bf16[64,1280]{1,0:T(8,128)(2,1)S(1)} %add_convert_fusion.2), channel_id=1, source_target_pairs={{0,96},{32,64},{64,32},{96,0},{1,97},{33,65},{65,33},{97,1},{2,98}... | collective-permute-start | bytes 491528 | tf_op jit(solution)/shard_map/ppermute | solution.py:421
  91.2 2.7 %collective-permute-start.22 = (bf16[8,256,256]{2,1,0:T(8,128)(2,1)S(1)}, bf16[8,256,256]{2,1,0:T(8,128)(2,1)S(1)}, u32[]{:S(2)}, u32[]{:S(2)}) collective-permute-start(bf16[8,256,256]{2,1,0:T(8,128)(2,1)S(1)} %get-tuple-element.112), channel_id=1, source_target_pairs={{0,16},{16,0},{1,17},{17,1},{2,18},{18,2},{3,19},{19,3},{4,20},{20... | collective-permute-start | bytes 3145736 | tf_op jit(solution)/shard_map/ppermute | solution.py:25
  92.2 2.9 %collective-permute-start.21 = (bf16[64,1280]{1,0:T(8,128)(2,1)S(1)}, bf16[64,1280]{1,0:T(8,128)(2,1)S(1)}, u32[]{:S(2)}, u32[]{:S(2)}) collective-permute-start(bf16[64,1280]{1,0:T(8,128)(2,1)S(1)} %add_convert_fusion.1), channel_id=1, source_target_pairs={{0,16},{16,0},{1,17},{17,1},{2,18},{18,2},{3,19},{19,3},{4,20},{20... | collective-permute-start | bytes 491528 | tf_op jit(solution)/shard_map/ppermute | solution.py:25
  95.1 20.4 %all-to-all-start.1 = ((bf16[8,256,256]{2,1,0:T(8,128)(2,1)}), bf16[8,256,256]{2,1,0:T(8,128)(2,1)S(1)}, u32[]{:S(2)}, u32[]{:S(2)}) async-start(bf16[8,256,256]{2,1,0:T(8,128)(2,1)} %add_convert_fusion), calls=%async_computation.1 | async-start | bytes 2097152 | tf_op jit(solution)/shard_map/all_to_all | solution.py:427
  100.5 9.4 %collective-permute-start.25 = (bf16[64,2048]{1,0:T(8,128)(2,1)S(1)}, bf16[64,2048]{1,0:T(8,128)(2,1)S(1)}, u32[]{:S(2)}, u32[]{:S(2)}) collective-permute-start(bf16[64,2048]{1,0:T(8,128)(2,1)S(1)} %pad_maximum_fusion.1.refs_0_), channel_id=1, source_target_pairs={{0,1},{1,2},{2,3},{3,4},{4,5},{5,6},{6,7},{7,0},{8,9},{9,10},{10,1... | collective-permute-start | bytes 786440 | tf_op jit(solution)/shard_map/ppermute | solution.py:25
  100.5 9.4 %collective-permute-start.24 = (bf16[64,2048]{1,0:T(8,128)(2,1)S(1)}, bf16[64,2048]{1,0:T(8,128)(2,1)S(1)}, u32[]{:S(2)}, u32[]{:S(2)}) collective-permute-start(bf16[64,2048]{1,0:T(8,128)(2,1)S(1)} %pad_maximum_fusion.1.refs_0_), channel_id=1, source_target_pairs={{0,7},{1,0},{2,1},{3,2},{4,3},{5,4},{6,5},{7,6},{8,15},{9,8},{10,9... | collective-permute-start | bytes 786440 | tf_op jit(solution)/shard_map/ppermute | solution.py:25
  109.8 6.6 %collective-permute-start.26 = (bf16[64,1024]{1,0:T(8,128)(2,1)S(1)}, bf16[64,1024]{1,0:T(8,128)(2,1)S(1)}, u32[]{:S(2)}, u32[]{:S(2)}) collective-permute-start(bf16[64,1024]{1,0:T(8,128)(2,1)S(1)} %slice.58), channel_id=1, source_target_pairs={{0,1},{1,2},{2,3},{3,4},{4,5},{5,6},{6,7},{7,0},{8,9},{9,10},{10,1... | collective-permute-start | bytes 393224 | tf_op jit(solution)/shard_map/ppermute | solution.py:25
  109.9 6.5 %collective-permute-start.27 = (bf16[64,1024]{1,0:T(8,128)(2,1)S(1)}, bf16[64,1024]{1,0:T(8,128)(2,1)S(1)}, u32[]{:S(2)}, u32[]{:S(2)}) collective-permute-start(bf16[64,1024]{1,0:T(8,128)(2,1)S(1)} %slice.59), channel_id=1, source_target_pairs={{0,7},{1,0},{2,1},{3,2},{4,3},{5,4},{6,5},{7,6},{8,15},{9,8},{10,9... | collective-permute-start | bytes 393224 | tf_op jit(solution)/shard_map/ppermute | solution.py:25
  115.7 5.1 %collective-permute-start.23 = (bf16[256,256]{1,0:T(8,128)(2,1)S(1)}, bf16[256,256]{1,0:T(8,128)(2,1)S(1)}, u32[]{:S(2)}, u32[]{:S(2)}) collective-permute-start(bf16[256,256]{1,0:T(8,128)(2,1)S(1)} %get-tuple-element.115), channel_id=1, source_target_pairs={{0,1},{1,0},{2,3},{3,2},{4,5},{5,4},{6,7},{7,6},{8,9},{9,8},{10,11... | collective-permute-start | bytes 393224 | tf_op jit(solution)/shard_map/ppermute | solution.py:436

commit v3 on v2

--- a/solution.py
+++ b/solution.py
@@ -306,31 +306,36 @@
     kv[0], kv[1] = kv_ref[...], other_kv_ref[...]
     dkv_ref[0], dkv_ref[1] = dkv_in[...], other_dkv_in[...]
     dq_sum[...] = dq_in[...]
-    key_at = lax.broadcasted_iota(jnp.int32, (HALF, heads * HALF), 0)
-    query_at = lax.broadcasted_iota(jnp.int32, (HALF, heads * HALF), 1) % HALF
-    ahead = query_at - key_at
+    side = (2 * HALF, heads * HALF)
+    key_at = lax.broadcasted_iota(jnp.int32, side, 0)
+    query_at = lax.broadcasted_iota(jnp.int32, side, 1) % HALF
+    ahead = query_at - key_at % HALF
+    second = key_at >= HALF
 
     def unit(i):
-        late = (i > c).astype(jnp.int32)
-        s = i - late
+        late = (i > lax.div(c, 2)).astype(jnp.int32)
+        k = i - late
         first = pl.multiple_of(late * HALF, HALF)
-        visible = ahead >= jnp.where(s == c, 0, -HALF)
-        other = jnp.where(lax.rem(s, 2) == core, 0, 1)
-        k = lax.div(s, 2)
-        keys = kv[other, k, pl.ds(first, HALF), :HEAD_DIM]
-        values = kv[other, k, pl.ds(first, HALF), HEAD_DIM:]
+        behind = [
+            jnp.where(s == c, 0, jnp.where((s < c) == (late == 0), -HALF, HALF))
+            for s in (2 * k + core, 2 * k + 1 - core)
+        ]
+        visible = ahead >= jnp.where(second, behind[1], behind[0])
+        keys = kv[:, k, pl.ds(first, HALF), :HEAD_DIM].reshape(2 * HALF, HEAD_DIM)
+        values = kv[:, k, pl.ds(first, HALF), HEAD_DIM:].reshape(2 * HALF, HEAD_DIM)
         query_grad, key_grad, value_grad = tile(
             qs[late], gs[late], norm[late], delta[late], keys, values, visible
         )
-        return late, (other, k), first, query_grad, jnp.concatenate([key_grad, value_grad], 1)
-
-    def stored(late, block, first, query_grad, now):
+        return late, k, first, query_grad, jnp.concatenate([key_grad, value_grad], 1)
+
+    def stored(late, k, first, query_grad, now):
         dq_sum[late] += query_grad
-        before = dkv_ref[*block, pl.ds(first, HALF), :].astype(F32)
-        dkv_ref[*block, pl.ds(first, HALF), :] = (before + now).astype(BF16)
-
-    for first in range(0, 17, 4):
-        for done in [unit(i) for i in range(first, min(first + 4, 17))]:
+        at = (slice(None), k, pl.ds(first, HALF), slice(None))
+        before = dkv_ref[at].astype(F32).reshape(now.shape)
+        dkv_ref[at] = (before + now).astype(BF16).reshape(2, HALF, now.shape[1])
+
+    for first in range(0, 9, 3):
+        for done in [unit(i) for i in range(first, first + 3)]:
             stored(*done)
     mine_ref[...] = dkv_ref[0]
     yours_ref[...] = dkv_ref[1]

time: 122 us -> 122 us (level)
  no operation moved by 1% of the time
where the time goes in v3:
time: 122 us; the launch traced here: 120 us
  starting transfers between devices  47.7 us (39%)
  waiting for transfers between devices  40.2 us (33%)
  Pallas kernels  20.5 us (17%)
  local copies, waits for them, and re-layouts  6.04 us (5%)
  other arithmetic  4.05 us (3%)
    ppermute x25, starting transfers between devices, turned(): return lax.ppermute(x, axis, [(i, (i + by) % size) for i in range(size)])  34.4 us
    ppermute x25, waiting for transfers between devices, turned(): return lax.ppermute(x, axis, [(i, (i + by) % size) for i in range(size)])  33.4 us
    all_to_all x1, starting transfers between devices, local(): lax.all_to_all(jnp.broadcast_to(kv[None], (8,) + kv.shape), CTX[:2], 0, 0)  5.84 us
    pallas_call x1, Pallas kernels, rest_call(): pl.pallas_call(rest_kernel, out_shape=(jax.ShapeDtypeStruct((2 * HALF, si...  5.66 us
    all_to_all x1, starting transfers between devices, local(): pieces = lax.all_to_all(mine, CTX[:2], 0, 0)  5.24 us
    unnamed x26, local copies, waits for them, and re-layouts  4.29 us
    pallas_call x1, Pallas kernels, adapter_call(): pl.pallas_call(adapter_kernel, out_shape=(jax.ShapeDtypeStruct((128, widt...  3.8 us
    pallas_call x1, Pallas kernels, late_call(): pl.pallas_call(late_kernel, out_shape=(stacked, stacked, line, line, jax....  3.29 us
  transfers between devices with their start and end apart: 30, of which 15 were waited for; matrix products, arithmetic and copies ran while one was open for 5% of the time, Pallas kernels for 14%

profile of v3, /device:TPU:2, one launch (start us, length us, event | category | flops | bytes accessed | tf_op | source)
XLA Modules:
  0.0 120.5 jit_solution(3297421409668862498)
XLA Ops:
  0.6 3.3 %collective-permute-start = (bf16[16,8192]{1,0:T(8,128)(2,1)}, bf16[16,8192]{1,0:T(8,128)(2,1)S(1)}, u32[]{:S(2)}, u32[]{:S(2)}) collective-permute-start(bf16[16,8192]{1,0:T(8,128)(2,1)} %refs_0_), channel_id=1, source_target_pairs={{0,8},{8,0},{1,9},{9,1},{2,10},{10,2},{3,11},{11,3},{4,12},{12,4},... | collective-permute-start | bytes 786440 | tf_op jit(solution)/shard_map/ppermute | solution.py:25
  3.9 1.9 %collective-permute-start.12 = (bf16[16,8192]{1,0:T(8,128)(2,1)}, bf16[16,8192]{1,0:T(8,128)(2,1)}, u32[]{:S(2)}, u32[]{:S(2)}) collective-permute-start(bf16[16,8192]{1,0:T(8,128)(2,1)} %refs_0_), channel_id=1, source_target_pairs={{0,1},{1,2},{2,3},{3,4},{4,5},{5,6},{6,7},{7,0},{8,9},{9,10},{10,1... | collective-permute-start | bytes 786440 | tf_op jit(solution)/shard_map/ppermute | solution.py:25
  5.8 1.2 fusion.3
  7.1 0.4 collective-permute-start.1
  7.5 0.9 pad_maximum_fusion.2
  8.4 4.2 %collective-permute-done.1 = bf16[16,1024]{1,0:T(8,128)(2,1)S(1)} collective-permute-done((bf16[16,1024]{1,0:T(8,128)(2,1)S(1)}, bf16[16,1024]{1,0:T(8,128)(2,1)S(1)}, u32[]{:S(2)}, u32[]{:S(2)}) %collective-permute-start.1) | collective-permute-done | bytes 32800 | tf_op jit(solution)/shard_map/ppermute | solution.py:25
  12.6 4.5 %collective-permute-start.2 = (bf16[16,9216]{1,0:T(8,128)(2,1)S(1)}, bf16[16,9216]{1,0:T(8,128)(2,1)S(1)}, u32[]{:S(2)}, u32[]{:S(2)}) collective-permute-start(bf16[16,9216]{1,0:T(8,128)(2,1)S(1)} %pad_maximum_fusion.refs_0_), channel_id=1, source_target_pairs={{0,7},{1,0},{2,1},{3,2},{4,3},{5,4},{6,5},{7,6},{8,15},{9,8},{10,9... | collective-permute-start | bytes 884744 | tf_op jit(solution)/shard_map/ppermute | solution.py:25
  17.2 1.0 broadcast_in_dim.2
  18.2 5.8 %all-to-all-start = ((bf16[8,256,256]{2,1,0:T(8,128)(2,1)}), bf16[8,256,256]{2,1,0:T(8,128)(2,1)S(1)}, u32[]{:S(2)}, u32[]{:S(2)}) async-start(bf16[8,256,256]{2,1,0:T(8,128)(2,1)} %broadcast_in_dim.2), calls=%async_computation | async-start | bytes 2097152 | tf_op jit(solution)/shard_map/all_to_all | solution.py:408
  24.0 1.0 collective-permute-start.9
  25.1 1.0 collective-permute-start.13
  26.1 0.0 collective-permute-start.6
  26.1 3.2 %collective-permute-start.3 = (bf16[16,9216]{1,0:T(8,128)(2,1)S(1)}, bf16[16,9216]{1,0:T(8,128)(2,1)}, u32[]{:S(2)}, u32[]{:S(2)}) collective-permute-start(bf16[16,9216]{1,0:T(8,128)(2,1)S(1)} %collective-permute-done.2.refs_1_), channel_id=1, source_target_pairs={{0,7},{1,0},{2,1},{3,2},{4,3},{5,4},{6,5},{7,6},{8,15},{9,8},{10,9... | collective-permute-start | bytes 884744 | tf_op jit(solution)/shard_map/ppermute | solution.py:25
  29.3 4.0 %collective-permute-done.9.refs_1_ = bf16[16,8192]{1,0:T(8,128)(2,1)S(1)} collective-permute-done((bf16[16,8192]{1,0:T(8,128)(2,1)S(1)}, bf16[16,8192]{1,0:T(8,128)(2,1)S(1)}, u32[]{:S(2)}, u32[]{:S(2)}) %collective-permute-start.9) | collective-permute-done | bytes 262176 | tf_op jit(solution)/shard_map/ppermute | solution.py:25
  33.3 1.6 %collective-permute-start.10 = (bf16[16,8192]{1,0:T(8,128)(2,1)S(1)}, bf16[16,8192]{1,0:T(8,128)(2,1)}, u32[]{:S(2)}, u32[]{:S(2)}) collective-permute-start(bf16[16,8192]{1,0:T(8,128)(2,1)S(1)} %collective-permute-done.9.refs_1_), channel_id=1, source_target_pairs={{0,7},{1,0},{2,1},{3,2},{4,3},{5,4},{6,5},{7,6},{8,15},{9,8},{10,9... | collective-permute-start | bytes 786440 | tf_op jit(solution)/shard_map/ppermute | solution.py:25
  34.9 0.7 copy-done.6
  35.6 0.1 collective-permute-done.13.refs_6_
  35.7 0.3 collective-permute-start.14
  36.0 0.7 copy-done.8
  36.7 5.3 %collective-permute-done.6.refs_7_ = bf16[16,9216]{1,0:T(8,128)(2,1)S(1)} collective-permute-done((bf16[16,9216]{1,0:T(8,128)(2,1)S(1)}, bf16[16,9216]{1,0:T(8,128)(2,1)S(1)}, u32[]{:S(2)}, u32[]{:S(2)}) %collective-permute-start.6) | collective-permute-done | bytes 294944 | tf_op jit(solution)/shard_map/ppermute | solution.py:25
  42.1 3.2 %collective-permute-start.4 = (bf16[16,9216]{1,0:T(8,128)(2,1)}, bf16[16,9216]{1,0:T(8,128)(2,1)}, u32[]{:S(2)}, u32[]{:S(2)}) collective-permute-start(bf16[16,9216]{1,0:T(8,128)(2,1)} %collective-permute-done.3.refs_2_), channel_id=1, source_target_pairs={{0,7},{1,0},{2,1},{3,2},{4,3},{5,4},{6,5},{7,6},{8,15},{9,8},{10,9... | collective-permute-start | bytes 884744 | tf_op jit(solution)/shard_map/ppermute | solution.py:25
  45.3 0.0 collective-permute-done.10.refs_2_
  45.3 1.1 collective-permute-start.11
  46.4 1.3 %collective-permute-done.14.refs_5_ = bf16[16,8192]{1,0:T(8,128)(2,1)} collective-permute-done((bf16[16,8192]{1,0:T(8,128)(2,1)S(1)}, bf16[16,8192]{1,0:T(8,128)(2,1)}, u32[]{:S(2)}, u32[]{:S(2)}) %collective-permute-start.14) | collective-permute-done | bytes 262176 | tf_op jit(solution)/shard_map/ppermute | solution.py:25
  47.8 6.3 %collective-permute-done.7.refs_6_ = bf16[16,9216]{1,0:T(8,128)(2,1)} collective-permute-done((bf16[16,9216]{1,0:T(8,128)(2,1)S(1)}, bf16[16,9216]{1,0:T(8,128)(2,1)}, u32[]{:S(2)}, u32[]{:S(2)}) %collective-permute-start.7) | collective-permute-done | bytes 294944 | tf_op jit(solution)/shard_map/ppermute | solution.py:25
  54.1 3.2 %collective-permute-start.5 = (bf16[16,9216]{1,0:T(8,128)(2,1)}, bf16[16,9216]{1,0:T(8,128)(2,1)}, u32[]{:S(2)}, u32[]{:S(2)}) collective-permute-start(bf16[16,9216]{1,0:T(8,128)(2,1)} %collective-permute-done.4.refs_3_), channel_id=1, source_target_pairs={{0,7},{1,0},{2,1},{3,2},{4,3},{5,4},{6,5},{7,6},{8,15},{9,8},{10,9... | collective-permute-start | bytes 884744 | tf_op jit(solution)/shard_map/ppermute | solution.py:25
  57.3 0.1 pad_add_fusion.where_ref
  57.4 0.1 collective-permute-done.11.refs_3_
  57.5 2.2 %collective-permute-done.15.refs_4_ = bf16[16,8192]{1,0:T(8,128)(2,1)} collective-permute-done((bf16[16,8192]{1,0:T(8,128)(2,1)}, bf16[16,8192]{1,0:T(8,128)(2,1)}, u32[]{:S(2)}, u32[]{:S(2)}) %collective-permute-start.15) | collective-permute-done | bytes 262176 | tf_op jit(solution)/shard_map/ppermute | solution.py:25
  59.7 0.9 copy-done.4
  60.6 0.9 copy-done.7
  61.6 0.9 copy-done.9
  62.5 3.0 %shard_map.128 = (bf16[128,8192]{1,0:T(8,128)(2,1)S(1)}, bf16[128,64]{1,0:T(8,128)(2,1)S(1)}) custom-call(s32[4]{0:T(128)S(1)} %pad_add_fusion.where_ref, bf16[16,8192]{1,0:T(8,128)(2,1)S(1)} %copy-done.4, bf16[16,8192]{1,0:T(8,128)(2,1)S(1)} %copy-done.7, bf16[16,8192]{1,0:T(8,128)(2,1)} %collective-permute-done.10.refs_2_, ...), custom_call_target="tpu_custom_call" | custom-call | flops 2000000000 | bytes 4194304 | tf_op jit(solution)/shard_map/pallas_call | solution.py:139
  65.6 0.0 copy-start.1
  65.6 0.0 slice-start.1
  65.6 3.8 %shard_map.129 = (bf16[128,8192]{1,0:T(8,128)(2,1)S(1)}, bf16[256,64]{1,0:T(8,128)(2,1)S(1)}, f32[64,1280]{1,0:T(8,128)S(1)}, bf16[64,1280]{1,0:T(8,128)(2,1)S(1)}) custom-call(s32[4]{0:T(128)S(1)} %pad_add_fusion.where_ref, bf16[16,9216]{1,0:T(8,128)(2,1)S(1)} %pad_maximum_fusion.refs_0_, bf16[16,9216]{1,0:T(8,128)(2,1)S(1)} %collective-permute-done.2.refs_1_, ...), custom_call_target="tpu_custom_call" | custom-call | flops 2000000000 | bytes 4194304 | tf_op jit(solution)/shard_map/pallas_call | solution.py:200
  69.4 0.1 collective-permute-start.16
  69.5 0.5 collective-permute-start.19
  70.0 0.9 collective-permute-done.16
  70.9 1.5 %collective-permute-start.17 = (bf16[64,1280]{1,0:T(8,128)(2,1)S(1)}, bf16[64,1280]{1,0:T(8,128)(2,1)S(1)}, u32[]{:S(2)}, u32[]{:S(2)}) collective-permute-start(bf16[64,1280]{1,0:T(8,128)(2,1)S(1)} %add_convert_fusion.4), channel_id=1, source_target_pairs={{0,128},{128,0},{1,129},{129,1},{2,130},{130,2},{3,131},{131,3},{4... | collective-permute-start | bytes 491528 | tf_op jit(solution)/shard_map/ppermute | solution.py:25
  72.5 3.0 %shard_map.130.g_ref = bf16[2,128,512]{2,1,0:T(8,128)(2,1)S(1)} custom-call(s32[4]{0:T(128)S(1)} %pad_add_fusion.where_ref, bf16[128,8192]{1,0:T(8,128)(2,1)S(1)} %get-tuple-element.71.refs_9_.own_ref, bf16[128,8192]{1,0:T(8,128)(2,1)S(1)} %get-tuple-element.77.peer_ref, bf16[512,8192]{1,0:T(8,128)(2,1)S(1)} %bitcast.11, ...), custom_call_target="tpu_custom_call" | custom-call | flops 10000000000 | bytes 8388608 | tf_op jit(solution)/shard_map/pallas_call | solution.py:240
  75.5 1.8 %collective-permute-done.17 = bf16[64,1280]{1,0:T(8,128)(2,1)S(1)} collective-permute-done((bf16[64,1280]{1,0:T(8,128)(2,1)S(1)}, bf16[64,1280]{1,0:T(8,128)(2,1)S(1)}, u32[]{:S(2)}, u32[]{:S(2)}) %collective-permute-start.17) | collective-permute-done | bytes 163872 | tf_op jit(solution)/shard_map/ppermute | solution.py:25
  77.3 0.4 collective-permute-start.18
  77.7 3.3 %shard_map.131 = (bf16[2,512,128]{2,1,0:T(8,128)(2,1)S(1)}, bf16[2,512,128]{2,1,0:T(8,128)(2,1)S(1)}, f32[2,1,512]{2,1,0:T(1,128)S(1)}, f32[2,1,512]{2,1,0:T(1,1...) custom-call(bf16[256,512]{1,0:T(8,128)(2,1)S(1)} %copy-done.5, ...), custom_call_target="tpu_custom_call" | custom-call | flops 10000000000 | bytes 4194304 | tf_op jit(solution)/shard_map/pallas_call | solution.py:355
  81.0 1.8 %collective-permute-done.18 = bf16[64,1280]{1,0:T(8,128)(2,1)S(1)} collective-permute-done((bf16[64,1280]{1,0:T(8,128)(2,1)S(1)}, bf16[64,1280]{1,0:T(8,128)(2,1)S(1)}, u32[]{:S(2)}, u32[]{:S(2)}) %collective-permute-start.18) | collective-permute-done | bytes 163872 | tf_op jit(solution)/shard_map/ppermute | solution.py:421
  82.9 1.8 %collective-permute-start.20 = (bf16[64,1280]{1,0:T(8,128)(2,1)S(1)}, bf16[64,1280]{1,0:T(8,128)(2,1)}, u32[]{:S(2)}, u32[]{:S(2)}) collective-permute-start(bf16[64,1280]{1,0:T(8,128)(2,1)S(1)} %add_convert_fusion.2), channel_id=1, source_target_pairs={{0,96},{32,64},{64,32},{96,0},{1,97},{33,65},{65,33},{97,1},{2,98}... | collective-permute-start | bytes 491528 | tf_op jit(solution)/shard_map/ppermute | solution.py:426
  84.6 5.7 %shard_map.132 = (bf16[256,512]{1,0:T(8,128)(2,1)}, bf16[8,256,256]{2,1,0:T(8,128)(2,1)S(1)}, bf16[8,256,256]{2,1,0:T(8,128)(2,1)S(1)}) custom-call(s32[4]{0:T(128)S(1)} %pad_add_fusion.where_ref, bf16[2,512,128]{2,1,0:T(8,128)(2,1)S(1)} %get-tuple-element.99.qs, bf16[2,512,128]{2,1,0:T(8,128)(2,1)S(1)} %get-tuple-element.100.gs, ...), custom_call_target="tpu_custom_call" | custom-call | flops 10000000000 | bytes 4194304 | tf_op jit(solution)/shard_map/pallas_call | solution.py:380
  90.3 1.0 add_convert_fusion.1
  91.3 0.6 collective-permute-start.21
  91.9 1.1 collective-permute-done.22
  93.0 1.2 %add_convert_fusion = bf16[8,256,256]{2,1,0:T(8,128)(2,1)} fusion(bf16[8,256,256]{2,1,0:T(8,128)(2,1)S(1)} %collective-permute-done.22, bf16[8,256,256]{2,1,0:T(8,128)(2,1)S(1)} %get-tuple-element.111), kind=kLoop, calls=%fused_computation | loop fusion | flops 2097152 | bytes 3145728 | tf_op jit(solution)/shard_map/convert_element_type | solution.py:430
  94.2 5.2 %all-to-all-start.1 = ((bf16[8,256,256]{2,1,0:T(8,128)(2,1)}), bf16[8,256,256]{2,1,0:T(8,128)(2,1)S(1)}, u32[]{:S(2)}, u32[]{:S(2)}) async-start(bf16[8,256,256]{2,1,0:T(8,128)(2,1)} %add_convert_fusion), calls=%async_computation.1 | async-start | bytes 2097152 | tf_op jit(solution)/shard_map/all_to_all | solution.py:432
  99.5 0.1 collective-permute-start.25
  99.6 3.2 %collective-permute-start.24 = (bf16[64,2048]{1,0:T(8,128)(2,1)S(1)}, bf16[64,2048]{1,0:T(8,128)(2,1)S(1)}, u32[]{:S(2)}, u32[]{:S(2)}) collective-permute-start(bf16[64,2048]{1,0:T(8,128)(2,1)S(1)} %pad_maximum_fusion.1.refs_0_), channel_id=1, source_target_pairs={{0,7},{1,0},{2,1},{3,2},{4,3},{5,4},{6,5},{7,6},{8,15},{9,8},{10,9... | collective-permute-start | bytes 786440 | tf_op jit(solution)/shard_map/ppermute | solution.py:25
  102.8 6.0 %collective-permute-done.25.refs_4_ = bf16[64,2048]{1,0:T(8,128)(2,1)S(1)} collective-permute-done((bf16[64,2048]{1,0:T(8,128)(2,1)S(1)}, bf16[64,2048]{1,0:T(8,128)(2,1)S(1)}, u32[]{:S(2)}, u32[]{:S(2)}) %collective-permute-start.25) | collective-permute-done | bytes 262176 | tf_op jit(solution)/shard_map/ppermute | solution.py:25
  108.9 0.1 collective-permute-start.26
  109.0 3.3 %collective-permute-start.27 = (bf16[64,1024]{1,0:T(8,128)(2,1)S(1)}, bf16[64,1024]{1,0:T(8,128)(2,1)S(1)}, u32[]{:S(2)}, u32[]{:S(2)}) collective-permute-start(bf16[64,1024]{1,0:T(8,128)(2,1)S(1)} %slice.59), channel_id=1, source_target_pairs={{0,7},{1,0},{2,1},{3,2},{4,3},{5,4},{6,5},{7,6},{8,15},{9,8},{10,9... | collective-permute-start | bytes 393224 | tf_op jit(solution)/shard_map/ppermute | solution.py:25
  112.3 2.3 %all-to-all-done.1.pieces_ref = bf16[8,256,256]{2,1,0:T(8,128)(2,1)S(1)} async-done(((bf16[8,256,256]{2,1,0:T(8,128)(2,1)}), bf16[8,256,256]{2,1,0:T(8,128)(2,1)S(1)}, u32[]{:S(2)}, u32[]{:S(2)}) %all-to-all-start.1) | async-done | bytes 1048608 | tf_op jit(solution)/shard_map/all_to_all | solution.py:432
  114.6 0.1 shard_map.133
  114.7 0.1 collective-permute-start.23
  114.9 0.7 convert_bitcast_fusion
  115.5 1.6 %shard_map.134 = bf16[64,8192]{1,0:T(8,128)(2,1)} custom-call(s32[4]{0:T(128)S(1)} %pad_add_fusion.where_ref, bf16[64,2048]{1,0:T(8,128)(2,1)S(1)} %pad_maximum_fusion.1.refs_0_, bf16[64,2048]{1,0:T(8,128)(2,1)S(1)} %collective-permute-done.24.refs_1_, bf16[64,1024]{1,0:T(8,128)(2,1)S(1)} %collective-permute-done.26.refs_2_, ...), custom_call_target="tpu_custom_call" | custom-call | bytes 1048576 | tf_op jit(solution)/shard_map/pallas_call | solution.py:58
  117.1 2.7 %collective-permute-done.23 = bf16[256,256]{1,0:T(8,128)(2,1)S(1)} collective-permute-done((bf16[256,256]{1,0:T(8,128)(2,1)S(1)}, bf16[256,256]{1,0:T(8,128)(2,1)S(1)}, u32[]{:S(2)}, u32[]{:S(2)}) %collective-permute-start.23) | collective-permute-done | bytes 131104 | tf_op jit(solution)/shard_map/ppermute | solution.py:441
  119.8 0.7 fusion.1
  (54 shorter events, 0.4 us)
Async XLA Ops:
  0.6 12.0 %collective-permute-start = (bf16[16,8192]{1,0:T(8,128)(2,1)}, bf16[16,8192]{1,0:T(8,128)(2,1)S(1)}, u32[]{:S(2)}, u32[]{:S(2)}) collective-permute-start(bf16[16,8192]{1,0:T(8,128)(2,1)} %refs_0_), channel_id=1, source_target_pairs={{0,8},{8,0},{1,9},{9,1},{2,10},{10,2},{3,11},{11,3},{4,12},{12,4},... | collective-permute-start | bytes 786440 | tf_op jit(solution)/shard_map/ppermute | solution.py:25
  3.9 21.1 %collective-permute-start.12 = (bf16[16,8192]{1,0:T(8,128)(2,1)}, bf16[16,8192]{1,0:T(8,128)(2,1)}, u32[]{:S(2)}, u32[]{:S(2)}) collective-permute-start(bf16[16,8192]{1,0:T(8,128)(2,1)} %refs_0_), channel_id=1, source_target_pairs={{0,1},{1,2},{2,3},{3,4},{4,5},{5,6},{6,7},{7,0},{8,9},{9,10},{10,1... | collective-permute-start | bytes 786440 | tf_op jit(solution)/shard_map/ppermute | solution.py:25
  7.0 17.0 %copy-start.3 = (bf16[16,8192]{1,0:T(8,128)(2,1)S(1)}, bf16[16,8192]{1,0:T(8,128)(2,1)}, u32[]{:S(2)}) copy-start(bf16[16,8192]{1,0:T(8,128)(2,1)} %refs_0_) | copy-start | bytes 786436
  7.1 52.6 %copy-start.2 = (bf16[64,8192]{1,0:T(8,128)(2,1)S(1)}, bf16[64,8192]{1,0:T(8,128)(2,1)}, u32[]{:S(2)}) copy-start(bf16[64,8192]{1,0:T(8,128)(2,1)} %refs_8_.3) | copy-start | bytes 3145732
  7.1 5.5 %collective-permute-start.1 = (bf16[16,1024]{1,0:T(8,128)(2,1)S(1)}, bf16[16,1024]{1,0:T(8,128)(2,1)S(1)}, u32[]{:S(2)}, u32[]{:S(2)}) collective-permute-start(bf16[16,1024]{1,0:T(8,128)(2,1)S(1)} %fusion), channel_id=1, source_target_pairs={{0,8},{8,0},{1,9},{9,1},{2,10},{10,2},{3,11},{11,3},{4,12},{12,4},... | collective-permute-start | bytes 98312 | tf_op jit(solution)/shard_map/ppermute | solution.py:25
  12.6 13.5 %collective-permute-start.2 = (bf16[16,9216]{1,0:T(8,128)(2,1)S(1)}, bf16[16,9216]{1,0:T(8,128)(2,1)S(1)}, u32[]{:S(2)}, u32[]{:S(2)}) collective-permute-start(bf16[16,9216]{1,0:T(8,128)(2,1)S(1)} %pad_maximum_fusion.refs_0_), channel_id=1, source_target_pairs={{0,7},{1,0},{2,1},{3,2},{4,3},{5,4},{6,5},{7,6},{8,15},{9,8},{10,9... | collective-permute-start | bytes 884744 | tf_op jit(solution)/shard_map/ppermute | solution.py:25
  18.2 41.5 %all-to-all-start = ((bf16[8,256,256]{2,1,0:T(8,128)(2,1)}), bf16[8,256,256]{2,1,0:T(8,128)(2,1)S(1)}, u32[]{:S(2)}, u32[]{:S(2)}) async-start(bf16[8,256,256]{2,1,0:T(8,128)(2,1)} %broadcast_in_dim.2), calls=%async_computation | async-start | bytes 2097152 | tf_op jit(solution)/shard_map/all_to_all | solution.py:408
  24.0 9.2 %collective-permute-start.9 = (bf16[16,8192]{1,0:T(8,128)(2,1)S(1)}, bf16[16,8192]{1,0:T(8,128)(2,1)S(1)}, u32[]{:S(2)}, u32[]{:S(2)}) collective-permute-start(bf16[16,8192]{1,0:T(8,128)(2,1)S(1)} %copy-done.3), channel_id=1, source_target_pairs={{0,7},{1,0},{2,1},{3,2},{4,3},{5,4},{6,5},{7,6},{8,15},{9,8},{10,9... | collective-permute-start | bytes 786440 | tf_op jit(solution)/shard_map/ppermute | solution.py:25
  25.1 10.7 %collective-permute-start.13 = (bf16[16,8192]{1,0:T(8,128)(2,1)}, bf16[16,8192]{1,0:T(8,128)(2,1)S(1)}, u32[]{:S(2)}, u32[]{:S(2)}) collective-permute-start(bf16[16,8192]{1,0:T(8,128)(2,1)} %collective-permute-done.12.refs_7_), channel_id=1, source_target_pairs={{0,1},{1,2},{2,3},{3,4},{4,5},{5,6},{6,7},{7,0},{8,9},{9,10},{10,1... | collective-permute-start | bytes 786440 | tf_op jit(solution)/shard_map/ppermute | solution.py:25
  26.1 16.0 %collective-permute-start.6 = (bf16[16,9216]{1,0:T(8,128)(2,1)S(1)}, bf16[16,9216]{1,0:T(8,128)(2,1)S(1)}, u32[]{:S(2)}, u32[]{:S(2)}) collective-permute-start(bf16[16,9216]{1,0:T(8,128)(2,1)S(1)} %pad_maximum_fusion.refs_0_), channel_id=1, source_target_pairs={{0,1},{1,2},{2,3},{3,4},{4,5},{5,6},{6,7},{7,0},{8,9},{9,10},{10,1... | collective-permute-start | bytes 884744 | tf_op jit(solution)/shard_map/ppermute | solution.py:25
  26.1 15.9 %collective-permute-start.3 = (bf16[16,9216]{1,0:T(8,128)(2,1)S(1)}, bf16[16,9216]{1,0:T(8,128)(2,1)}, u32[]{:S(2)}, u32[]{:S(2)}) collective-permute-start(bf16[16,9216]{1,0:T(8,128)(2,1)S(1)} %collective-permute-done.2.refs_1_), channel_id=1, source_target_pairs={{0,7},{1,0},{2,1},{3,2},{4,3},{5,4},{6,5},{7,6},{8,15},{9,8},{10,9... | collective-permute-start | bytes 884744 | tf_op jit(solution)/shard_map/ppermute | solution.py:25
  33.3 12.0 %collective-permute-start.10 = (bf16[16,8192]{1,0:T(8,128)(2,1)S(1)}, bf16[16,8192]{1,0:T(8,128)(2,1)}, u32[]{:S(2)}, u32[]{:S(2)}) collective-permute-start(bf16[16,8192]{1,0:T(8,128)(2,1)S(1)} %collective-permute-done.9.refs_1_), channel_id=1, source_target_pairs={{0,7},{1,0},{2,1},{3,2},{4,3},{5,4},{6,5},{7,6},{8,15},{9,8},{10,9... | collective-permute-start | bytes 786440 | tf_op jit(solution)/shard_map/ppermute | solution.py:25
  34.9 0.7 copy-start.6
  35.7 12.0 %collective-permute-start.14 = (bf16[16,8192]{1,0:T(8,128)(2,1)S(1)}, bf16[16,8192]{1,0:T(8,128)(2,1)}, u32[]{:S(2)}, u32[]{:S(2)}) collective-permute-start(bf16[16,8192]{1,0:T(8,128)(2,1)S(1)} %collective-permute-done.13.refs_6_), channel_id=1, source_target_pairs={{0,1},{1,2},{2,3},{3,4},{4,5},{5,6},{6,7},{7,0},{8,9},{9,10},{10,1... | collective-permute-start | bytes 786440 | tf_op jit(solution)/shard_map/ppermute | solution.py:25
  36.0 0.7 copy-start.8
  42.0 12.0 %collective-permute-start.7 = (bf16[16,9216]{1,0:T(8,128)(2,1)S(1)}, bf16[16,9216]{1,0:T(8,128)(2,1)}, u32[]{:S(2)}, u32[]{:S(2)}) collective-permute-start(bf16[16,9216]{1,0:T(8,128)(2,1)S(1)} %collective-permute-done.6.refs_7_), channel_id=1, source_target_pairs={{0,1},{1,2},{2,3},{3,4},{4,5},{5,6},{6,7},{7,0},{8,9},{9,10},{10,1... | collective-permute-start | bytes 884744 | tf_op jit(solution)/shard_map/ppermute | solution.py:25
  42.1 12.0 %collective-permute-start.4 = (bf16[16,9216]{1,0:T(8,128)(2,1)}, bf16[16,9216]{1,0:T(8,128)(2,1)}, u32[]{:S(2)}, u32[]{:S(2)}) collective-permute-start(bf16[16,9216]{1,0:T(8,128)(2,1)} %collective-permute-done.3.refs_2_), channel_id=1, source_target_pairs={{0,7},{1,0},{2,1},{3,2},{4,3},{5,4},{6,5},{7,6},{8,15},{9,8},{10,9... | collective-permute-start | bytes 884744 | tf_op jit(solution)/shard_map/ppermute | solution.py:25
  45.3 12.2 %collective-permute-start.11 = (bf16[16,8192]{1,0:T(8,128)(2,1)}, bf16[16,8192]{1,0:T(8,128)(2,1)}, u32[]{:S(2)}, u32[]{:S(2)}) collective-permute-start(bf16[16,8192]{1,0:T(8,128)(2,1)} %collective-permute-done.10.refs_2_), channel_id=1, source_target_pairs={{0,7},{1,0},{2,1},{3,2},{4,3},{5,4},{6,5},{7,6},{8,15},{9,8},{10,9... | collective-permute-start | bytes 786440 | tf_op jit(solution)/shard_map/ppermute | solution.py:25
  47.8 11.9 %collective-permute-start.15 = (bf16[16,8192]{1,0:T(8,128)(2,1)}, bf16[16,8192]{1,0:T(8,128)(2,1)}, u32[]{:S(2)}, u32[]{:S(2)}) collective-permute-start(bf16[16,8192]{1,0:T(8,128)(2,1)} %collective-permute-done.14.refs_5_), channel_id=1, source_target_pairs={{0,1},{1,2},{2,3},{3,4},{4,5},{5,6},{6,7},{7,0},{8,9},{9,10},{10,1... | collective-permute-start | bytes 786440 | tf_op jit(solution)/shard_map/ppermute | solution.py:25
  54.1 11.5 %collective-permute-start.8 = (bf16[16,9216]{1,0:T(8,128)(2,1)}, bf16[16,9216]{1,0:T(8,128)(2,1)}, u32[]{:S(2)}, u32[]{:S(2)}) collective-permute-start(bf16[16,9216]{1,0:T(8,128)(2,1)} %collective-permute-done.7.refs_6_), channel_id=1, source_target_pairs={{0,1},{1,2},{2,3},{3,4},{4,5},{5,6},{6,7},{7,0},{8,9},{9,10},{10,1... | collective-permute-start | bytes 884744 | tf_op jit(solution)/shard_map/ppermute | solution.py:25
  54.1 11.5 %collective-permute-start.5 = (bf16[16,9216]{1,0:T(8,128)(2,1)}, bf16[16,9216]{1,0:T(8,128)(2,1)}, u32[]{:S(2)}, u32[]{:S(2)}) collective-permute-start(bf16[16,9216]{1,0:T(8,128)(2,1)} %collective-permute-done.4.refs_3_), channel_id=1, source_target_pairs={{0,7},{1,0},{2,1},{3,2},{4,3},{5,4},{6,5},{7,6},{8,15},{9,8},{10,9... | collective-permute-start | bytes 884744 | tf_op jit(solution)/shard_map/ppermute | solution.py:25
  57.4 8.2 %copy-start = (bf16[256,512]{1,0:T(8,128)(2,1)S(1)}, bf16[256,512]{1,0:T(8,128)(2,1)}, u32[]{:S(2)}) copy-start(bf16[256,512]{1,0:T(8,128)(2,1)} %o_ref.1) | copy-start | bytes 786436
  59.7 1.0 copy-start.4
  60.6 0.9 copy-start.7
  61.6 0.9 copy-start.9
  62.5 10.0 %slice-start = ((s8[8388608]{0:T(1024)(128)(4,1)}), s8[4194304]{0:T(1024)(128)(4,1)S(1)}, s32[]{:S(2)}) async-start(s8[8388608]{0:T(1024)(128)(4,1)} %bitcast.10), calls=%async_computation.2 | async-start | bytes 8388608
  65.6 6.9 %copy-start.1 = (bf16[512,64]{0,1:T(8,128)(2,1)S(1)}, bf16[512,64]{0,1:T(8,128)(2,1)}, u32[]{:S(2)}) copy-start(bf16[512,64]{0,1:T(8,128)(2,1)} %param.16) | copy-start | bytes 196612
  65.6 6.9 %slice-start.1 = ((s8[8388608]{0:T(1024)(128)(4,1)}), s8[4194304]{0:T(1024)(128)(4,1)S(1)}, s32[]{:S(2)}) async-start(s8[8388608]{0:T(1024)(128)(4,1)} %bitcast.10), calls=%async_computation.3 | async-start | bytes 8388608
  69.4 1.5 %collective-permute-start.16 = (bf16[64,1280]{1,0:T(8,128)(2,1)S(1)}, bf16[64,1280]{1,0:T(8,128)(2,1)S(1)}, u32[]{:S(2)}, u32[]{:S(2)}) collective-permute-start(bf16[64,1280]{1,0:T(8,128)(2,1)S(1)} %get-tuple-element.75), channel_id=1, source_target_pairs={{0,16},{16,0},{1,17},{17,1},{2,18},{18,2},{3,19},{19,3},{4,20},{20... | collective-permute-start | bytes 491528 | tf_op jit(solution)/shard_map/ppermute | solution.py:25
  69.5 8.2 %collective-permute-start.19 = (bf16[8,256,256]{2,1,0:T(8,128)(2,1)S(1)}, bf16[8,256,256]{2,1,0:T(8,128)(2,1)S(1)}, u32[]{:S(2)}, u32[]{:S(2)}) collective-permute-start(bf16[8,256,256]{2,1,0:T(8,128)(2,1)S(1)} %all-to-all-done.kv_ref), channel_id=1, source_target_pairs={{0,16},{16,0},{1,17},{17,1},{2,18},{18,2},{3,19},{19,3},{4,20},{20... | collective-permute-start | bytes 3145736 | tf_op jit(solution)/shard_map/ppermute | solution.py:25
  70.9 6.3 %collective-permute-start.17 = (bf16[64,1280]{1,0:T(8,128)(2,1)S(1)}, bf16[64,1280]{1,0:T(8,128)(2,1)S(1)}, u32[]{:S(2)}, u32[]{:S(2)}) collective-permute-start(bf16[64,1280]{1,0:T(8,128)(2,1)S(1)} %add_convert_fusion.4), channel_id=1, source_target_pairs={{0,128},{128,0},{1,129},{129,1},{2,130},{130,2},{3,131},{131,3},{4... | collective-permute-start | bytes 491528 | tf_op jit(solution)/shard_map/ppermute | solution.py:25
  72.5 5.2 %copy-start.5 = (bf16[256,512]{1,0:T(8,128)(2,1)S(1)}, bf16[256,512]{1,0:T(8,128)(2,1)}, u32[]{:S(2)}) copy-start(bf16[256,512]{1,0:T(8,128)(2,1)} %q_ref.1) | copy-start | bytes 786436
  72.5 5.2 %copy-start.10 = (f32[4,256]{1,0:T(4,128)S(1)}, f32[4,256]{1,0:T(4,128)}, u32[]{:S(2)}) copy-start(f32[4,256]{1,0:T(4,128)} %norm_ref.1) | copy-start | bytes 12292
  77.3 5.5 %collective-permute-start.18 = (bf16[64,1280]{1,0:T(8,128)(2,1)S(1)}, bf16[64,1280]{1,0:T(8,128)(2,1)S(1)}, u32[]{:S(2)}, u32[]{:S(2)}) collective-permute-start(bf16[64,1280]{1,0:T(8,128)(2,1)S(1)} %add_convert_fusion.3), channel_id=1, source_target_pairs={{0,32},{32,0},{64,96},{96,64},{1,33},{33,1},{65,97},{97,65},{2,34}... | collective-permute-start | bytes 491528 | tf_op jit(solution)/shard_map/ppermute | solution.py:421
  82.9 7.4 %collective-permute-start.20 = (bf16[64,1280]{1,0:T(8,128)(2,1)S(1)}, bf16[64,1280]{1,0:T(8,128)(2,1)}, u32[]{:S(2)}, u32[]{:S(2)}) collective-permute-start(bf16[64,1280]{1,0:T(8,128)(2,1)S(1)} %add_convert_fusion.2), channel_id=1, source_target_pairs={{0,96},{32,64},{64,32},{96,0},{1,97},{33,65},{65,33},{97,1},{2,98}... | collective-permute-start | bytes 491528 | tf_op jit(solution)/shard_map/ppermute | solution.py:426
  90.3 2.7 %collective-permute-start.22 = (bf16[8,256,256]{2,1,0:T(8,128)(2,1)S(1)}, bf16[8,256,256]{2,1,0:T(8,128)(2,1)S(1)}, u32[]{:S(2)}, u32[]{:S(2)}) collective-permute-start(bf16[8,256,256]{2,1,0:T(8,128)(2,1)S(1)} %get-tuple-element.112), channel_id=1, source_target_pairs={{0,16},{16,0},{1,17},{17,1},{2,18},{18,2},{3,19},{19,3},{4,20},{20... | collective-permute-start | bytes 3145736 | tf_op jit(solution)/shard_map/ppermute | solution.py:25
  91.3 2.9 %collective-permute-start.21 = (bf16[64,1280]{1,0:T(8,128)(2,1)S(1)}, bf16[64,1280]{1,0:T(8,128)(2,1)S(1)}, u32[]{:S(2)}, u32[]{:S(2)}) collective-permute-start(bf16[64,1280]{1,0:T(8,128)(2,1)S(1)} %add_convert_fusion.1), channel_id=1, source_target_pairs={{0,16},{16,0},{1,17},{17,1},{2,18},{18,2},{3,19},{19,3},{4,20},{20... | collective-permute-start | bytes 491528 | tf_op jit(solution)/shard_map/ppermute | solution.py:25
  94.2 20.4 %all-to-all-start.1 = ((bf16[8,256,256]{2,1,0:T(8,128)(2,1)}), bf16[8,256,256]{2,1,0:T(8,128)(2,1)S(1)}, u32[]{:S(2)}, u32[]{:S(2)}) async-start(bf16[8,256,256]{2,1,0:T(8,128)(2,1)} %add_convert_fusion), calls=%async_computation.1 | async-start | bytes 2097152 | tf_op jit(solution)/shard_map/all_to_all | solution.py:432
  99.5 9.4 %collective-permute-start.25 = (bf16[64,2048]{1,0:T(8,128)(2,1)S(1)}, bf16[64,2048]{1,0:T(8,128)(2,1)S(1)}, u32[]{:S(2)}, u32[]{:S(2)}) collective-permute-start(bf16[64,2048]{1,0:T(8,128)(2,1)S(1)} %pad_maximum_fusion.1.refs_0_), channel_id=1, source_target_pairs={{0,1},{1,2},{2,3},{3,4},{4,5},{5,6},{6,7},{7,0},{8,9},{9,10},{10,1... | collective-permute-start | bytes 786440 | tf_op jit(solution)/shard_map/ppermute | solution.py:25
  99.6 9.4 %collective-permute-start.24 = (bf16[64,2048]{1,0:T(8,128)(2,1)S(1)}, bf16[64,2048]{1,0:T(8,128)(2,1)S(1)}, u32[]{:S(2)}, u32[]{:S(2)}) collective-permute-start(bf16[64,2048]{1,0:T(8,128)(2,1)S(1)} %pad_maximum_fusion.1.refs_0_), channel_id=1, source_target_pairs={{0,7},{1,0},{2,1},{3,2},{4,3},{5,4},{6,5},{7,6},{8,15},{9,8},{10,9... | collective-permute-start | bytes 786440 | tf_op jit(solution)/shard_map/ppermute | solution.py:25
  108.9 6.6 %collective-permute-start.26 = (bf16[64,1024]{1,0:T(8,128)(2,1)S(1)}, bf16[64,1024]{1,0:T(8,128)(2,1)S(1)}, u32[]{:S(2)}, u32[]{:S(2)}) collective-permute-start(bf16[64,1024]{1,0:T(8,128)(2,1)S(1)} %slice.58), channel_id=1, source_target_pairs={{0,1},{1,2},{2,3},{3,4},{4,5},{5,6},{6,7},{7,0},{8,9},{9,10},{10,1... | collective-permute-start | bytes 393224 | tf_op jit(solution)/shard_map/ppermute | solution.py:25
  109.0 6.5 %collective-permute-start.27 = (bf16[64,1024]{1,0:T(8,128)(2,1)S(1)}, bf16[64,1024]{1,0:T(8,128)(2,1)S(1)}, u32[]{:S(2)}, u32[]{:S(2)}) collective-permute-start(bf16[64,1024]{1,0:T(8,128)(2,1)S(1)} %slice.59), channel_id=1, source_target_pairs={{0,7},{1,0},{2,1},{3,2},{4,3},{5,4},{6,5},{7,6},{8,15},{9,8},{10,9... | collective-permute-start | bytes 393224 | tf_op jit(solution)/shard_map/ppermute | solution.py:25
  114.7 5.1 %collective-permute-start.23 = (bf16[256,256]{1,0:T(8,128)(2,1)S(1)}, bf16[256,256]{1,0:T(8,128)(2,1)S(1)}, u32[]{:S(2)}, u32[]{:S(2)}) collective-permute-start(bf16[256,256]{1,0:T(8,128)(2,1)S(1)} %get-tuple-element.115), channel_id=1, source_target_pairs={{0,1},{1,0},{2,3},{3,2},{4,5},{5,4},{6,7},{7,6},{8,9},{9,8},{10,11... | collective-permute-start | bytes 393224 | tf_op jit(solution)/shard_map/ppermute | solution.py:441

commit v4 on v3

--- a/solution.py
+++ b/solution.py
@@ -404,7 +404,9 @@
     peer = turned(dy, "yhi", 1)
     other = turned(mixed.astype(BF16), "yhi", 1)
     peer = jnp.concatenate([peer, (mixed + other.astype(F32)).astype(BF16)], 1)
-    kv, peer = together((jnp.concatenate([k, v], 1), peer))
+    kv, own_blocks[1], own_blocks[7], peer = together(
+        (jnp.concatenate([k, v], 1), own_blocks[1], own_blocks[7], peer)
+    )
     kv = lax.all_to_all(jnp.broadcast_to(kv[None], (8,) + kv.shape), CTX[:2], 0, 0)
     own_blocks, kv = together((own_blocks, kv))
     other_kv = turned(kv, "core", 1)

time: 122 us -> 121 us (level)
  waiting for transfers between devices: 40.2 us -> 42.6 us
  starting transfers between devices: 47.7 us -> 45.9 us
    ppermute x25, waiting for transfers between devices: 33.4 us -> 35.7 us  [turned(): return lax.ppermute(x, axis, [(i, (i + by) % size) for i in range(size)])]
    ppermute x25, starting transfers between devices: 34.4 us -> 32.6 us  [turned(): return lax.ppermute(x, axis, [(i, (i + by) % size) for i in range(size)])]
    unnamed x26 -> x24, local copies, waits for them, and re-layouts: 4.29 us -> 3.59 us
  transfers between devices with their start and end apart: 30 -> 30, of which waited for: 15 -> 13; matrix products, arithmetic and copies ran while one was open for 5% -> 5% of each run, Pallas kernels for 14% -> 14%
where the time goes in v4:
time: 121 us; the launch traced here: 120 us
  starting transfers between devices  45.9 us (38%)
  waiting for transfers between devices  42.6 us (35%)
  Pallas kernels  20.2 us (17%)
  local copies, waits for them, and re-layouts  5.35 us (4%)
  other arithmetic  4.09 us (3%)
    ppermute x25, waiting for transfers between devices, turned(): return lax.ppermute(x, axis, [(i, (i + by) % size) for i in range(size)])  35.7 us
    ppermute x25, starting transfers between devices, turned(): return lax.ppermute(x, axis, [(i, (i + by) % size) for i in range(size)])  32.6 us
    all_to_all x1, starting transfers between devices, local(): lax.all_to_all(jnp.broadcast_to(kv[None], (8,) + kv.shape), CTX[:2], 0, 0)  5.81 us
    pallas_call x1, Pallas kernels, rest_call(): pl.pallas_call(rest_kernel, out_shape=(jax.ShapeDtypeStruct((2 * HALF, si...  5.52 us
    all_to_all x1, starting transfers between devices, local(): pieces = lax.all_to_all(mine, CTX[:2], 0, 0)  5.24 us
    pallas_call x1, Pallas kernels, adapter_call(): pl.pallas_call(adapter_kernel, out_shape=(jax.ShapeDtypeStruct((128, widt...  3.8 us
    unnamed x24, local copies, waits for them, and re-layouts  3.59 us
    pallas_call x1, Pallas kernels, late_call(): pl.pallas_call(late_kernel, out_shape=(stacked, stacked, line, line, jax....  3.25 us
  transfers between devices with their start and end apart: 30, of which 13 were waited for; matrix products, arithmetic and copies ran while one was open for 5% of the time, Pallas kernels for 14%

profile of v4, /device:TPU:2, one launch (start us, length us, event | category | flops | bytes accessed | tf_op | source)
XLA Modules:
  0.0 120.3 jit_solution(15586164126876288161)
XLA Ops:
  0.6 2.0 %collective-permute-start.1 = (bf16[16,8192]{1,0:T(8,128)(2,1)}, bf16[16,8192]{1,0:T(8,128)(2,1)S(1)}, u32[]{:S(2)}, u32[]{:S(2)}) collective-permute-start(bf16[16,8192]{1,0:T(8,128)(2,1)} %refs_0_), channel_id=1, source_target_pairs={{0,1},{1,2},{2,3},{3,4},{4,5},{5,6},{6,7},{7,0},{8,9},{9,10},{10,1... | collective-permute-start | bytes 786440 | tf_op jit(solution)/shard_map/ppermute | solution.py:25
  2.6 4.0 %collective-permute-start = (bf16[16,8192]{1,0:T(8,128)(2,1)}, bf16[16,8192]{1,0:T(8,128)(2,1)}, u32[]{:S(2)}, u32[]{:S(2)}) collective-permute-start(bf16[16,8192]{1,0:T(8,128)(2,1)} %refs_0_), channel_id=1, source_target_pairs={{0,7},{1,0},{2,1},{3,2},{4,3},{5,4},{6,5},{7,6},{8,15},{9,8},{10,9... | collective-permute-start | bytes 786440 | tf_op jit(solution)/shard_map/ppermute | solution.py:25
  6.7 3.2 %collective-permute-start.2 = (bf16[16,8192]{1,0:T(8,128)(2,1)}, bf16[16,8192]{1,0:T(8,128)(2,1)S(1)}, u32[]{:S(2)}, u32[]{:S(2)}) collective-permute-start(bf16[16,8192]{1,0:T(8,128)(2,1)} %refs_0_), channel_id=1, source_target_pairs={{0,8},{8,0},{1,9},{9,1},{2,10},{10,2},{3,11},{11,3},{4,12},{12,4},... | collective-permute-start | bytes 786440 | tf_op jit(solution)/shard_map/ppermute | solution.py:25
  9.8 1.2 fusion.3
  11.1 0.0 copy-start.2
  11.1 0.4 collective-permute-start.3
  11.5 0.9 pad_maximum_fusion.2
  12.4 4.5 %collective-permute-done.3 = bf16[16,1024]{1,0:T(8,128)(2,1)S(1)} collective-permute-done((bf16[16,1024]{1,0:T(8,128)(2,1)S(1)}, bf16[16,1024]{1,0:T(8,128)(2,1)S(1)}, u32[]{:S(2)}, u32[]{:S(2)}) %collective-permute-start.3) | collective-permute-done | bytes 32800 | tf_op jit(solution)/shard_map/ppermute | solution.py:25
  16.9 0.0 collective-permute-done.refs_1_
  16.9 1.7 %collective-permute-start.4 = (bf16[16,9216]{1,0:T(8,128)(2,1)S(1)}, bf16[16,9216]{1,0:T(8,128)(2,1)S(1)}, u32[]{:S(2)}, u32[]{:S(2)}) collective-permute-start(bf16[16,9216]{1,0:T(8,128)(2,1)S(1)} %pad_maximum_fusion.refs_0_), channel_id=1, source_target_pairs={{0,7},{1,0},{2,1},{3,2},{4,3},{5,4},{6,5},{7,6},{8,15},{9,8},{10,9... | collective-permute-start | bytes 884744 | tf_op jit(solution)/shard_map/ppermute | solution.py:25
  18.7 1.0 broadcast_in_dim.2
  19.7 5.8 %all-to-all-start = ((bf16[8,256,256]{2,1,0:T(8,128)(2,1)}), bf16[8,256,256]{2,1,0:T(8,128)(2,1)S(1)}, u32[]{:S(2)}, u32[]{:S(2)}) async-start(bf16[8,256,256]{2,1,0:T(8,128)(2,1)} %broadcast_in_dim.2), calls=%async_computation | async-start | bytes 2097152 | tf_op jit(solution)/shard_map/all_to_all | solution.py:410
  25.5 0.4 collective-permute-start.13
  25.9 0.0 collective-permute-start.8
  25.9 0.0 collective-permute-done.4.refs_1_
  25.9 3.2 %collective-permute-start.5 = (bf16[16,9216]{1,0:T(8,128)(2,1)S(1)}, bf16[16,9216]{1,0:T(8,128)(2,1)}, u32[]{:S(2)}, u32[]{:S(2)}) collective-permute-start(bf16[16,9216]{1,0:T(8,128)(2,1)S(1)} %collective-permute-done.4.refs_1_), channel_id=1, source_target_pairs={{0,7},{1,0},{2,1},{3,2},{4,3},{5,4},{6,5},{7,6},{8,15},{9,8},{10,9... | collective-permute-start | bytes 884744 | tf_op jit(solution)/shard_map/ppermute | solution.py:25
  29.1 1.7 %collective-permute-start.11 = (bf16[16,8192]{1,0:T(8,128)(2,1)}, bf16[16,8192]{1,0:T(8,128)(2,1)}, u32[]{:S(2)}, u32[]{:S(2)}) collective-permute-start(bf16[16,8192]{1,0:T(8,128)(2,1)} %collective-permute-done.refs_1_), channel_id=1, source_target_pairs={{0,7},{1,0},{2,1},{3,2},{4,3},{5,4},{6,5},{7,6},{8,15},{9,8},{10,9... | collective-permute-start | bytes 786440 | tf_op jit(solution)/shard_map/ppermute | solution.py:25
  30.8 5.2 %collective-permute-done.13.refs_6_ = bf16[16,8192]{1,0:T(8,128)(2,1)S(1)} collective-permute-done((bf16[16,8192]{1,0:T(8,128)(2,1)S(1)}, bf16[16,8192]{1,0:T(8,128)(2,1)S(1)}, u32[]{:S(2)}, u32[]{:S(2)}) %collective-permute-start.13) | collective-permute-done | bytes 262176 | tf_op jit(solution)/shard_map/ppermute | solution.py:25
  36.0 0.7 copy-done.7
  36.7 5.6 %collective-permute-done.8.refs_7_ = bf16[16,9216]{1,0:T(8,128)(2,1)S(1)} collective-permute-done((bf16[16,9216]{1,0:T(8,128)(2,1)S(1)}, bf16[16,9216]{1,0:T(8,128)(2,1)S(1)}, u32[]{:S(2)}, u32[]{:S(2)}) %collective-permute-start.8) | collective-permute-done | bytes 294944 | tf_op jit(solution)/shard_map/ppermute | solution.py:25
  42.3 3.2 %collective-permute-start.6 = (bf16[16,9216]{1,0:T(8,128)(2,1)}, bf16[16,9216]{1,0:T(8,128)(2,1)}, u32[]{:S(2)}, u32[]{:S(2)}) collective-permute-start(bf16[16,9216]{1,0:T(8,128)(2,1)} %collective-permute-done.5.refs_2_), channel_id=1, source_target_pairs={{0,7},{1,0},{2,1},{3,2},{4,3},{5,4},{6,5},{7,6},{8,15},{9,8},{10,9... | collective-permute-start | bytes 884744 | tf_op jit(solution)/shard_map/ppermute | solution.py:25
  45.6 0.1 collective-permute-start.12
  45.6 2.4 %collective-permute-done.14.refs_5_ = bf16[16,8192]{1,0:T(8,128)(2,1)} collective-permute-done((bf16[16,8192]{1,0:T(8,128)(2,1)S(1)}, bf16[16,8192]{1,0:T(8,128)(2,1)}, u32[]{:S(2)}, u32[]{:S(2)}) %collective-permute-start.14) | collective-permute-done | bytes 262176 | tf_op jit(solution)/shard_map/ppermute | solution.py:25
  48.0 6.3 %collective-permute-done.9.refs_6_ = bf16[16,9216]{1,0:T(8,128)(2,1)} collective-permute-done((bf16[16,9216]{1,0:T(8,128)(2,1)S(1)}, bf16[16,9216]{1,0:T(8,128)(2,1)}, u32[]{:S(2)}, u32[]{:S(2)}) %collective-permute-start.9) | collective-permute-done | bytes 294944 | tf_op jit(solution)/shard_map/ppermute | solution.py:25
  54.4 3.2 %collective-permute-start.7 = (bf16[16,9216]{1,0:T(8,128)(2,1)}, bf16[16,9216]{1,0:T(8,128)(2,1)}, u32[]{:S(2)}, u32[]{:S(2)}) collective-permute-start(bf16[16,9216]{1,0:T(8,128)(2,1)} %collective-permute-done.6.refs_3_), channel_id=1, source_target_pairs={{0,7},{1,0},{2,1},{3,2},{4,3},{5,4},{6,5},{7,6},{8,15},{9,8},{10,9... | collective-permute-start | bytes 884744 | tf_op jit(solution)/shard_map/ppermute | solution.py:25
  57.6 0.1 pad_add_fusion.where_ref
  57.7 1.9 %collective-permute-done.15.refs_4_ = bf16[16,8192]{1,0:T(8,128)(2,1)} collective-permute-done((bf16[16,8192]{1,0:T(8,128)(2,1)}, bf16[16,8192]{1,0:T(8,128)(2,1)}, u32[]{:S(2)}, u32[]{:S(2)}) %collective-permute-start.15) | collective-permute-done | bytes 262176 | tf_op jit(solution)/shard_map/ppermute | solution.py:25
  59.6 0.9 copy-done.3
  60.6 0.9 copy-done.6
  61.5 0.9 copy-done.8
  62.5 3.0 %shard_map.128 = (bf16[128,8192]{1,0:T(8,128)(2,1)S(1)}, bf16[128,64]{1,0:T(8,128)(2,1)S(1)}) custom-call(s32[4]{0:T(128)S(1)} %pad_add_fusion.where_ref, bf16[16,8192]{1,0:T(8,128)(2,1)S(1)} %copy-done.3, bf16[16,8192]{1,0:T(8,128)(2,1)} %collective-permute-done.refs_1_, bf16[16,8192]{1,0:T(8,128)(2,1)} %collective-permute-done.11.refs_2_, ...), custom_call_target="tpu_custom_call" | custom-call | flops 2000000000 | bytes 4194304 | tf_op jit(solution)/shard_map/pallas_call | solution.py:139
  65.5 0.0 copy-start.1
  65.5 0.0 slice-start.1
  65.5 3.8 %shard_map.129 = (bf16[128,8192]{1,0:T(8,128)(2,1)S(1)}, bf16[256,64]{1,0:T(8,128)(2,1)S(1)}, f32[64,1280]{1,0:T(8,128)S(1)}, bf16[64,1280]{1,0:T(8,128)(2,1)S(1)}) custom-call(s32[4]{0:T(128)S(1)} %pad_add_fusion.where_ref, bf16[16,9216]{1,0:T(8,128)(2,1)S(1)} %pad_maximum_fusion.refs_0_, bf16[16,9216]{1,0:T(8,128)(2,1)S(1)} %collective-permute-done.4.refs_1_, ...), custom_call_target="tpu_custom_call" | custom-call | flops 2000000000 | bytes 4194304 | tf_op jit(solution)/shard_map/pallas_call | solution.py:200
  69.3 0.1 collective-permute-start.16
  69.4 0.5 collective-permute-start.19
  69.9 0.9 collective-permute-done.16
  70.8 1.5 %collective-permute-start.17 = (bf16[64,1280]{1,0:T(8,128)(2,1)S(1)}, bf16[64,1280]{1,0:T(8,128)(2,1)S(1)}, u32[]{:S(2)}, u32[]{:S(2)}) collective-permute-start(bf16[64,1280]{1,0:T(8,128)(2,1)S(1)} %add_convert_fusion.4), channel_id=1, source_target_pairs={{0,128},{128,0},{1,129},{129,1},{2,130},{130,2},{3,131},{131,3},{4... | collective-permute-start | bytes 491528 | tf_op jit(solution)/shard_map/ppermute | solution.py:25
  72.4 0.0 copy-start.4
  72.4 0.0 copy-start.9
  72.4 3.0 %shard_map.130.g_ref = bf16[2,128,512]{2,1,0:T(8,128)(2,1)S(1)} custom-call(s32[4]{0:T(128)S(1)} %pad_add_fusion.where_ref, bf16[128,8192]{1,0:T(8,128)(2,1)S(1)} %get-tuple-element.75.refs_9_.own_ref, bf16[128,8192]{1,0:T(8,128)(2,1)S(1)} %get-tuple-element.81.peer_ref, bf16[512,8192]{1,0:T(8,128)(2,1)S(1)} %bitcast.11, ...), custom_call_target="tpu_custom_call" | custom-call | flops 10000000000 | bytes 8388608 | tf_op jit(solution)/shard_map/pallas_call | solution.py:240
  75.4 1.8 %collective-permute-done.17 = bf16[64,1280]{1,0:T(8,128)(2,1)S(1)} collective-permute-done((bf16[64,1280]{1,0:T(8,128)(2,1)S(1)}, bf16[64,1280]{1,0:T(8,128)(2,1)S(1)}, u32[]{:S(2)}, u32[]{:S(2)}) %collective-permute-start.17) | collective-permute-done | bytes 163872 | tf_op jit(solution)/shard_map/ppermute | solution.py:25
  77.2 0.4 collective-permute-start.18
  77.6 3.3 %shard_map.131 = (bf16[2,512,128]{2,1,0:T(8,128)(2,1)S(1)}, bf16[2,512,128]{2,1,0:T(8,128)(2,1)S(1)}, f32[2,1,512]{2,1,0:T(1,128)S(1)}, f32[2,1,512]{2,1,0:T(1,1...) custom-call(bf16[256,512]{1,0:T(8,128)(2,1)S(1)} %copy-done.4, ...), custom_call_target="tpu_custom_call" | custom-call | flops 10000000000 | bytes 4194304 | tf_op jit(solution)/shard_map/pallas_call | solution.py:355
  80.9 1.9 %collective-permute-done.18 = bf16[64,1280]{1,0:T(8,128)(2,1)S(1)} collective-permute-done((bf16[64,1280]{1,0:T(8,128)(2,1)S(1)}, bf16[64,1280]{1,0:T(8,128)(2,1)S(1)}, u32[]{:S(2)}, u32[]{:S(2)}) %collective-permute-start.18) | collective-permute-done | bytes 163872 | tf_op jit(solution)/shard_map/ppermute | solution.py:423
  82.8 1.8 %collective-permute-start.20 = (bf16[64,1280]{1,0:T(8,128)(2,1)S(1)}, bf16[64,1280]{1,0:T(8,128)(2,1)}, u32[]{:S(2)}, u32[]{:S(2)}) collective-permute-start(bf16[64,1280]{1,0:T(8,128)(2,1)S(1)} %add_convert_fusion.2), channel_id=1, source_target_pairs={{0,96},{32,64},{64,32},{96,0},{1,97},{33,65},{65,33},{97,1},{2,98}... | collective-permute-start | bytes 491528 | tf_op jit(solution)/shard_map/ppermute | solution.py:428
  84.5 5.5 %shard_map.132 = (bf16[256,512]{1,0:T(8,128)(2,1)}, bf16[8,256,256]{2,1,0:T(8,128)(2,1)S(1)}, bf16[8,256,256]{2,1,0:T(8,128)(2,1)S(1)}) custom-call(s32[4]{0:T(128)S(1)} %pad_add_fusion.where_ref, bf16[2,512,128]{2,1,0:T(8,128)(2,1)S(1)} %get-tuple-element.103.qs, bf16[2,512,128]{2,1,0:T(8,128)(2,1)S(1)} %get-tuple-element.104.gs, ...), custom_call_target="tpu_custom_call" | custom-call | flops 10000000000 | bytes 4194304 | tf_op jit(solution)/shard_map/pallas_call | solution.py:380
  90.1 1.0 add_convert_fusion.1
  91.0 0.6 collective-permute-start.21
  91.6 1.1 collective-permute-done.22
  92.7 1.3 %add_convert_fusion = bf16[8,256,256]{2,1,0:T(8,128)(2,1)} fusion(bf16[8,256,256]{2,1,0:T(8,128)(2,1)S(1)} %collective-permute-done.22, bf16[8,256,256]{2,1,0:T(8,128)(2,1)S(1)} %get-tuple-element.115), kind=kLoop, calls=%fused_computation | loop fusion | flops 2097152 | bytes 3145728 | tf_op jit(solution)/shard_map/convert_element_type | solution.py:432
  94.0 5.2 %all-to-all-start.1 = ((bf16[8,256,256]{2,1,0:T(8,128)(2,1)}), bf16[8,256,256]{2,1,0:T(8,128)(2,1)S(1)}, u32[]{:S(2)}, u32[]{:S(2)}) async-start(bf16[8,256,256]{2,1,0:T(8,128)(2,1)} %add_convert_fusion), calls=%async_computation.1 | async-start | bytes 2097152 | tf_op jit(solution)/shard_map/all_to_all | solution.py:434
  99.3 0.1 collective-permute-start.25
  99.4 3.2 %collective-permute-start.24 = (bf16[64,2048]{1,0:T(8,128)(2,1)S(1)}, bf16[64,2048]{1,0:T(8,128)(2,1)S(1)}, u32[]{:S(2)}, u32[]{:S(2)}) collective-permute-start(bf16[64,2048]{1,0:T(8,128)(2,1)S(1)} %pad_maximum_fusion.1.refs_0_), channel_id=1, source_target_pairs={{0,7},{1,0},{2,1},{3,2},{4,3},{5,4},{6,5},{7,6},{8,15},{9,8},{10,9... | collective-permute-start | bytes 786440 | tf_op jit(solution)/shard_map/ppermute | solution.py:25
  102.6 6.0 %collective-permute-done.25.refs_4_ = bf16[64,2048]{1,0:T(8,128)(2,1)S(1)} collective-permute-done((bf16[64,2048]{1,0:T(8,128)(2,1)S(1)}, bf16[64,2048]{1,0:T(8,128)(2,1)S(1)}, u32[]{:S(2)}, u32[]{:S(2)}) %collective-permute-start.25) | collective-permute-done | bytes 262176 | tf_op jit(solution)/shard_map/ppermute | solution.py:25
  108.7 0.1 collective-permute-start.26
  108.8 3.3 %collective-permute-start.27 = (bf16[64,1024]{1,0:T(8,128)(2,1)S(1)}, bf16[64,1024]{1,0:T(8,128)(2,1)S(1)}, u32[]{:S(2)}, u32[]{:S(2)}) collective-permute-start(bf16[64,1024]{1,0:T(8,128)(2,1)S(1)} %slice.59), channel_id=1, source_target_pairs={{0,7},{1,0},{2,1},{3,2},{4,3},{5,4},{6,5},{7,6},{8,15},{9,8},{10,9... | collective-permute-start | bytes 393224 | tf_op jit(solution)/shard_map/ppermute | solution.py:25
  112.1 2.3 %all-to-all-done.1.pieces_ref = bf16[8,256,256]{2,1,0:T(8,128)(2,1)S(1)} async-done(((bf16[8,256,256]{2,1,0:T(8,128)(2,1)}), bf16[8,256,256]{2,1,0:T(8,128)(2,1)S(1)}, u32[]{:S(2)}, u32[]{:S(2)}) %all-to-all-start.1) | async-done | bytes 1048608 | tf_op jit(solution)/shard_map/all_to_all | solution.py:434
  114.4 0.1 shard_map.133
  114.5 0.1 collective-permute-start.23
  114.7 0.7 convert_bitcast_fusion
  115.3 1.6 %shard_map.134 = bf16[64,8192]{1,0:T(8,128)(2,1)} custom-call(s32[4]{0:T(128)S(1)} %pad_add_fusion.where_ref, bf16[64,2048]{1,0:T(8,128)(2,1)S(1)} %pad_maximum_fusion.1.refs_0_, bf16[64,2048]{1,0:T(8,128)(2,1)S(1)} %collective-permute-done.24.refs_1_, bf16[64,1024]{1,0:T(8,128)(2,1)S(1)} %collective-permute-done.26.refs_2_, ...), custom_call_target="tpu_custom_call" | custom-call | bytes 1048576 | tf_op jit(solution)/shard_map/pallas_call | solution.py:58
  116.9 2.7 %collective-permute-done.23 = bf16[256,256]{1,0:T(8,128)(2,1)S(1)} collective-permute-done((bf16[256,256]{1,0:T(8,128)(2,1)S(1)}, bf16[256,256]{1,0:T(8,128)(2,1)S(1)}, u32[]{:S(2)}, u32[]{:S(2)}) %collective-permute-start.23) | collective-permute-done | bytes 131104 | tf_op jit(solution)/shard_map/ppermute | solution.py:443
  119.6 0.7 fusion.1
  (52 shorter events, 0.4 us)
Async XLA Ops:
  0.6 16.3 %collective-permute-start.1 = (bf16[16,8192]{1,0:T(8,128)(2,1)}, bf16[16,8192]{1,0:T(8,128)(2,1)S(1)}, u32[]{:S(2)}, u32[]{:S(2)}) collective-permute-start(bf16[16,8192]{1,0:T(8,128)(2,1)} %refs_0_), channel_id=1, source_target_pairs={{0,1},{1,2},{2,3},{3,4},{4,5},{5,6},{6,7},{7,0},{8,9},{9,10},{10,1... | collective-permute-start | bytes 786440 | tf_op jit(solution)/shard_map/ppermute | solution.py:25
  2.6 14.3 %collective-permute-start = (bf16[16,8192]{1,0:T(8,128)(2,1)}, bf16[16,8192]{1,0:T(8,128)(2,1)}, u32[]{:S(2)}, u32[]{:S(2)}) collective-permute-start(bf16[16,8192]{1,0:T(8,128)(2,1)} %refs_0_), channel_id=1, source_target_pairs={{0,7},{1,0},{2,1},{3,2},{4,3},{5,4},{6,5},{7,6},{8,15},{9,8},{10,9... | collective-permute-start | bytes 786440 | tf_op jit(solution)/shard_map/ppermute | solution.py:25
  6.7 10.2 %collective-permute-start.2 = (bf16[16,8192]{1,0:T(8,128)(2,1)}, bf16[16,8192]{1,0:T(8,128)(2,1)S(1)}, u32[]{:S(2)}, u32[]{:S(2)}) collective-permute-start(bf16[16,8192]{1,0:T(8,128)(2,1)} %refs_0_), channel_id=1, source_target_pairs={{0,8},{8,0},{1,9},{9,1},{2,10},{10,2},{3,11},{11,3},{4,12},{12,4},... | collective-permute-start | bytes 786440 | tf_op jit(solution)/shard_map/ppermute | solution.py:25
  11.1 48.5 %copy-start.2 = (bf16[64,8192]{1,0:T(8,128)(2,1)S(1)}, bf16[64,8192]{1,0:T(8,128)(2,1)}, u32[]{:S(2)}) copy-start(bf16[64,8192]{1,0:T(8,128)(2,1)} %refs_8_.3) | copy-start | bytes 3145732
  11.1 5.8 %collective-permute-start.3 = (bf16[16,1024]{1,0:T(8,128)(2,1)S(1)}, bf16[16,1024]{1,0:T(8,128)(2,1)S(1)}, u32[]{:S(2)}, u32[]{:S(2)}) collective-permute-start(bf16[16,1024]{1,0:T(8,128)(2,1)S(1)} %fusion), channel_id=1, source_target_pairs={{0,8},{8,0},{1,9},{9,1},{2,10},{10,2},{3,11},{11,3},{4,12},{12,4},... | collective-permute-start | bytes 98312 | tf_op jit(solution)/shard_map/ppermute | solution.py:25
  16.9 40.7 %copy-start.5 = (bf16[16,8192]{1,0:T(8,128)(2,1)}, bf16[16,8192]{1,0:T(8,128)(2,1)S(1)}, u32[]{:S(2)}) copy-start(bf16[16,8192]{1,0:T(8,128)(2,1)S(1)} %collective-permute-done.1.refs_7_) | copy-start | bytes 786436
  16.9 9.0 %collective-permute-start.4 = (bf16[16,9216]{1,0:T(8,128)(2,1)S(1)}, bf16[16,9216]{1,0:T(8,128)(2,1)S(1)}, u32[]{:S(2)}, u32[]{:S(2)}) collective-permute-start(bf16[16,9216]{1,0:T(8,128)(2,1)S(1)} %pad_maximum_fusion.refs_0_), channel_id=1, source_target_pairs={{0,7},{1,0},{2,1},{3,2},{4,3},{5,4},{6,5},{7,6},{8,15},{9,8},{10,9... | collective-permute-start | bytes 884744 | tf_op jit(solution)/shard_map/ppermute | solution.py:25
  19.7 39.9 %all-to-all-start = ((bf16[8,256,256]{2,1,0:T(8,128)(2,1)}), bf16[8,256,256]{2,1,0:T(8,128)(2,1)S(1)}, u32[]{:S(2)}, u32[]{:S(2)}) async-start(bf16[8,256,256]{2,1,0:T(8,128)(2,1)} %broadcast_in_dim.2), calls=%async_computation | async-start | bytes 2097152 | tf_op jit(solution)/shard_map/all_to_all | solution.py:410
  25.5 10.5 %collective-permute-start.13 = (bf16[16,8192]{1,0:T(8,128)(2,1)S(1)}, bf16[16,8192]{1,0:T(8,128)(2,1)S(1)}, u32[]{:S(2)}, u32[]{:S(2)}) collective-permute-start(bf16[16,8192]{1,0:T(8,128)(2,1)S(1)} %collective-permute-done.1.refs_7_), channel_id=1, source_target_pairs={{0,1},{1,2},{2,3},{3,4},{4,5},{5,6},{6,7},{7,0},{8,9},{9,10},{10,1... | collective-permute-start | bytes 786440 | tf_op jit(solution)/shard_map/ppermute | solution.py:25
  25.9 16.4 %collective-permute-start.8 = (bf16[16,9216]{1,0:T(8,128)(2,1)S(1)}, bf16[16,9216]{1,0:T(8,128)(2,1)S(1)}, u32[]{:S(2)}, u32[]{:S(2)}) collective-permute-start(bf16[16,9216]{1,0:T(8,128)(2,1)S(1)} %pad_maximum_fusion.refs_0_), channel_id=1, source_target_pairs={{0,1},{1,2},{2,3},{3,4},{4,5},{5,6},{6,7},{7,0},{8,9},{9,10},{10,1... | collective-permute-start | bytes 884744 | tf_op jit(solution)/shard_map/ppermute | solution.py:25
  25.9 16.4 %collective-permute-start.5 = (bf16[16,9216]{1,0:T(8,128)(2,1)S(1)}, bf16[16,9216]{1,0:T(8,128)(2,1)}, u32[]{:S(2)}, u32[]{:S(2)}) collective-permute-start(bf16[16,9216]{1,0:T(8,128)(2,1)S(1)} %collective-permute-done.4.refs_1_), channel_id=1, source_target_pairs={{0,7},{1,0},{2,1},{3,2},{4,3},{5,4},{6,5},{7,6},{8,15},{9,8},{10,9... | collective-permute-start | bytes 884744 | tf_op jit(solution)/shard_map/ppermute | solution.py:25
  29.1 16.4 %collective-permute-start.11 = (bf16[16,8192]{1,0:T(8,128)(2,1)}, bf16[16,8192]{1,0:T(8,128)(2,1)}, u32[]{:S(2)}, u32[]{:S(2)}) collective-permute-start(bf16[16,8192]{1,0:T(8,128)(2,1)} %collective-permute-done.refs_1_), channel_id=1, source_target_pairs={{0,7},{1,0},{2,1},{3,2},{4,3},{5,4},{6,5},{7,6},{8,15},{9,8},{10,9... | collective-permute-start | bytes 786440 | tf_op jit(solution)/shard_map/ppermute | solution.py:25
  36.0 12.0 %collective-permute-start.14 = (bf16[16,8192]{1,0:T(8,128)(2,1)S(1)}, bf16[16,8192]{1,0:T(8,128)(2,1)}, u32[]{:S(2)}, u32[]{:S(2)}) collective-permute-start(bf16[16,8192]{1,0:T(8,128)(2,1)S(1)} %collective-permute-done.13.refs_6_), channel_id=1, source_target_pairs={{0,1},{1,2},{2,3},{3,4},{4,5},{5,6},{6,7},{7,0},{8,9},{9,10},{10,1... | collective-permute-start | bytes 786440 | tf_op jit(solution)/shard_map/ppermute | solution.py:25
  36.0 0.7 copy-start.7
  42.3 12.0 %collective-permute-start.9 = (bf16[16,9216]{1,0:T(8,128)(2,1)S(1)}, bf16[16,9216]{1,0:T(8,128)(2,1)}, u32[]{:S(2)}, u32[]{:S(2)}) collective-permute-start(bf16[16,9216]{1,0:T(8,128)(2,1)S(1)} %collective-permute-done.8.refs_7_), channel_id=1, source_target_pairs={{0,1},{1,2},{2,3},{3,4},{4,5},{5,6},{6,7},{7,0},{8,9},{9,10},{10,1... | collective-permute-start | bytes 884744 | tf_op jit(solution)/shard_map/ppermute | solution.py:25
  42.3 12.0 %collective-permute-start.6 = (bf16[16,9216]{1,0:T(8,128)(2,1)}, bf16[16,9216]{1,0:T(8,128)(2,1)}, u32[]{:S(2)}, u32[]{:S(2)}) collective-permute-start(bf16[16,9216]{1,0:T(8,128)(2,1)} %collective-permute-done.5.refs_2_), channel_id=1, source_target_pairs={{0,7},{1,0},{2,1},{3,2},{4,3},{5,4},{6,5},{7,6},{8,15},{9,8},{10,9... | collective-permute-start | bytes 884744 | tf_op jit(solution)/shard_map/ppermute | solution.py:25
  45.6 12.1 %collective-permute-start.12 = (bf16[16,8192]{1,0:T(8,128)(2,1)}, bf16[16,8192]{1,0:T(8,128)(2,1)}, u32[]{:S(2)}, u32[]{:S(2)}) collective-permute-start(bf16[16,8192]{1,0:T(8,128)(2,1)} %collective-permute-done.11.refs_2_), channel_id=1, source_target_pairs={{0,7},{1,0},{2,1},{3,2},{4,3},{5,4},{6,5},{7,6},{8,15},{9,8},{10,9... | collective-permute-start | bytes 786440 | tf_op jit(solution)/shard_map/ppermute | solution.py:25
  48.0 11.6 %collective-permute-start.15 = (bf16[16,8192]{1,0:T(8,128)(2,1)}, bf16[16,8192]{1,0:T(8,128)(2,1)}, u32[]{:S(2)}, u32[]{:S(2)}) collective-permute-start(bf16[16,8192]{1,0:T(8,128)(2,1)} %collective-permute-done.14.refs_5_), channel_id=1, source_target_pairs={{0,1},{1,2},{2,3},{3,4},{4,5},{5,6},{6,7},{7,0},{8,9},{9,10},{10,1... | collective-permute-start | bytes 786440 | tf_op jit(solution)/shard_map/ppermute | solution.py:25
  54.3 11.1 %collective-permute-start.10 = (bf16[16,9216]{1,0:T(8,128)(2,1)}, bf16[16,9216]{1,0:T(8,128)(2,1)}, u32[]{:S(2)}, u32[]{:S(2)}) collective-permute-start(bf16[16,9216]{1,0:T(8,128)(2,1)} %collective-permute-done.9.refs_6_), channel_id=1, source_target_pairs={{0,1},{1,2},{2,3},{3,4},{4,5},{5,6},{6,7},{7,0},{8,9},{9,10},{10,1... | collective-permute-start | bytes 884744 | tf_op jit(solution)/shard_map/ppermute | solution.py:25
  54.4 11.1 %collective-permute-start.7 = (bf16[16,9216]{1,0:T(8,128)(2,1)}, bf16[16,9216]{1,0:T(8,128)(2,1)}, u32[]{:S(2)}, u32[]{:S(2)}) collective-permute-start(bf16[16,9216]{1,0:T(8,128)(2,1)} %collective-permute-done.6.refs_3_), channel_id=1, source_target_pairs={{0,7},{1,0},{2,1},{3,2},{4,3},{5,4},{6,5},{7,6},{8,15},{9,8},{10,9... | collective-permute-start | bytes 884744 | tf_op jit(solution)/shard_map/ppermute | solution.py:25
  57.7 7.8 %copy-start = (bf16[256,512]{1,0:T(8,128)(2,1)S(1)}, bf16[256,512]{1,0:T(8,128)(2,1)}, u32[]{:S(2)}) copy-start(bf16[256,512]{1,0:T(8,128)(2,1)} %o_ref.1) | copy-start | bytes 786436
  59.6 1.0 copy-start.3
  60.6 0.9 copy-start.6
  61.5 0.9 copy-start.8
  62.5 9.9 %slice-start = ((s8[8388608]{0:T(1024)(128)(4,1)}), s8[4194304]{0:T(1024)(128)(4,1)S(1)}, s32[]{:S(2)}) async-start(s8[8388608]{0:T(1024)(128)(4,1)} %bitcast.10), calls=%async_computation.2 | async-start | bytes 8388608
  65.5 6.9 %copy-start.1 = (bf16[512,64]{0,1:T(8,128)(2,1)S(1)}, bf16[512,64]{0,1:T(8,128)(2,1)}, u32[]{:S(2)}) copy-start(bf16[512,64]{0,1:T(8,128)(2,1)} %param.16) | copy-start | bytes 196612
  65.5 6.9 %slice-start.1 = ((s8[8388608]{0:T(1024)(128)(4,1)}), s8[4194304]{0:T(1024)(128)(4,1)S(1)}, s32[]{:S(2)}) async-start(s8[8388608]{0:T(1024)(128)(4,1)} %bitcast.10), calls=%async_computation.3 | async-start | bytes 8388608
  69.3 1.5 %collective-permute-start.16 = (bf16[64,1280]{1,0:T(8,128)(2,1)S(1)}, bf16[64,1280]{1,0:T(8,128)(2,1)S(1)}, u32[]{:S(2)}, u32[]{:S(2)}) collective-permute-start(bf16[64,1280]{1,0:T(8,128)(2,1)S(1)} %get-tuple-element.79), channel_id=1, source_target_pairs={{0,16},{16,0},{1,17},{17,1},{2,18},{18,2},{3,19},{19,3},{4,20},{20... | collective-permute-start | bytes 491528 | tf_op jit(solution)/shard_map/ppermute | solution.py:25
  69.4 8.2 %collective-permute-start.19 = (bf16[8,256,256]{2,1,0:T(8,128)(2,1)S(1)}, bf16[8,256,256]{2,1,0:T(8,128)(2,1)S(1)}, u32[]{:S(2)}, u32[]{:S(2)}) collective-permute-start(bf16[8,256,256]{2,1,0:T(8,128)(2,1)S(1)} %all-to-all-done.kv_ref), channel_id=1, source_target_pairs={{0,16},{16,0},{1,17},{17,1},{2,18},{18,2},{3,19},{19,3},{4,20},{20... | collective-permute-start | bytes 3145736 | tf_op jit(solution)/shard_map/ppermute | solution.py:25
  70.8 6.3 %collective-permute-start.17 = (bf16[64,1280]{1,0:T(8,128)(2,1)S(1)}, bf16[64,1280]{1,0:T(8,128)(2,1)S(1)}, u32[]{:S(2)}, u32[]{:S(2)}) collective-permute-start(bf16[64,1280]{1,0:T(8,128)(2,1)S(1)} %add_convert_fusion.4), channel_id=1, source_target_pairs={{0,128},{128,0},{1,129},{129,1},{2,130},{130,2},{3,131},{131,3},{4... | collective-permute-start | bytes 491528 | tf_op jit(solution)/shard_map/ppermute | solution.py:25
  72.4 5.2 %copy-start.4 = (bf16[256,512]{1,0:T(8,128)(2,1)S(1)}, bf16[256,512]{1,0:T(8,128)(2,1)}, u32[]{:S(2)}) copy-start(bf16[256,512]{1,0:T(8,128)(2,1)} %q_ref.1) | copy-start | bytes 786436
  72.4 5.2 %copy-start.9 = (f32[4,256]{1,0:T(4,128)S(1)}, f32[4,256]{1,0:T(4,128)}, u32[]{:S(2)}) copy-start(f32[4,256]{1,0:T(4,128)} %norm_ref.1) | copy-start | bytes 12292
  77.2 5.5 %collective-permute-start.18 = (bf16[64,1280]{1,0:T(8,128)(2,1)S(1)}, bf16[64,1280]{1,0:T(8,128)(2,1)S(1)}, u32[]{:S(2)}, u32[]{:S(2)}) collective-permute-start(bf16[64,1280]{1,0:T(8,128)(2,1)S(1)} %add_convert_fusion.3), channel_id=1, source_target_pairs={{0,32},{32,0},{64,96},{96,64},{1,33},{33,1},{65,97},{97,65},{2,34}... | collective-permute-start | bytes 491528 | tf_op jit(solution)/shard_map/ppermute | solution.py:423
  82.8 7.3 %collective-permute-start.20 = (bf16[64,1280]{1,0:T(8,128)(2,1)S(1)}, bf16[64,1280]{1,0:T(8,128)(2,1)}, u32[]{:S(2)}, u32[]{:S(2)}) collective-permute-start(bf16[64,1280]{1,0:T(8,128)(2,1)S(1)} %add_convert_fusion.2), channel_id=1, source_target_pairs={{0,96},{32,64},{64,32},{96,0},{1,97},{33,65},{65,33},{97,1},{2,98}... | collective-permute-start | bytes 491528 | tf_op jit(solution)/shard_map/ppermute | solution.py:428
  90.1 2.7 %collective-permute-start.22 = (bf16[8,256,256]{2,1,0:T(8,128)(2,1)S(1)}, bf16[8,256,256]{2,1,0:T(8,128)(2,1)S(1)}, u32[]{:S(2)}, u32[]{:S(2)}) collective-permute-start(bf16[8,256,256]{2,1,0:T(8,128)(2,1)S(1)} %get-tuple-element.116), channel_id=1, source_target_pairs={{0,16},{16,0},{1,17},{17,1},{2,18},{18,2},{3,19},{19,3},{4,20},{20... | collective-permute-start | bytes 3145736 | tf_op jit(solution)/shard_map/ppermute | solution.py:25
  91.0 3.0 %collective-permute-start.21 = (bf16[64,1280]{1,0:T(8,128)(2,1)S(1)}, bf16[64,1280]{1,0:T(8,128)(2,1)S(1)}, u32[]{:S(2)}, u32[]{:S(2)}) collective-permute-start(bf16[64,1280]{1,0:T(8,128)(2,1)S(1)} %add_convert_fusion.1), channel_id=1, source_target_pairs={{0,16},{16,0},{1,17},{17,1},{2,18},{18,2},{3,19},{19,3},{4,20},{20... | collective-permute-start | bytes 491528 | tf_op jit(solution)/shard_map/ppermute | solution.py:25
  94.0 20.4 %all-to-all-start.1 = ((bf16[8,256,256]{2,1,0:T(8,128)(2,1)}), bf16[8,256,256]{2,1,0:T(8,128)(2,1)S(1)}, u32[]{:S(2)}, u32[]{:S(2)}) async-start(bf16[8,256,256]{2,1,0:T(8,128)(2,1)} %add_convert_fusion), calls=%async_computation.1 | async-start | bytes 2097152 | tf_op jit(solution)/shard_map/all_to_all | solution.py:434
  99.3 9.4 %collective-permute-start.25 = (bf16[64,2048]{1,0:T(8,128)(2,1)S(1)}, bf16[64,2048]{1,0:T(8,128)(2,1)S(1)}, u32[]{:S(2)}, u32[]{:S(2)}) collective-permute-start(bf16[64,2048]{1,0:T(8,128)(2,1)S(1)} %pad_maximum_fusion.1.refs_0_), channel_id=1, source_target_pairs={{0,1},{1,2},{2,3},{3,4},{4,5},{5,6},{6,7},{7,0},{8,9},{9,10},{10,1... | collective-permute-start | bytes 786440 | tf_op jit(solution)/shard_map/ppermute | solution.py:25
  99.4 9.4 %collective-permute-start.24 = (bf16[64,2048]{1,0:T(8,128)(2,1)S(1)}, bf16[64,2048]{1,0:T(8,128)(2,1)S(1)}, u32[]{:S(2)}, u32[]{:S(2)}) collective-permute-start(bf16[64,2048]{1,0:T(8,128)(2,1)S(1)} %pad_maximum_fusion.1.refs_0_), channel_id=1, source_target_pairs={{0,7},{1,0},{2,1},{3,2},{4,3},{5,4},{6,5},{7,6},{8,15},{9,8},{10,9... | collective-permute-start | bytes 786440 | tf_op jit(solution)/shard_map/ppermute | solution.py:25
  108.7 6.6 %collective-permute-start.26 = (bf16[64,1024]{1,0:T(8,128)(2,1)S(1)}, bf16[64,1024]{1,0:T(8,128)(2,1)S(1)}, u32[]{:S(2)}, u32[]{:S(2)}) collective-permute-start(bf16[64,1024]{1,0:T(8,128)(2,1)S(1)} %slice.58), channel_id=1, source_target_pairs={{0,1},{1,2},{2,3},{3,4},{4,5},{5,6},{6,7},{7,0},{8,9},{9,10},{10,1... | collective-permute-start | bytes 393224 | tf_op jit(solution)/shard_map/ppermute | solution.py:25
  108.8 6.5 %collective-permute-start.27 = (bf16[64,1024]{1,0:T(8,128)(2,1)S(1)}, bf16[64,1024]{1,0:T(8,128)(2,1)S(1)}, u32[]{:S(2)}, u32[]{:S(2)}) collective-permute-start(bf16[64,1024]{1,0:T(8,128)(2,1)S(1)} %slice.59), channel_id=1, source_target_pairs={{0,7},{1,0},{2,1},{3,2},{4,3},{5,4},{6,5},{7,6},{8,15},{9,8},{10,9... | collective-permute-start | bytes 393224 | tf_op jit(solution)/shard_map/ppermute | solution.py:25
  114.5 5.1 %collective-permute-start.23 = (bf16[256,256]{1,0:T(8,128)(2,1)S(1)}, bf16[256,256]{1,0:T(8,128)(2,1)S(1)}, u32[]{:S(2)}, u32[]{:S(2)}) collective-permute-start(bf16[256,256]{1,0:T(8,128)(2,1)S(1)} %get-tuple-element.119), channel_id=1, source_target_pairs={{0,1},{1,0},{2,3},{3,2},{4,5},{5,4},{6,7},{7,6},{8,9},{9,8},{10,11... | collective-permute-start | bytes 393224 | tf_op jit(solution)/shard_map/ppermute | solution.py:443
